TPU v7x, 512 devices: a whole 4x4x16 slice. The times are simulated.
512 devices in a mesh: dp: 16 (over z_lo, core), tm: 32 (over y, z_hi, x).
Axes of the slice: x: 4, y: 4, z: 16 (z_hi: 2, z_lo: 8; z = z_hi * 8 + z_lo), core: 2. Of those that a mesh axis runs over, the one named last changes fastest.
Arguments:
- query_rows: bfloat16 [16, 4096, 1024], P('dp', 'tm'), may hold values from -24 to 24
- key_rows: bfloat16 [16, 4096, 1024], P('dp', 'tm'), may hold values from -24 to 24
- value_rows: bfloat16 [16, 4096, 1024], P('dp', 'tm'), may hold values from -6 to 6
- grad_out: bfloat16 [16, 4096, 1024], P('dp', 'tm'), may hold values from -6 to 6
- conv_weight: float32 [9, 1024], replicated, may hold values from -0.6 to 0.6
- frames: int32 [16], P('dp'), may hold values from 2048 to 4096, as said below
- window_links: int32 [16, 32, 2], P('dp', 'tm'), may hold values 0 or 1
Outputs:
- grad_query: bfloat16 [16, 4096, 1024], P('dp', 'tm')
- grad_key: bfloat16 [16, 4096, 1024], P('dp', 'tm')
- grad_value: bfloat16 [16, 4096, 1024], P('dp', 'tm')
- grad_conv: float32 [9, 1024], replicated
Inputs may be any that keep to these rules, and one draw needn't show every extreme that they name: Some recording has all 4096 frames valid.
All inputs are finite; a program needn't handle non-finite values. No bound on the sum of `window_links` on one device may be relied on, other than what follows from the above.
Results may differ from a plain program's by a relative error of at most 0.015.
Values may be sent and summed in bfloat16 or wider, within the bound.
No kernel may reach another device: no remote copies, remote signals or barrier semaphores. Data moves between devices by JAX's collectives and lax.ppermute only.
A program may use at most 64 MiB of HBM per device.

v0:
```python
import jax
import jax.numpy as jnp
from jax import lax
from jax.sharding import PartitionSpec as P

H = 8
BLK = 128
SUMM = 8


MASKED = -1e30


def extended(cells, sides, width):
    for axis, dim in sides:
        count = lax.axis_size(axis)
        ends = count - 1
        head = lax.slice_in_dim(cells, 0, width, axis=dim)
        tail = lax.slice_in_dim(cells, cells.shape[dim] - width, cells.shape[dim], axis=dim)
        cells = jnp.concatenate(
            [
                lax.ppermute(tail, axis, [(i, (i + 1) % count) for i in range(ends)]),
                cells,
                lax.ppermute(head, axis, [((i + 1) % count, i) for i in range(ends)]),
            ],
            axis=dim,
        )
    return cells


def passed_along(array, axis, by):
    devices = lax.axis_size(axis)
    pairs = [(i, i + by) for i in range(devices) if 0 <= i + by < devices]
    return lax.ppermute(array, axis, pairs)


def product(form, left_op, right_op):
    return jnp.einsum(form, left_op, right_op, preferred_element_type=jnp.float32)


def unwind_window(window, blocks, block_rows, group_cols):
    parts = window.reshape(blocks, 3, block_rows, group_cols)
    spread = jnp.pad(parts[:, 0], ((0, 2), (0, 0), (0, 0)))
    spread = spread + jnp.pad(parts[:, 1], ((1, 1), (0, 0), (0, 0)))
    spread = spread + jnp.pad(parts[:, 2], ((2, 0), (0, 0), (0, 0)))
    return spread.reshape((blocks + 2) * block_rows, group_cols)


def block_pass(
    queries, padded_kv, pad_ok, link_rows, summary, summary_ok, attn_grad, block_rows, heads
):
    row_count, full_width = queries.shape
    blocks = row_count // block_rows
    head_size = full_width // heads
    per_group = min(4, heads)
    group_cols = per_group * head_size
    glob_rows = summary.shape[0]
    score_scale = head_size ** (-0.5)
    ok_blocks = pad_ok.reshape(blocks + 2, block_rows)
    left_link = link_rows[:, 0:1] == 1
    right_link = link_rows[:, 1:2] == 1
    window_ok = jnp.concatenate(
        [ok_blocks[:-2] & left_link, ok_blocks[1:-1], ok_blocks[2:] & right_link], axis=1
    )
    anchor = jnp.zeros((), jnp.int32)

    def one_group(group_index, running):
        attn_all, query_all, kv_all, summary_all = running
        column = (group_index * group_cols).astype(jnp.int32)
        other = column + full_width
        query_part = lax.dynamic_slice_in_dim(queries, column, group_cols, 1).reshape(
            blocks, block_rows, per_group, head_size
        )
        key_pad = lax.dynamic_slice_in_dim(padded_kv, column, group_cols, 1).reshape(
            blocks + 2, block_rows, per_group, head_size
        )
        value_pad = lax.dynamic_slice_in_dim(padded_kv, other, group_cols, 1).reshape(
            blocks + 2, block_rows, per_group, head_size
        )
        key_window = jnp.concatenate([key_pad[:-2], key_pad[1:-1], key_pad[2:]], axis=1)
        value_window = jnp.concatenate([value_pad[:-2], value_pad[1:-1], value_pad[2:]], axis=1)
        key_summary = lax.dynamic_slice_in_dim(summary, column, group_cols, 1).reshape(
            glob_rows, per_group, head_size
        )
        value_summary = lax.dynamic_slice_in_dim(summary, other, group_cols, 1).reshape(
            glob_rows, per_group, head_size
        )
        grad_part = lax.dynamic_slice_in_dim(attn_grad, column, group_cols, 1).reshape(
            blocks, block_rows, per_group, head_size
        )
        local_scores = product("cihd,cjhd->chij", query_part, key_window) * score_scale
        global_scores = product("cihd,ghd->chig", query_part, key_summary) * score_scale
        local_scores = jnp.where(window_ok[:, None, None, :], local_scores, MASKED)
        global_scores = jnp.where(summary_ok[None, None, None, :], global_scores, MASKED)
        highest = jnp.maximum(jnp.max(local_scores, axis=-1), jnp.max(global_scores, axis=-1))[
            ..., None
        ]
        local_exp = jnp.exp(local_scores - highest)
        global_exp = jnp.exp(global_scores - highest)
        row_total = jnp.sum(local_exp, axis=-1, keepdims=True) + jnp.sum(
            global_exp, axis=-1, keepdims=True
        )
        local_prob = local_exp / row_total
        global_prob = global_exp / row_total
        local_pbf = local_prob.astype(jnp.bfloat16)
        global_pbf = global_prob.astype(jnp.bfloat16)
        mixed = product("chij,cjhd->cihd", local_pbf, value_window) + product(
            "chig,ghd->cihd", global_pbf, value_summary
        )
        attn_part = mixed.astype(jnp.bfloat16)
        delta = product("cihd,cihd->chi", grad_part, attn_part)[..., None]
        local_dprob = product("cihd,cjhd->chij", grad_part, value_window)
        global_dprob = product("cihd,ghd->chig", grad_part, value_summary)
        local_dscore = (local_prob * (local_dprob - delta)).astype(jnp.bfloat16)
        global_dscore = (global_prob * (global_dprob - delta)).astype(jnp.bfloat16)
        query_grad = (
            product("chij,cjhd->cihd", local_dscore, key_window)
            + product("chig,ghd->cihd", global_dscore, key_summary)
        ) * score_scale
        key_wgrad = product("chij,cihd->cjhd", local_dscore, query_part) * score_scale
        value_wgrad = product("chij,cihd->cjhd", local_pbf, grad_part)
        key_sgrad = product("chig,cihd->ghd", global_dscore, query_part) * score_scale
        value_sgrad = product("chig,cihd->ghd", global_pbf, grad_part)
        attn_all = lax.dynamic_update_slice(
            attn_all, attn_part.reshape(row_count, group_cols), (anchor, column)
        )
        query_all = lax.dynamic_update_slice(
            query_all, query_grad.reshape(row_count, group_cols), (anchor, column)
        )
        kv_all = lax.dynamic_update_slice(
            kv_all, unwind_window(key_wgrad, blocks, block_rows, group_cols), (anchor, column)
        )
        kv_all = lax.dynamic_update_slice(
            kv_all, unwind_window(value_wgrad, blocks, block_rows, group_cols), (anchor, other)
        )
        summary_all = lax.dynamic_update_slice(
            summary_all, key_sgrad.reshape(glob_rows, group_cols), (anchor, column)
        )
        summary_all = lax.dynamic_update_slice(
            summary_all, value_sgrad.reshape(glob_rows, group_cols), (anchor, other)
        )
        return (attn_all, query_all, kv_all, summary_all)

    start_state = (
        jnp.zeros((row_count, full_width), jnp.bfloat16),
        jnp.zeros((row_count, full_width), jnp.float32),
        jnp.zeros((row_count + 2 * block_rows, 2 * full_width), jnp.float32),
        jnp.zeros((glob_rows, 2 * full_width), jnp.float32),
    )
    return lax.fori_loop(0, heads // per_group, one_group, start_state)


def conv_input_grad(grad_pad, conv_weight, row_count, half_width):
    accum = grad_pad[half_width : half_width + row_count].astype(jnp.float32)
    for shift_index in range(conv_weight.shape[0]):
        start = 2 * half_width - shift_index
        accum = accum + conv_weight[shift_index] * grad_pad[start : start + row_count].astype(
            jnp.float32
        )
    return accum.astype(jnp.bfloat16)


def conv_weight_grad(left_rows, right_pad, row_count, kernel):
    terms = []
    for shift_index in range(kernel):
        terms.append(
            jnp.sum(
                left_rows.astype(jnp.float32)
                * right_pad[shift_index : shift_index + row_count].astype(jnp.float32),
                axis=0,
            )
        )
    return jnp.stack(terms)


def pool_weights(valid_rows, pools):
    pool_valid = valid_rows.reshape(pools, -1).astype(jnp.float32)
    counts = jnp.sum(pool_valid, axis=1, keepdims=True)
    return (pool_valid / jnp.maximum(counts, 1.0)).reshape(-1)


def pooled(key_value, share, pools):
    weighted = key_value.astype(jnp.float32).reshape(pools, -1, key_value.shape[1]) * share.reshape(
        pools, -1, 1
    )
    return jnp.sum(weighted, axis=1).astype(jnp.bfloat16)


def per_device(query_rows, key_rows, value_rows, grad_out, conv_weight, frames, window_links):
    queries = query_rows[0]
    row_count, full_width = queries.shape
    kernel = conv_weight.shape[0]
    half_width = (kernel - 1) // 2
    device = lax.axis_index("tm")
    first_row = device * row_count
    frame_count = frames[0]
    position = first_row + jnp.arange(row_count, dtype=jnp.int32)
    valid_rows = position < frame_count
    masked_grad = jnp.where(valid_rows[:, None], grad_out[0], jnp.zeros_like(grad_out[0]))
    grad_pad = extended(masked_grad, (("tm", 0),), half_width)
    attn_grad = conv_input_grad(grad_pad, conv_weight, row_count, half_width)
    key_value = jnp.concatenate([key_rows[0], value_rows[0]], axis=1)
    padded_kv = extended(key_value, (("tm", 0),), BLK)
    share = pool_weights(valid_rows, SUMM)
    local_summary = pooled(key_value, share, SUMM)
    summary = lax.all_gather(local_summary, "tm", axis=0, tiled=True)
    glob_rows = summary.shape[0]
    pool_size = row_count // SUMM
    summary_ok = jnp.arange(glob_rows, dtype=jnp.int32) * pool_size < frame_count
    pad_pos = first_row - BLK + jnp.arange(row_count + 2 * BLK, dtype=jnp.int32)
    pad_ok = (pad_pos >= 0) & (pad_pos < frame_count)
    attn_out, query_grad, kv_grad_pad, summary_grad = block_pass(
        queries, padded_kv, pad_ok, window_links[0], summary, summary_ok, attn_grad, BLK, H
    )
    attn_pad = extended(attn_out, (("tm", 0),), half_width)
    kernel_grad = conv_weight_grad(masked_grad, attn_pad, row_count, kernel)
    summed = lax.psum(summary_grad.astype(jnp.bfloat16), "tm").astype(jnp.float32)
    own_rows = lax.dynamic_slice_in_dim(summed, device * SUMM, SUMM, 0)
    upper_rim = kv_grad_pad[:BLK]
    lower_rim = kv_grad_pad[BLK + row_count :]
    center = kv_grad_pad[BLK : BLK + row_count]
    from_below = passed_along(upper_rim.astype(jnp.bfloat16), "tm", -1).astype(upper_rim.dtype)
    from_above = passed_along(lower_rim.astype(jnp.bfloat16), "tm", 1).astype(lower_rim.dtype)
    center = center + from_above + from_below
    center = center + jnp.repeat(own_rows, pool_size, axis=0) * share[:, None]
    conv_total = lax.psum(kernel_grad, ("dp", "tm"))
    return (
        query_grad.astype(jnp.bfloat16)[None],
        center[:, :full_width].astype(jnp.bfloat16)[None],
        center[:, full_width:].astype(jnp.bfloat16)[None],
        conv_total,
    )


def solution(mesh):
    placed = (
        P("dp", "tm", None),
        P("dp", "tm", None),
        P("dp", "tm", None),
        P("dp", "tm", None),
        P(),
        P("dp"),
        P("dp", "tm", None),
    )
    return jax.shard_map(
        per_device,
        mesh=mesh,
        in_specs=placed,
        out_specs=(P("dp", "tm", None), P("dp", "tm", None), P("dp", "tm", None), P()),
        check_vma=False,
    )
```

profile of v0, /device:TPU:2, one launch (start us, length us, event | category | flops | bytes accessed | tf_op | source)
XLA Modules:
  0.0 833.8 jit_solution(9945736735633712515)
XLA Ops:
  8.1 2.0 multiply_reduce_fusion
  10.2 1.1 copy.102
  11.3 1.1 copy.103
  12.5 7.8 collective-permute-start.1
  20.3 1.9 collective-permute-start
  22.4 1.1 copy.105
  24.4 3.9 collective-permute-start.2
  28.3 1.9 collective-permute-start.3
  33.7 3.5 collective-permute-done.3
  37.1 4.1 fusion.46
  41.2 1.3 pad_maximum_fusion
  42.6 142.5 %all-gather.2.cloned.1.call-done = bf16[256,2048]{1,0:T(8,128)(2,1)} async-done(((bf16[8,2048]{1,0:T(8,128)(2,1)}), bf16[256,2048]{1,0:T(8,128)(2,1)}) %all-gather.2.cloned.1.call-update) | async-done | bytes 1048592 | tf_op jit(solution)/shard_map/all_gather | solution.py:206
  185.0 2.3 copy.106
  188.1 1.1 broadcast_in_dim.103
  189.2 2.0 broadcast_in_dim.102
  191.2 30.1 %while.22 = (s32[]{:T(128)}, bf16[128,1024]{0,1:T(8,128)(2,1)S(1)}, bf16[128,1024]{1,0:T(8,128)(2,1)}, f32[384,2048]{1,0:T(8,128)}, bf16[256,2048]{0,1:T(8,128)(...) while((s32[]{:T(128)}, bf16[128,1024]{0,1:T(8,128)(2,1)S(1)}, ...), condition=%wide.region_7.8_spmd.clone, body=%wide.region_2.7_spmd.clone.sunk | while | flops 515111936 | bytes 43573404 | solution.py:150
  191.9 1.1 constant_dynamic-slice_fusion.10
  193.0 1.3 constant_dynamic-slice_fusion.9
  205.3 1.0 constant_dynamic-update-slice_fusion.17
  207.0 1.1 constant_dynamic-slice_fusion.10
  208.0 1.3 constant_dynamic-slice_fusion.9
  219.4 1.0 constant_dynamic-update-slice_fusion.16
  221.4 3.1 collective-permute-start.6
  224.5 2.8 collective-permute-start.7
  227.3 2.2 convert.8
  229.6 3.1 collective-permute-start.4
  232.7 3.0 collective-permute-start.5
  235.8 2.3 fusion.55
  238.1 164.6 %psum.15 = f32[9,1024]{1,0:T(8,128)} all-reduce(f32[9,1024]{1,0:T(8,128)S(1)} %stack.39), channel_id=1, replica_groups=mesh['dp'=16,'tm'=32] {'dp','tm'}, use_global_device_ids=true, to_apply=%region_18.19 | all-reduce | flops 9216 | bytes 73728 | tf_op jit(solution)/shard_map/psum | solution.py:226
  402.8 420.3 %all-reduce.8.cloned.1.call-done = bf16[256,2048]{0,1:T(8,128)(2,1)} async-done(((bf16[256,2048]{0,1:T(8,128)(2,1)}), bf16[256,2048]{0,1:T(8,128)(2,1)}) %all-reduce.8.cloned.1.call-update) | async-done | bytes 1048592 | tf_op jit(solution)/shard_map/psum | solution.py:217
  823.0 1.2 dynamic-slice_convert_fusion
  824.6 1.5 fusion.37
  (141 shorter events, 28.5 us)
Async XLA Ops:
  7.2 23.1 %copy-start.10 = (s32[1,1,2]{2,1,0:T(1,128)S(1)}, s32[1,1,2]{2,1,0:T(1,128)}, u32[]{:S(2)}) copy-start(s32[1,1,2]{2,1,0:T(1,128)} %param.15) | copy-start | bytes 28
  7.2 25.0 %copy-start.9 = (f32[9,1024]{1,0:T(8,128)S(1)}, f32[9,1024]{1,0:T(8,128)}, u32[]{:S(2)}) copy-start(f32[9,1024]{1,0:T(8,128)} %param.13) | copy-start | bytes 110596
  7.2 25.0 %copy-start.6 = (bf16[1,128,1024]{2,1,0:T(8,128)(2,1)S(1)}, bf16[1,128,1024]{2,1,0:T(8,128)(2,1)}, u32[]{:S(2)}) copy-start(bf16[1,128,1024]{2,1,0:T(8,128)(2,1)} %param.9) | copy-start | bytes 786436
  7.2 177.9 %all-gather.2.cloned.1.call-start = ((), (), s32[]{:S(2)}) async-start(), calls=%async_computation | async-start | bytes 1081344 | tf_op jit(solution)/shard_map/all_gather | solution.py:206
  10.1 812.9 %all-reduce.8.cloned.1.call-start = ((), (), s32[]{:S(2)}) async-start(), calls=%async_computation.1 | async-start | bytes 2097152 | tf_op jit(solution)/shard_map/psum | solution.py:217
  12.5 28.7 %collective-permute-start.1 = (bf16[128,2048]{0,1:T(8,128)(2,1)S(1)}, bf16[128,2048]{0,1:T(8,128)(2,1)S(1)}, u32[]{:S(2)}, u32[]{:S(2)}) collective-permute-start(bf16[128,2048]{0,1:T(8,128)(2,1)S(1)} %pad_maximum_fusion.1), channel_id=1, source_target_pairs={{1,0},{2,1},{3,2},{4,3},{5,4},{6,5},{7,6},{8,7},{9,8},{10,9},{11,1... | collective-permute-start | bytes 1572872 | tf_op jit(solution)/shard_map/ppermute | solution.py:24
  20.3 20.9 %collective-permute-start = (bf16[128,2048]{0,1:T(8,128)(2,1)S(1)}, bf16[128,2048]{0,1:T(8,128)(2,1)S(1)}, u32[]{:S(2)}, u32[]{:S(2)}) collective-permute-start(bf16[128,2048]{0,1:T(8,128)(2,1)S(1)} %pad_maximum_fusion.1), channel_id=1, source_target_pairs={{0,1},{1,2},{2,3},{3,4},{4,5},{5,6},{6,7},{7,8},{8,9},{9,10},{10,1... | collective-permute-start | bytes 1572872 | tf_op jit(solution)/shard_map/ppermute | solution.py:22
  23.5 19.1 %copy-start.4 = (bf16[1,128,1024]{1,2,0:T(8,128)(2,1)}, bf16[1,128,1024]{1,2,0:T(8,128)(2,1)S(1)}, u32[]{:S(2)}) copy-start(bf16[1,128,1024]{1,2,0:T(8,128)(2,1)S(1)} %copy.105) | copy-start | bytes 786436
  24.4 9.3 %collective-permute-start.2 = (bf16[4,1024]{0,1:T(8,128)(2,1)}, bf16[4,1024]{0,1:T(8,128)(2,1)S(1)}, u32[]{:S(2)}, u32[]{:S(2)}) collective-permute-start(bf16[4,1024]{0,1:T(8,128)(2,1)} %get-tuple-element.388), channel_id=1, source_target_pairs={{1,0},{2,1},{3,2},{4,3},{5,4},{6,5},{7,6},{8,7},{9,8},{10,9},{11,1... | collective-permute-start | bytes 24584 | tf_op jit(solution)/shard_map/ppermute | solution.py:24
  28.3 8.8 %collective-permute-start.3 = (bf16[4,1024]{0,1:T(8,128)(2,1)S(1)}, bf16[4,1024]{0,1:T(8,128)(2,1)}, u32[]{:S(2)}, u32[]{:S(2)}) collective-permute-start(bf16[4,1024]{0,1:T(8,128)(2,1)S(1)} %get-tuple-element.389), channel_id=1, source_target_pairs={{0,1},{1,2},{2,3},{3,4},{4,5},{5,6},{6,7},{7,8},{8,9},{9,10},{10,1... | collective-permute-start | bytes 24584 | tf_op jit(solution)/shard_map/ppermute | solution.py:22
  191.2 5.3 copy-start.2
  197.9 1.8 copy-start.7
  199.8 1.0 copy-start.8
  199.8 1.0 copy-start
  202.6 3.7 copy-start.1
  202.6 3.7 copy-start.3
  206.2 5.3 copy-start.2
  213.0 1.8 copy-start.7
  214.8 1.0 copy-start.8
  214.9 1.0 copy-start
  217.6 3.7 copy-start.1
  217.6 3.6 copy-start.3
  221.4 14.3 %collective-permute-start.6 = (bf16[4,1024]{0,1:T(8,128)(2,1)S(1)}, bf16[4,1024]{0,1:T(8,128)(2,1)S(1)}, u32[]{:S(2)}, u32[]{:S(2)}) collective-permute-start(bf16[4,1024]{0,1:T(8,128)(2,1)S(1)} %get-tuple-element.386), channel_id=1, source_target_pairs={{0,1},{1,2},{2,3},{3,4},{4,5},{5,6},{6,7},{7,8},{8,9},{9,10},{10,1... | collective-permute-start | bytes 24584 | tf_op jit(solution)/shard_map/ppermute | solution.py:22
  224.5 11.2 %collective-permute-start.7 = (bf16[4,1024]{0,1:T(8,128)(2,1)S(1)}, bf16[4,1024]{0,1:T(8,128)(2,1)S(1)}, u32[]{:S(2)}, u32[]{:S(2)}) collective-permute-start(bf16[4,1024]{0,1:T(8,128)(2,1)S(1)} %get-tuple-element.387), channel_id=1, source_target_pairs={{1,0},{2,1},{3,2},{4,3},{5,4},{6,5},{7,6},{8,7},{9,8},{10,9},{11,1... | collective-permute-start | bytes 24584 | tf_op jit(solution)/shard_map/ppermute | solution.py:24
  227.3 8.5 %copy-start.5 = (bf16[1,128,1024]{1,2,0:T(8,128)(2,1)S(1)}, bf16[1,128,1024]{1,2,0:T(8,128)(2,1)}, u32[]{:S(2)}) copy-start(bf16[1,128,1024]{1,2,0:T(8,128)(2,1)} %copy-done.4) | copy-start | bytes 786436
  229.6 595.0 %collective-permute-start.4 = (bf16[128,2048]{1,0:T(8,128)(2,1)S(1)}, bf16[128,2048]{1,0:T(8,128)(2,1)S(1)}, u32[]{:S(2)}, u32[]{:S(2)}) collective-permute-start(bf16[128,2048]{1,0:T(8,128)(2,1)S(1)} %get-tuple-element.382), channel_id=1, source_target_pairs={{0,1},{1,2},{2,3},{3,4},{4,5},{5,6},{6,7},{7,8},{8,9},{9,10},{10,1... | collective-permute-start | bytes 1572872 | tf_op jit(solution)/shard_map/ppermute | solution.py:34
  232.7 591.9 %collective-permute-start.5 = (bf16[128,2048]{1,0:T(8,128)(2,1)S(1)}, bf16[128,2048]{1,0:T(8,128)(2,1)S(1)}, u32[]{:S(2)}, u32[]{:S(2)}) collective-permute-start(bf16[128,2048]{1,0:T(8,128)(2,1)S(1)} %get-tuple-element.383), channel_id=1, source_target_pairs={{1,0},{2,1},{3,2},{4,3},{5,4},{6,5},{7,6},{8,7},{9,8},{10,9},{11,1... | collective-permute-start | bytes 1572872 | tf_op jit(solution)/shard_map/ppermute | solution.py:34
Sparse Core Ops, SparseCore 0:
  12.9 172.1 all-gather.1
  221.4 601.5 all-reduce.7
where the time goes:
time: 835 us; the launch traced here: 834 us
  waiting for transfers between devices  567 us (68%)
  blocking collectives  165 us (20%)
  local copies, waits for them, and re-layouts  30.6 us (4%)
  starting transfers between devices  27.6 us (3%)
  other arithmetic  19.8 us (2%)
  between operations  16.3 us (2%)
    psum x1, waiting for transfers between devices, per_device(): lax.psum(summary_grad.astype(jnp.bfloat16), 'tm').astype(jnp.float32)  420 us
    psum x1, blocking collectives, per_device(): conv_total = lax.psum(kernel_grad, ('dp', 'tm'))  165 us
    all_gather x1, waiting for transfers between devices, per_device(): summary = lax.all_gather(local_summary, 'tm', axis=0, tiled=True)  142 us
  transfers between devices with their start and end apart: 10, of which 4 were waited for; matrix products, arithmetic and copies ran while one was open for 2% of the time, Pallas kernels for 0%

commit v1 on v0

v1 whole, which is shorter than its diff:
```python
import functools

import jax
import jax.numpy as jnp
from jax import lax
from jax.experimental import pallas as pl
from jax.experimental.pallas import tpu as pltpu
from jax.sharding import Mesh
from jax.sharding import PartitionSpec as P

H = 8
HD = 128
BLK = 128
POOL = 16
SUMM = BLK // POOL
KW = 9
HALF = 4
WIN = 3 * BLK
ROWS = WIN + 256
SCALE = HD ** (-0.5)
MASKED = -1e30
AXES = (("zl", 8), ("core", 2), ("y", 4), ("zh", 2), ("x", 4))
DP = ("zl", "core")
TM = ("y", "zh", "x")
PLANE = ("y", "x")
LINE = ("zl", "core", "zh")


def pack_kernel(info, k_ref, v_ref, go_ref, packed_ref, summary_ref):
    first, frame_count = info[0], info[1]
    row = first + lax.broadcasted_iota(jnp.int32, (BLK, 1), 0)
    grad = go_ref[...].astype(jnp.float32)
    grad = jnp.where(row < frame_count, grad, 0.0).astype(jnp.bfloat16)
    packed_ref[0, :BLK, :] = k_ref[...]
    packed_ref[1, :BLK, :] = v_ref[...]
    packed_ref[0, BLK:, :] = grad[BLK - 8 :]
    packed_ref[1, BLK:, :] = grad[:8]
    pool = lax.broadcasted_iota(jnp.int32, (SUMM, 1, 1), 0) * POOL + first
    count = jnp.clip(frame_count - pool, 0, POOL)
    frame = pool + lax.broadcasted_iota(jnp.int32, (SUMM, POOL, 1), 1)
    share = jnp.where(
        frame < frame_count, 1.0 / jnp.maximum(count, 1).astype(jnp.float32), 0.0
    )
    for side, ref in ((0, k_ref), (1, v_ref)):
        rows = ref[...].astype(jnp.float32).reshape(SUMM, POOL, ref.shape[1])
        summary_ref[side] = jnp.sum(rows * share, axis=1).astype(jnp.bfloat16)


def pack(info, keys, values, grad_out):
    width = keys.shape[1]
    whole = pl.BlockSpec(memory_space=pltpu.VMEM)
    return pl.pallas_call(
        pack_kernel,
        out_shape=(
            jax.ShapeDtypeStruct((2, BLK + 8, width), jnp.bfloat16),
            jax.ShapeDtypeStruct((2, SUMM, width), jnp.bfloat16),
        ),
        in_specs=[pl.BlockSpec(memory_space=pltpu.SMEM), whole, whole, whole],
        out_specs=(whole, whole),
        compiler_params=pltpu.CompilerParams(vmem_limit_bytes=32 * 2**20),
        name="pack",
    )(info, keys, values, grad_out)


def dot(left, right, contract):
    return lax.dot_general(
        left, right, (contract, ((), ())), preferred_element_type=jnp.float32
    )


NN = ((1,), (0,))
NT = ((1,), (1,))
TN = ((0,), (0,))


def attend_kernel(
    info,
    q_ref,
    k_ref,
    v_ref,
    go_ref,
    prev_ref,
    next_ref,
    prev_go_ref,
    next_go_ref,
    summary_ref,
    w_ref,
    dq_ref,
    center_ref,
    to_prev_ref,
    to_next_ref,
    dsum_ref,
    conv_ref,
    bias_ref,
):
    first, frame_count, left, right, z_half = (info[i] for i in range(5))

    @pl.when(pl.program_id(0) == 0)
    def _():
        row = lax.broadcasted_iota(jnp.int32, (BLK, HD), 0)
        seen_left = jnp.where(left == 1, frame_count - first + BLK, 0)
        seen_right = jnp.where(right == 1, frame_count - first - BLK, 0)
        for part, seen in enumerate((seen_left, frame_count - first, seen_right)):
            bias_ref[pl.ds(part * BLK, BLK), :] = jnp.where(row < seen, 0.0, MASKED)
        row = lax.broadcasted_iota(jnp.int32, (ROWS - WIN, HD), 0)
        source, half, pool = row >> 4, (row >> 3) & 1, row & 7
        block = ((source >> 2) * 2 + (half ^ z_half)) * 4 + (source & 3)
        start = (block * SUMM + pool) * POOL
        bias_ref[WIN:, :] = jnp.where(start < frame_count, 0.0, MASKED)

    summary = summary_ref[...]
    keys = jnp.concatenate(
        [prev_ref[0], k_ref[...], next_ref[0], summary[:, 0].reshape(-1, HD)], axis=0
    )
    values = jnp.concatenate(
        [prev_ref[1], v_ref[...], next_ref[1], summary[:, 1].reshape(-1, HD)], axis=0
    )
    queries = q_ref[...]

    row = first + lax.broadcasted_iota(jnp.int32, (BLK, 1), 0)
    grad = jnp.where(row < frame_count, go_ref[...].astype(jnp.float32), 0.0)
    reach = jnp.concatenate(
        [prev_go_ref[0].astype(jnp.float32), grad, next_go_ref[0].astype(jnp.float32)],
        axis=0,
    )
    shifted = [reach[8 + HALF - j : 8 + HALF - j + BLK] for j in range(KW)]
    total = grad
    for j in range(KW):
        total = total + w_ref[j : j + 1, :] * shifted[j]
    grad_attn = total.astype(jnp.bfloat16)

    scores = dot(keys, queries, NT) * SCALE + bias_ref[...]
    top = jnp.max(scores, axis=0, keepdims=True)
    weight = jnp.exp(scores - top)
    prob = weight * (1.0 / jnp.sum(weight, axis=0, keepdims=True))
    prob_bf = prob.astype(jnp.bfloat16)
    attn = dot(prob_bf, values, TN).astype(jnp.bfloat16).astype(jnp.float32)
    delta = jnp.sum(
        (grad_attn.astype(jnp.float32) * attn).T, axis=0, keepdims=True
    )
    dprob = dot(values, grad_attn, NT)
    dscore = (prob * (dprob - delta)).astype(jnp.bfloat16)

    dq_ref[...] = (dot(dscore, keys, TN) * SCALE).astype(jnp.bfloat16)
    for side, part in (
        (0, dot(dscore, queries, NN) * SCALE),
        (1, dot(prob_bf, grad_attn, NN)),
    ):
        to_prev_ref[side] = part[:BLK].astype(jnp.bfloat16)
        center_ref[side] = part[BLK : 2 * BLK]
        to_next_ref[side] = part[2 * BLK : WIN].astype(jnp.bfloat16)
        dsum_ref[:, side] = (
            part[WIN:].astype(jnp.bfloat16).reshape(dsum_ref.shape[0], 2 * SUMM, HD)
        )
    conv_ref[...] = jnp.concatenate(
        [jnp.sum(attn * shifted[j], axis=0, keepdims=True) for j in range(KW)]
        + [jnp.zeros((16 - KW, HD), jnp.float32)],
        axis=0,
    )


def attend(info, queries, keys, values, grad_out, prev, next_, summary, taps):
    width = queries.shape[1]
    own = pl.BlockSpec((BLK, HD), lambda h: (0, h))
    pair = pl.BlockSpec((2, BLK, HD), lambda h: (0, 0, h))
    many = pl.BlockSpec((16, 2, 2 * SUMM, HD), lambda h: (0, 0, 0, h))
    rim = BLK // 8
    return pl.pallas_call(
        attend_kernel,
        grid=(width // HD,),
        out_shape=(
            jax.ShapeDtypeStruct((BLK, width), jnp.bfloat16),
            jax.ShapeDtypeStruct((2, BLK, width), jnp.float32),
            jax.ShapeDtypeStruct((2, BLK, width), jnp.bfloat16),
            jax.ShapeDtypeStruct((2, BLK, width), jnp.bfloat16),
            jax.ShapeDtypeStruct((16, 2, 2 * SUMM, width), jnp.bfloat16),
            jax.ShapeDtypeStruct((16, width), jnp.float32),
        ),
        in_specs=[
            pl.BlockSpec(memory_space=pltpu.SMEM),
            own,
            own,
            own,
            own,
            pair,
            pair,
            pl.BlockSpec((1, 8, HD), lambda h: (0, rim, h)),
            pl.BlockSpec((1, 8, HD), lambda h: (1, rim, h)),
            many,
            pl.BlockSpec((KW, HD), lambda h: (0, h)),
        ],
        out_specs=(
            own,
            pair,
            pair,
            pair,
            many,
            pl.BlockSpec((16, HD), lambda h: (0, h)),
        ),
        scratch_shapes=[pltpu.VMEM((ROWS, HD), jnp.float32)],
        compiler_params=pltpu.CompilerParams(vmem_limit_bytes=32 * 2**20),
        cost_estimate=pl.CostEstimate(
            flops=6 * 2 * ROWS * BLK * width,
            bytes_accessed=8 * 2**20,
            transcendentals=ROWS * BLK * (width // HD),
        ),
        name="attend",
    )(info, queries, keys, values, grad_out, prev, next_, prev, next_, summary, taps)


def spread(block, axes, count):
    return lax.all_to_all(
        jnp.broadcast_to(block[None], (count,) + block.shape), axes, 0, 0, tiled=True
    )


def per_device(query_rows, key_rows, value_rows, grad_out, conv_weight, frames, window_links):
    queries, keys, values, grad = query_rows[0], key_rows[0], value_rows[0], grad_out[0]
    device = lax.axis_index(TM)
    z_half = lax.axis_index("zh")
    last = lax.axis_size(TM) - 1
    upward = [(i, i + 1) for i in range(last)]
    downward = [(i + 1, i) for i in range(last)]
    swap = [(0, 1), (1, 0)]
    first = device * BLK
    links = window_links[0, 0]
    info = jnp.stack(
        [
            first,
            frames[0],
            jnp.where(device > 0, links[0], 0),
            jnp.where(device < last, links[1], 0),
            z_half,
        ]
    ).astype(jnp.int32)

    packed, own_summary = pack(info, keys, values, grad)
    other_summary = lax.ppermute(own_summary, "zh", swap)
    prev = lax.ppermute(packed, TM, upward)
    next_ = lax.ppermute(packed, TM, downward)
    summary = spread(jnp.concatenate([own_summary, other_summary], axis=1), PLANE, 16)

    dq, center, to_prev, to_next, dsum, conv = attend(
        info, queries, keys, values, grad, prev, next_, summary, conv_weight
    )
    from_prev = lax.ppermute(to_next, TM, upward)
    from_next = lax.ppermute(to_prev, TM, downward)

    dsum = lax.all_to_all(dsum, PLANE, 0, 0, tiled=True)
    dsum = jnp.sum(dsum.astype(jnp.float32), axis=0)
    other = lax.ppermute(dsum[:, SUMM:].astype(jnp.bfloat16), "zh", swap)
    dsum = dsum[:, :SUMM] + other.astype(jnp.float32)

    tap = lax.all_to_all(conv[:, None], PLANE, 0, 0, tiled=True)
    tap = jnp.sum(tap, axis=0)
    tap = jnp.sum(spread(tap, LINE, 32), axis=0)
    taps = spread(tap, PLANE, 16)[:KW, 0]

    row = first + jnp.arange(BLK, dtype=jnp.int32)
    valid = (row < frames[0]).astype(jnp.float32).reshape(SUMM, POOL)
    share = valid / jnp.maximum(jnp.sum(valid, axis=1, keepdims=True), 1.0)
    spread_sum = (dsum[:, :, None] * share[None, :, :, None]).reshape(center.shape)
    total = center + from_prev.astype(jnp.float32) + from_next.astype(jnp.float32)
    total = (total + spread_sum).astype(jnp.bfloat16)
    return dq[None], total[0][None], total[1][None], taps


def solution(mesh):
    names, sizes = zip(*AXES, strict=True)
    fine = Mesh(mesh.devices.reshape(sizes), names)
    rows = P(DP, TM, None)
    return jax.shard_map(
        per_device,
        mesh=fine,
        in_specs=(rows, rows, rows, rows, P(), P(DP), rows),
        out_specs=(rows, rows, rows, P()),
        check_vma=False,
    )
```

time: 835 us -> 234 us (0.28)
  the two profiles are of different devices: /device:TPU:2 before, /device:TPU:32 now
where the time goes in v1:
time: 234 us; the launch traced here: 233 us
  blocking collectives  84.7 us (36%)
  waiting for transfers between devices  71.9 us (31%)
  starting transfers between devices  45.2 us (19%)
  local copies, waits for them, and re-layouts  13.2 us (6%)
  Pallas kernels  13.1 us (6%)
  between operations  2.66 us (1%)
    all_to_all x1, blocking collectives, per_device(): tap = lax.all_to_all(conv[:, None], PLANE, 0, 0, tiled=True)  63.3 us
    ppermute x1, waiting for transfers between devices, per_device(): other = lax.ppermute(dsum[:, SUMM:].astype(jnp.bfloat16), 'zh', swap)  34.7 us
    all_to_all x1, blocking collectives, spread(): lax.all_to_all(jnp.broadcast_to(block[None], (count,) + block.shape), axe...  21.5 us
    ppermute x1, waiting for transfers between devices, per_device(): next_ = lax.ppermute(packed, TM, downward)  18.3 us
    ppermute x1, starting transfers between devices, per_device(): other_summary = lax.ppermute(own_summary, 'zh', swap)  14.8 us
    all_to_all x1, waiting for transfers between devices, per_device(): dsum = lax.all_to_all(dsum, PLANE, 0, 0, tiled=True)  12.5 us
    pallas_call x1, Pallas kernels, attend(): pl.pallas_call(attend_kernel, grid=(width // HD,), out_shape=(jax.ShapeDt...  12.3 us
    all_to_all x2, starting transfers between devices, spread(): lax.all_to_all(jnp.broadcast_to(block[None], (count,) + block.shape), axe...  11.2 us
  transfers between devices with their start and end apart: 9, of which 5 were waited for; matrix products, arithmetic and copies ran while one was open for 1% of the time, Pallas kernels for 0%

profile of v1, /device:TPU:32, one launch (start us, length us, event | category | flops | bytes accessed | tf_op | source)
XLA Modules:
  0.0 232.9 jit_solution(1614299577806648944)
XLA Ops:
  1.3 1.3 fusion.3
  3.9 0.9 copy-done.1
  4.8 0.9 copy-done.3
  5.8 0.9 copy-done.5
  6.7 0.8 pack.1
  7.6 14.8 %collective-permute-start.2 = (bf16[2,8,1024]{2,1,0:T(8,128)(2,1)S(1)}, bf16[2,8,1024]{2,1,0:T(8,128)(2,1)S(1)}, u32[]{:S(2)}, u32[]{:S(2)}) collective-permute-start(bf16[2,8,1024]{2,1,0:T(8,128)(2,1)S(1)} %get-tuple-element.13), channel_id=1, source_target_pairs={{0,4},{4,0},{1,5},{5,1},{2,6},{6,2},{3,7},{7,3},{8,12},{12,8},{9,1... | collective-permute-start | bytes 98312 | tf_op jit(solution)/shard_map/ppermute | solution.py:238
  22.4 2.3 %collective-permute-done.2 = bf16[2,8,1024]{2,1,0:T(8,128)(2,1)S(1)} collective-permute-done((bf16[2,8,1024]{2,1,0:T(8,128)(2,1)S(1)}, bf16[2,8,1024]{2,1,0:T(8,128)(2,1)S(1)}, u32[]{:S(2)}, u32[]{:S(2)}) %collective-permute-start.2) | collective-permute-done | bytes 32800 | tf_op jit(solution)/shard_map/ppermute | solution.py:238
  24.7 1.1 broadcast_in_dim.10
  25.9 7.2 %all-to-all-start = ((bf16[16,2,16,1024]{3,2,1,0:T(8,128)(2,1)}), bf16[16,2,16,1024]{3,2,1,0:T(8,128)(2,1)S(1)}, u32[]{:S(2)}, u32[]{:S(2)}) async-start(bf16[16,2,16,1024]{3,2,1,0:T(8,128)(2,1)} %broadcast_in_dim.10), calls=%async_computation | async-start | bytes 2097152 | tf_op jit(solution)/shard_map/all_to_all | solution.py:212
  33.0 1.3 collective-permute-start.1
  34.3 4.6 %collective-permute-start = (bf16[2,136,1024]{2,1,0:T(8,128)(2,1)S(1)}, bf16[2,136,1024]{2,1,0:T(8,128)(2,1)S(1)}, u32[]{:S(2)}, u32[]{:S(2)}) collective-permute-start(bf16[2,136,1024]{2,1,0:T(8,128)(2,1)S(1)} %get-tuple-element.12), channel_id=1, source_target_pairs={{0,1},{1,2},{2,3},{3,4},{4,5},{5,6},{6,7},{7,8},{8,9},{9,10},{10,1... | collective-permute-start | bytes 1671176 | tf_op jit(solution)/shard_map/ppermute | solution.py:239
  38.9 18.3 %collective-permute-done.1.next_ref.next_go_ref = bf16[2,136,1024]{2,1,0:T(8,128)(2,1)S(1)} collective-permute-done((bf16[2,136,1024]{2,1,0:T(8,128)(2,1)S(1)}, bf16[2,136,1024]{2,1,0:T(8,128)(2,1)S(1)}, u32[]{:S(2)}, u32[]{:S(2)}) %collective-permute-start.1) | collective-permute-done | bytes 557088 | tf_op jit(solution)/shard_map/ppermute | solution.py:240
  57.2 0.9 copy-done.4
  58.2 0.9 copy-done.6
  59.1 0.9 copy-done.7
  60.1 12.3 %attend.1 = (bf16[128,1024]{1,0:T(8,128)(2,1)}, f32[2,128,1024]{2,1,0:T(8,128)S(1)}, bf16[2,128,1024]{2,1,0:T(8,128)(2,1)S(1)}, bf16[2,128,1024]{2,1,0:T(8,128)(...) custom-call(s32[5]{0:T(128)S(1)} %stack.19.info, bf16[128,1024]{1,0:T(8,128)(2,1)S(1)} %bitcast.30, ...), custom_call_target="tpu_custom_call" | custom-call | flops 1006632960 | bytes 8388608 | tf_op jit(solution)/shard_map/attend/pallas_call | solution.py:168
  72.4 1.0 copy-done
  73.4 0.8 copy-done.9
  74.2 0.8 copy-done.11
  75.1 63.3 %all_to_all.25 = f32[16,1,1024]{2,1,0:T(1,128)S(1)} all-to-all(f32[16,1,1024]{2,1,0:T(1,128)S(1)} %copy.13), channel_id=1, replica_groups=mesh['zl'=8,'core'=2,'y'=4,'zh'=2,'x'=4] {'y','x'}, dimensions={0} | all-to-all | bytes 131072 | tf_op jit(solution)/shard_map/all_to_all | solution.py:254
  138.5 21.5 %all_to_all.26 = f32[32,1,1024]{2,1,0:T(1,128)S(1)} all-to-all(f32[32,1,1024]{2,1,0:T(1,128)S(1)} %broadcast_in_dim.13), channel_id=1, replica_groups=mesh['zl'=8,'core'=2,'y'=4,'zh'=2,'x'=4] {'zl','core','zh'}, dimensions={0} | all-to-all | bytes 262144 | tf_op jit(solution)/shard_map/all_to_all | solution.py:212
  160.0 3.8 %all-to-all-start.1 = ((bf16[16,2,16,1024]{3,2,1,0:T(8,128)(2,1)}), bf16[16,2,16,1024]{3,2,1,0:T(8,128)(2,1)S(1)}, u32[]{:S(2)}, u32[]{:S(2)}) async-start(bf16[16,2,16,1024]{3,2,1,0:T(8,128)(2,1)} %copy-done), calls=%async_computation.1 | async-start | bytes 2097152 | tf_op jit(solution)/shard_map/all_to_all | solution.py:249
  163.9 4.5 %collective-permute-start.3 = (bf16[2,128,1024]{2,1,0:T(8,128)(2,1)S(1)}, bf16[2,128,1024]{2,1,0:T(8,128)(2,1)}, u32[]{:S(2)}, u32[]{:S(2)}) collective-permute-start(bf16[2,128,1024]{2,1,0:T(8,128)(2,1)S(1)} %copy-done.12), channel_id=1, source_target_pairs={{0,1},{1,2},{2,3},{3,4},{4,5},{5,6},{6,7},{7,8},{8,9},{9,10},{10,1... | collective-permute-start | bytes 1572872 | tf_op jit(solution)/shard_map/ppermute | solution.py:246
  168.4 1.3 collective-permute-start.4
  169.8 12.5 %all-to-all-done.1 = bf16[16,2,16,1024]{3,2,1,0:T(8,128)(2,1)S(1)} async-done(((bf16[16,2,16,1024]{3,2,1,0:T(8,128)(2,1)}), bf16[16,2,16,1024]{3,2,1,0:T(8,128)(2,1)S(1)}, u32[]{:S(2)}, u32[]{:S(2)}) %all-to-all-start.1) | async-done | bytes 1048608 | tf_op jit(solution)/shard_map/all_to_all | solution.py:249
  182.3 0.7 broadcast_in_dim.14
  183.0 4.0 %all-to-all-start.4 = ((f32[16,1,1024]{2,1,0:T(1,128)}), f32[16,1,1024]{2,1,0:T(1,128)S(1)}, u32[]{:S(2)}, u32[]{:S(2)}) async-start(f32[16,1,1024]{2,1,0:T(1,128)} %broadcast_in_dim.14), calls=%async_computation.4 | async-start | bytes 131072 | tf_op jit(solution)/shard_map/all_to_all | solution.py:212
  187.2 3.7 %collective-permute-start.5 = (bf16[2,8,1024]{2,1,0:T(8,128)(2,1)S(1)}, bf16[2,8,1024]{2,1,0:T(8,128)(2,1)S(1)}, u32[]{:S(2)}, u32[]{:S(2)}) collective-permute-start(bf16[2,8,1024]{2,1,0:T(8,128)(2,1)S(1)} %slice.38), channel_id=1, source_target_pairs={{0,4},{4,0},{1,5},{5,1},{2,6},{6,2},{3,7},{7,3},{8,12},{12,8},{9,1... | collective-permute-start | bytes 98312 | tf_op jit(solution)/shard_map/ppermute | solution.py:251
  191.1 4.1 %all-to-all-done.4 = f32[16,1,1024]{2,1,0:T(1,128)S(1)} async-done(((f32[16,1,1024]{2,1,0:T(1,128)}), f32[16,1,1024]{2,1,0:T(1,128)S(1)}, u32[]{:S(2)}, u32[]{:S(2)}) %all-to-all-start.4) | async-done | bytes 65568 | tf_op jit(solution)/shard_map/all_to_all | solution.py:212
  195.8 34.7 %collective-permute-done.5 = bf16[2,8,1024]{2,1,0:T(8,128)(2,1)S(1)} collective-permute-done((bf16[2,8,1024]{2,1,0:T(8,128)(2,1)S(1)}, bf16[2,8,1024]{2,1,0:T(8,128)(2,1)S(1)}, u32[]{:S(2)}, u32[]{:S(2)}) %collective-permute-start.5) | collective-permute-done | bytes 32800 | tf_op jit(solution)/shard_map/ppermute | solution.py:251
  230.5 1.5 fusion.1
  232.0 0.8 fusion.2
  (36 shorter events, 1.6 us)
Async XLA Ops:
  3.9 1.0 copy-start.1
  4.8 0.9 copy-start.3
  5.8 0.9 copy-start.5
  7.6 17.2 %collective-permute-start.2 = (bf16[2,8,1024]{2,1,0:T(8,128)(2,1)S(1)}, bf16[2,8,1024]{2,1,0:T(8,128)(2,1)S(1)}, u32[]{:S(2)}, u32[]{:S(2)}) collective-permute-start(bf16[2,8,1024]{2,1,0:T(8,128)(2,1)S(1)} %get-tuple-element.13), channel_id=1, source_target_pairs={{0,4},{4,0},{1,5},{5,1},{2,6},{6,2},{3,7},{7,3},{8,12},{12,8},{9,1... | collective-permute-start | bytes 98312 | tf_op jit(solution)/shard_map/ppermute | solution.py:238
  25.8 31.3 %copy-start.2 = (bf16[1,128,1024]{2,1,0:T(8,128)(2,1)S(1)}, bf16[1,128,1024]{2,1,0:T(8,128)(2,1)}, u32[]{:S(2)}) copy-start(bf16[1,128,1024]{2,1,0:T(8,128)(2,1)} %param.8) | copy-start | bytes 786436
  25.9 31.3 %copy-start.8 = (f32[9,1024]{1,0:T(8,128)S(1)}, f32[9,1024]{1,0:T(8,128)}, u32[]{:S(2)}) copy-start(f32[9,1024]{1,0:T(8,128)} %w_ref.1) | copy-start | bytes 110596
  25.9 31.3 %all-to-all-start = ((bf16[16,2,16,1024]{3,2,1,0:T(8,128)(2,1)}), bf16[16,2,16,1024]{3,2,1,0:T(8,128)(2,1)S(1)}, u32[]{:S(2)}, u32[]{:S(2)}) async-start(bf16[16,2,16,1024]{3,2,1,0:T(8,128)(2,1)} %broadcast_in_dim.10), calls=%async_computation | async-start | bytes 2097152 | tf_op jit(solution)/shard_map/all_to_all | solution.py:212
  33.0 24.1 %collective-permute-start.1 = (bf16[2,136,1024]{2,1,0:T(8,128)(2,1)S(1)}, bf16[2,136,1024]{2,1,0:T(8,128)(2,1)S(1)}, u32[]{:S(2)}, u32[]{:S(2)}) collective-permute-start(bf16[2,136,1024]{2,1,0:T(8,128)(2,1)S(1)} %get-tuple-element.12), channel_id=1, source_target_pairs={{1,0},{2,1},{3,2},{4,3},{5,4},{6,5},{7,6},{8,7},{9,8},{10,9},{11,1... | collective-permute-start | bytes 1671176 | tf_op jit(solution)/shard_map/ppermute | solution.py:240
  34.3 22.9 %collective-permute-start = (bf16[2,136,1024]{2,1,0:T(8,128)(2,1)S(1)}, bf16[2,136,1024]{2,1,0:T(8,128)(2,1)S(1)}, u32[]{:S(2)}, u32[]{:S(2)}) collective-permute-start(bf16[2,136,1024]{2,1,0:T(8,128)(2,1)S(1)} %get-tuple-element.12), channel_id=1, source_target_pairs={{0,1},{1,2},{2,3},{3,4},{4,5},{5,6},{6,7},{7,8},{8,9},{9,10},{10,1... | collective-permute-start | bytes 1671176 | tf_op jit(solution)/shard_map/ppermute | solution.py:239
  57.2 1.0 copy-start.4
  58.2 0.9 copy-start.6
  59.1 0.9 copy-start.7
  72.4 1.0 copy-start
  73.4 0.8 copy-start.9
  74.2 0.8 copy-start.11
  160.0 3.9 %copy-start.12 = (bf16[2,128,1024]{2,1,0:T(8,128)(2,1)S(1)}, bf16[2,128,1024]{2,1,0:T(8,128)(2,1)}, u32[]{:S(2)}) copy-start(bf16[2,128,1024]{2,1,0:T(8,128)(2,1)} %copy-done.11) | copy-start | bytes 1572868
  160.0 8.5 %copy-start.10 = (bf16[2,128,1024]{2,1,0:T(8,128)(2,1)S(1)}, bf16[2,128,1024]{2,1,0:T(8,128)(2,1)}, u32[]{:S(2)}) copy-start(bf16[2,128,1024]{2,1,0:T(8,128)(2,1)} %copy-done.9) | copy-start | bytes 1572868
  160.0 22.3 %all-to-all-start.1 = ((bf16[16,2,16,1024]{3,2,1,0:T(8,128)(2,1)}), bf16[16,2,16,1024]{3,2,1,0:T(8,128)(2,1)S(1)}, u32[]{:S(2)}, u32[]{:S(2)}) async-start(bf16[16,2,16,1024]{3,2,1,0:T(8,128)(2,1)} %copy-done), calls=%async_computation.1 | async-start | bytes 2097152 | tf_op jit(solution)/shard_map/all_to_all | solution.py:249
  163.9 66.6 %collective-permute-start.3 = (bf16[2,128,1024]{2,1,0:T(8,128)(2,1)S(1)}, bf16[2,128,1024]{2,1,0:T(8,128)(2,1)}, u32[]{:S(2)}, u32[]{:S(2)}) collective-permute-start(bf16[2,128,1024]{2,1,0:T(8,128)(2,1)S(1)} %copy-done.12), channel_id=1, source_target_pairs={{0,1},{1,2},{2,3},{3,4},{4,5},{5,6},{6,7},{7,8},{8,9},{9,10},{10,1... | collective-permute-start | bytes 1572872 | tf_op jit(solution)/shard_map/ppermute | solution.py:246
  168.4 62.1 %collective-permute-start.4 = (bf16[2,128,1024]{2,1,0:T(8,128)(2,1)S(1)}, bf16[2,128,1024]{2,1,0:T(8,128)(2,1)}, u32[]{:S(2)}, u32[]{:S(2)}) collective-permute-start(bf16[2,128,1024]{2,1,0:T(8,128)(2,1)S(1)} %copy-done.10), channel_id=1, source_target_pairs={{1,0},{2,1},{3,2},{4,3},{5,4},{6,5},{7,6},{8,7},{9,8},{10,9},{11,1... | collective-permute-start | bytes 1572872 | tf_op jit(solution)/shard_map/ppermute | solution.py:247
  183.0 12.2 %all-to-all-start.4 = ((f32[16,1,1024]{2,1,0:T(1,128)}), f32[16,1,1024]{2,1,0:T(1,128)S(1)}, u32[]{:S(2)}, u32[]{:S(2)}) async-start(f32[16,1,1024]{2,1,0:T(1,128)} %broadcast_in_dim.14), calls=%async_computation.4 | async-start | bytes 131072 | tf_op jit(solution)/shard_map/all_to_all | solution.py:212
  187.2 43.3 %collective-permute-start.5 = (bf16[2,8,1024]{2,1,0:T(8,128)(2,1)S(1)}, bf16[2,8,1024]{2,1,0:T(8,128)(2,1)S(1)}, u32[]{:S(2)}, u32[]{:S(2)}) collective-permute-start(bf16[2,8,1024]{2,1,0:T(8,128)(2,1)S(1)} %slice.38), channel_id=1, source_target_pairs={{0,4},{4,0},{1,5},{5,1},{2,6},{6,2},{3,7},{7,3},{8,12},{12,8},{9,1... | collective-permute-start | bytes 98312 | tf_op jit(solution)/shard_map/ppermute | solution.py:251

commit v2 on v1

v2 whole, which is shorter than its diff:
```python
import jax
import jax.numpy as jnp
from jax import lax
from jax.experimental import pallas as pl
from jax.experimental.pallas import tpu as pltpu
from jax.sharding import Mesh
from jax.sharding import PartitionSpec as P

H = 8
HD = 128
BLK = 128
POOL = 16
SUMM = BLK // POOL
KW = 9
HALF = 4
WIN = 3 * BLK
ROWS = WIN + 256
SCALE = HD ** (-0.5)
MASKED = -1e30
VMEM = 56 * 2**20
AXES = (("zl", 8), ("core", 2), ("y", 4), ("zh", 2), ("x", 4))
DP = ("zl", "core")
TM = ("y", "zh", "x")
PLANE = ("y", "x")
LINE = ("zl", "core", "zh")


def place():
    z_half = lax.axis_index("zh")
    return (lax.axis_index("y") * 2 + z_half) * 4 + lax.axis_index("x"), z_half


def pack_kernel(frames, k_ref, v_ref, go_ref, packed_ref, summary_ref):
    first, frame_count = place()[0] * BLK, frames[0]
    row = first + lax.broadcasted_iota(jnp.int32, (BLK, 1), 0)
    grad = go_ref[...].astype(jnp.float32)
    grad = jnp.where(row < frame_count, grad, 0.0)
    packed_ref[:BLK, :] = k_ref[...]
    rims = jnp.concatenate([grad[BLK - HALF :], grad[:HALF]], axis=0)
    packed_ref[BLK:, :] = rims.astype(jnp.bfloat16)
    pool = lax.broadcasted_iota(jnp.int32, (SUMM, 1, 1), 0) * POOL + first
    count = jnp.clip(frame_count - pool, 0, POOL)
    frame = pool + lax.broadcasted_iota(jnp.int32, (SUMM, POOL, 1), 1)
    share = jnp.where(
        frame < frame_count, 1.0 / jnp.maximum(count, 1).astype(jnp.float32), 0.0
    )
    for side, ref in ((0, k_ref), (1, v_ref)):
        rows = ref[...].astype(jnp.float32).reshape(SUMM, POOL, ref.shape[1])
        summary_ref[side] = jnp.sum(rows * share, axis=1).astype(jnp.bfloat16)


def pack(frames, keys, values, grad_out):
    width = keys.shape[1]
    chunk = 256
    own = pl.BlockSpec((BLK, chunk), lambda c: (0, c))
    return pl.pallas_call(
        pack_kernel,
        grid=(width // chunk,),
        out_shape=(
            jax.ShapeDtypeStruct((BLK + 8, width), jnp.bfloat16),
            jax.ShapeDtypeStruct((2, SUMM, width), jnp.bfloat16),
        ),
        in_specs=[pl.BlockSpec(memory_space=pltpu.SMEM), own, own, own],
        out_specs=(
            pl.BlockSpec((BLK + 8, chunk), lambda c: (0, c)),
            pl.BlockSpec((2, SUMM, chunk), lambda c: (0, 0, c)),
        ),
        compiler_params=pltpu.CompilerParams(vmem_limit_bytes=VMEM),
        name="pack",
    )(frames, keys, values, grad_out)


def dot(left, right, contract):
    return lax.dot_general(
        left, right, (contract, ((), ())), preferred_element_type=jnp.float32
    )


NN = ((1,), (0,))
NT = ((1,), (1,))
TN = ((0,), (0,))


def attend_kernel(
    frames,
    links,
    q_ref,
    k_ref,
    v_ref,
    go_ref,
    up_k_ref,
    down_k_ref,
    cross_k_ref,
    up_v_ref,
    down_v_ref,
    cross_v_ref,
    up_go_ref,
    down_go_ref,
    cross_go_ref,
    summary_ref,
    w_ref,
    dq_ref,
    center_ref,
    to_prev_ref,
    to_next_ref,
    cross_dk_ref,
    cross_dv_ref,
    dsum_ref,
    conv_ref,
    bias_ref,
):
    device, z_half = place()
    first, frame_count = device * BLK, frames[0]

    @pl.when(pl.program_id(0) == 0)
    def _():
        row = lax.broadcasted_iota(jnp.int32, (BLK, HD), 0)
        seen_left = jnp.where((links[0] == 1) & (device > 0), frame_count - first + BLK, 0)
        seen_right = jnp.where(links[1] == 1, frame_count - first - BLK, 0)
        for part, seen in enumerate((seen_left, frame_count - first, seen_right)):
            bias_ref[pl.ds(part * BLK, BLK), :] = jnp.where(row < seen, 0.0, MASKED)
        row = lax.broadcasted_iota(jnp.int32, (ROWS - WIN, HD), 0)
        source, half, pool = row >> 4, (row >> 3) & 1, row & 7
        block = ((source >> 2) * 2 + (half ^ z_half)) * 4 + (source & 3)
        start = (block * SUMM + pool) * POOL
        bias_ref[WIN:, :] = jnp.where(start < frame_count, 0.0, MASKED)

    x = lax.axis_index("x")
    low, high = x == 0, x == 3
    summary = summary_ref[...]

    def window(up_ref, own_ref, down_ref, cross_ref):
        cross = cross_ref[...]
        return [
            jnp.where(low, cross, up_ref[...]),
            own_ref[...],
            jnp.where(high, cross, down_ref[...]),
        ]

    keys = jnp.concatenate(
        window(up_k_ref, k_ref, down_k_ref, cross_k_ref) + [summary[:, 0].reshape(-1, HD)],
        axis=0,
    )
    values = jnp.concatenate(
        window(up_v_ref, v_ref, down_v_ref, cross_v_ref) + [summary[:, 1].reshape(-1, HD)],
        axis=0,
    )
    queries = q_ref[...]

    row = first + lax.broadcasted_iota(jnp.int32, (BLK, 1), 0)
    grad = jnp.where(row < frame_count, go_ref[...].astype(jnp.float32), 0.0)
    cross_go = cross_go_ref[...].astype(jnp.float32)
    before = jnp.where(low, cross_go, up_go_ref[...].astype(jnp.float32))
    after = jnp.where(high, cross_go, down_go_ref[...].astype(jnp.float32))
    reach = jnp.concatenate([before[:HALF], grad, after[HALF:]], axis=0)
    shifted = [reach[2 * HALF - j : 2 * HALF - j + BLK] for j in range(KW)]
    total = grad
    for j in range(KW):
        total = total + w_ref[j : j + 1, :] * shifted[j]
    grad_attn = total.astype(jnp.bfloat16)

    scores = dot(keys, queries, NT) * SCALE + bias_ref[...]
    top = jnp.max(scores, axis=0, keepdims=True)
    weight = jnp.exp(scores - top)
    prob = weight * (1.0 / jnp.sum(weight, axis=0, keepdims=True))
    prob_bf = prob.astype(jnp.bfloat16)
    attn = dot(prob_bf, values, TN).astype(jnp.bfloat16).astype(jnp.float32)
    delta = jnp.sum(
        (grad_attn.astype(jnp.float32) * attn).T, axis=0, keepdims=True
    )
    dprob = dot(values, grad_attn, NT)
    dscore = (prob * (dprob - delta)).astype(jnp.bfloat16)

    dq_ref[...] = (dot(dscore, keys, TN) * SCALE).astype(jnp.bfloat16)
    for side, part, cross_ref in (
        (0, dot(dscore, queries, NN) * SCALE, cross_dk_ref),
        (1, dot(prob_bf, grad_attn, NN), cross_dv_ref),
    ):
        to_prev_ref[side] = part[:BLK].astype(jnp.bfloat16)
        center_ref[side] = part[BLK : 2 * BLK]
        to_next_ref[side] = part[2 * BLK : WIN].astype(jnp.bfloat16)
        cross_ref[...] = jnp.where(high, part[2 * BLK : WIN], part[:BLK]).astype(jnp.bfloat16)
        dsum_ref[:, side] = (
            part[WIN:].astype(jnp.bfloat16).reshape(dsum_ref.shape[0], 2 * SUMM, HD)
        )
    conv_ref[...] = jnp.concatenate(
        [jnp.sum(attn * shifted[j], axis=0, keepdims=True) for j in range(KW)]
        + [jnp.zeros((16 - KW, HD), jnp.float32)],
        axis=0,
    )


def attend(frames, links, queries, keys, values, grad_out, halo_k, halo_v, summary, taps):
    width = queries.shape[1]
    smem = pl.BlockSpec(memory_space=pltpu.SMEM)
    own = pl.BlockSpec((BLK, HD), lambda h: (0, h))
    pair = pl.BlockSpec((2, BLK, HD), lambda h: (0, 0, h))
    many = pl.BlockSpec((16, 2, 2 * SUMM, HD), lambda h: (0, 0, 0, h))
    rim = pl.BlockSpec((8, HD), lambda h: (BLK // 8, h))
    return pl.pallas_call(
        attend_kernel,
        grid=(width // HD,),
        out_shape=(
            jax.ShapeDtypeStruct((BLK, width), jnp.bfloat16),
            jax.ShapeDtypeStruct((2, BLK, width), jnp.float32),
            jax.ShapeDtypeStruct((2, BLK, width), jnp.bfloat16),
            jax.ShapeDtypeStruct((2, BLK, width), jnp.bfloat16),
            jax.ShapeDtypeStruct((BLK, width), jnp.bfloat16),
            jax.ShapeDtypeStruct((BLK, width), jnp.bfloat16),
            jax.ShapeDtypeStruct((16, 2, 2 * SUMM, width), jnp.bfloat16),
            jax.ShapeDtypeStruct((16, width), jnp.float32),
        ),
        in_specs=[smem, smem]
        + [own] * 10
        + [rim] * 3
        + [many, pl.BlockSpec((KW, HD), lambda h: (0, h))],
        out_specs=(
            own,
            pair,
            pair,
            pair,
            own,
            own,
            many,
            pl.BlockSpec((16, HD), lambda h: (0, h)),
        ),
        scratch_shapes=[pltpu.VMEM((ROWS, HD), jnp.float32)],
        compiler_params=pltpu.CompilerParams(vmem_limit_bytes=VMEM),
        cost_estimate=pl.CostEstimate(
            flops=6 * 2 * ROWS * BLK * width,
            bytes_accessed=8 * 2**20,
            transcendentals=ROWS * BLK * (width // HD),
        ),
        name="attend",
    )(
        frames, links, queries, keys, values, grad_out, *halo_k, *halo_v, *halo_k, summary, taps
    )


def spread(block, axes, count):
    return lax.all_to_all(
        jnp.broadcast_to(block[None], (count,) + block.shape), axes, 0, 0, tiled=True
    )


def fenced(there, step, *operands):
    shapes = jax.eval_shape(step, *operands)
    return lax.cond(
        there,
        step,
        lambda *_: jax.tree.map(lambda leaf: jnp.zeros(leaf.shape, leaf.dtype), shapes),
        *operands,
    )


def routes():
    rows, width = 8, 4
    up, down, diagonal, outward, inward = [], [], [], [], []
    for row in range(rows):
        at = [row * width + x for x in range(width)]
        up += [(at[x], at[x + 1]) for x in range(width - 1)]
        down += [(at[x + 1], at[x]) for x in range(width - 1)]
        inward += [(at[3], at[2]), (at[0], at[1])]
        outward += [(at[2], at[3]), (at[1], at[0])]
        if row + 1 < rows:
            for ours, theirs in ((at[3], at[3] + 1), (at[2], at[3] + 2)):
                diagonal += [(ours, theirs), (theirs, ours)]
    return up, down, diagonal, outward, inward


def per_device(query_rows, key_rows, value_rows, grad_out, conv_weight, frames, window_links):
    queries, keys, values, grad = query_rows[0], key_rows[0], value_rows[0], grad_out[0]
    up, down, diagonal, outward, inward = routes()
    swap = [(0, 1), (1, 0)]
    x = lax.axis_index("x")
    edge = (x == 0) | (x == 3)
    links = window_links[0, 0]
    there = frames[0] > 0

    up_v = lax.ppermute(values, TM, up)
    down_v = lax.ppermute(values, TM, down)
    packed, own_summary = pack(frames, keys, values, grad)
    other_summary = lax.ppermute(own_summary, "zh", swap)
    up_k = lax.ppermute(packed, TM, up)
    down_k = lax.ppermute(packed, TM, down)
    relay = jnp.pad(jnp.where(x == 1, up_v, down_v), ((0, 8), (0, 0)))
    crossing = jnp.where(edge, packed, relay)
    crossing, other_summary = lax.optimization_barrier((crossing, other_summary))
    cross_k = lax.ppermute(crossing, TM, diagonal)
    summary = fenced(
        there,
        lambda own, other: spread(jnp.concatenate([own, other], axis=1), PLANE, 16),
        own_summary,
        other_summary,
    )
    cross_k, summary = lax.optimization_barrier((cross_k, summary))
    cross_v = lax.ppermute(cross_k[:BLK], TM, outward)

    dq, center, to_prev, to_next, cross_dk, cross_dv, dsum, conv = attend(
        frames,
        links,
        queries,
        keys,
        values,
        grad,
        (up_k, down_k, cross_k),
        (up_v, down_v, cross_v),
        summary,
        conv_weight,
    )

    from_prev = lax.ppermute(to_next, TM, up)
    from_next = lax.ppermute(to_prev, TM, down)
    relay = lax.ppermute(cross_dv, TM, inward)

    def to_owners(dsum, conv):
        dsum = lax.all_to_all(dsum, PLANE, 0, 0, tiled=True)
        tap = lax.all_to_all(conv[:, None], PLANE, 0, 0, tiled=True)
        return jnp.sum(dsum.astype(jnp.float32), axis=0), jnp.sum(tap, axis=0)

    dsum, tap = fenced(there, to_owners, dsum, conv)
    relay, dsum, tap = lax.optimization_barrier((relay, dsum, tap))
    cross_dk = lax.ppermute(jnp.where(edge, cross_dk, relay), TM, diagonal)

    def along_line(dsum, tap):
        other = lax.ppermute(dsum[:, SUMM:].astype(jnp.bfloat16), "zh", swap)
        tap = jnp.sum(spread(tap, LINE, 32), axis=0)
        return dsum[:, :SUMM] + other.astype(jnp.float32), tap

    dsum, tap = fenced(there, along_line, dsum, tap)
    cross_dk, dsum, tap = lax.optimization_barrier((cross_dk, dsum, tap))
    cross_dv = lax.ppermute(cross_dk, TM, outward)
    taps = spread(tap, PLANE, 16)[:KW, 0]

    row = lax.axis_index(TM) * BLK + jnp.arange(BLK, dtype=jnp.int32)
    valid = (row < frames[0]).astype(jnp.float32).reshape(SUMM, POOL)
    share = valid / jnp.maximum(jnp.sum(valid, axis=1, keepdims=True), 1.0)

    def total(side, cross):
        spread_sum = (dsum[side][:, None] * share[:, :, None]).reshape(center[side].shape)
        near = from_prev[side].astype(jnp.float32) + from_next[side].astype(jnp.float32)
        far = jnp.where(edge, cross.astype(jnp.float32), 0.0)
        return (center[side] + near + far + spread_sum).astype(jnp.bfloat16)[None]

    return dq[None], total(0, cross_dk), total(1, cross_dv), taps


def solution(mesh):
    names, sizes = zip(*AXES, strict=True)
    fine = Mesh(mesh.devices.reshape(sizes), names)
    rows = P(DP, TM, None)
    return jax.shard_map(
        per_device,
        mesh=fine,
        in_specs=(rows, rows, rows, rows, P(), P(DP), rows),
        out_specs=(rows, rows, rows, P()),
        check_vma=False,
    )
```

time: 234 us -> 185 us (0.79)
  the two profiles are of different devices: /device:TPU:32 before, /device:TPU:2 now
where the time goes in v2:
time: 185 us; the launch traced here: 184 us
  starting transfers between devices  98.1 us (53%)
  blocking collectives  33.9 us (18%)
  waiting for transfers between devices  29.9 us (16%)
  Pallas kernels  15.2 us (8%)
  local copies, waits for them, and re-layouts  3.04 us (2%)
  other arithmetic  1.9 us (1%)
    all_to_all x1, blocking collectives, spread(): lax.all_to_all(jnp.broadcast_to(block[None], (count,) + block.shape), axe...  22.2 us
    all_to_all x2, starting transfers between devices, spread(): lax.all_to_all(jnp.broadcast_to(block[None], (count,) + block.shape), axe...  18.9 us
    ppermute x1, starting transfers between devices, per_device(): from_prev = lax.ppermute(to_next, TM, up)  14.2 us
    ppermute x1, starting transfers between devices, per_device(): up_k = lax.ppermute(packed, TM, up)  12.5 us
    ppermute x1, starting transfers between devices, along_line(): other = lax.ppermute(dsum[:, SUMM:].astype(jnp.bfloat16), 'zh', swap)  12.4 us
    all_to_all x1, waiting for transfers between devices, to_owners(): dsum = lax.all_to_all(dsum, PLANE, 0, 0, tiled=True)  12.2 us
    pallas_call x1, Pallas kernels, attend(): pl.pallas_call(attend_kernel, grid=(width // HD,), out_shape=(jax.ShapeDt...  12.1 us
    ppermute x1, starting transfers between devices, per_device(): other_summary = lax.ppermute(own_summary, 'zh', swap)  11.9 us
  transfers between devices with their start and end apart: 16, of which 5 were waited for; matrix products, arithmetic and copies ran while one was open for 2% of the time, Pallas kernels for 2%

profile of v2, /device:TPU:2, one launch (start us, length us, event | category | flops | bytes accessed | tf_op | source)
XLA Modules:
  0.0 183.7 jit_solution(7915561124787462709)
XLA Ops:
  0.6 7.8 %collective-permute-start.4 = (bf16[128,1024]{1,0:T(8,128)(2,1)}, bf16[128,1024]{1,0:T(8,128)(2,1)S(1)}, u32[]{:S(2)}, u32[]{:S(2)}) collective-permute-start(bf16[128,1024]{1,0:T(8,128)(2,1)} %bitcast.45), channel_id=1, source_target_pairs={{1,0},{2,1},{3,2},{5,4},{6,5},{7,6},{9,8},{10,9},{11,10},{13,12},{... | collective-permute-start | bytes 786440 | tf_op jit(solution)/shard_map/ppermute | solution.py:281
  8.5 1.9 %collective-permute-start.3 = (bf16[128,1024]{1,0:T(8,128)(2,1)}, bf16[128,1024]{1,0:T(8,128)(2,1)S(1)}, u32[]{:S(2)}, u32[]{:S(2)}) collective-permute-start(bf16[128,1024]{1,0:T(8,128)(2,1)} %bitcast.46), channel_id=1, source_target_pairs={{0,1},{1,2},{2,3},{4,5},{5,6},{6,7},{8,9},{9,10},{10,11},{12,13},{... | collective-permute-start | bytes 786440 | tf_op jit(solution)/shard_map/ppermute | solution.py:280
  11.0 3.1 %pack.1 = (bf16[136,1024]{1,0:T(8,128)(2,1)}, bf16[2,8,1024]{2,1,0:T(8,128)(2,1)S(1)}) custom-call(s32[1]{0:T(128)} %copy.26.frames, bf16[128,1024]{1,0:T(8,128)(2,1)} %bitcast.43, bf16[128,1024]{1,0:T(8,128)(2,1)} %bitcast.47, bf16[128,1024]{1,0:T(8,128)(2,1)} %bitcast.49), custom_call_target="tpu_custom_call" | custom-call | tf_op jit(solution)/shard_map/pack/pallas_call | solution.py:56
  14.2 11.9 %collective-permute-start.5 = (bf16[2,8,1024]{2,1,0:T(8,128)(2,1)S(1)}, bf16[2,8,1024]{2,1,0:T(8,128)(2,1)S(1)}, u32[]{:S(2)}, u32[]{:S(2)}) collective-permute-start(bf16[2,8,1024]{2,1,0:T(8,128)(2,1)S(1)} %get-tuple-element.50), channel_id=1, source_target_pairs={{0,4},{4,0},{1,5},{5,1},{2,6},{6,2},{3,7},{7,3},{8,12},{12,8},{9,1... | collective-permute-start | bytes 98312 | tf_op jit(solution)/shard_map/ppermute | solution.py:283
  26.3 2.5 %collective-permute-done.5 = bf16[2,8,1024]{2,1,0:T(8,128)(2,1)S(1)} collective-permute-done((bf16[2,8,1024]{2,1,0:T(8,128)(2,1)S(1)}, bf16[2,8,1024]{2,1,0:T(8,128)(2,1)S(1)}, u32[]{:S(2)}, u32[]{:S(2)}) %collective-permute-start.5) | collective-permute-done | bytes 32800 | tf_op jit(solution)/shard_map/ppermute | solution.py:283
  28.8 0.7 collective-permute-start.6
  29.5 3.9 %collective-permute-start.2 = (bf16[136,1024]{1,0:T(8,128)(2,1)S(1)}, bf16[136,1024]{1,0:T(8,128)(2,1)S(1)}, u32[]{:S(2)}, u32[]{:S(2)}) collective-permute-start(bf16[136,1024]{1,0:T(8,128)(2,1)S(1)} %copy-done.6), channel_id=1, source_target_pairs={{1,0},{2,1},{3,2},{5,4},{6,5},{7,6},{9,8},{10,9},{11,10},{13,12},{... | collective-permute-start | bytes 835592 | tf_op jit(solution)/shard_map/ppermute | solution.py:285
  33.4 12.5 %collective-permute-start.1 = (bf16[136,1024]{1,0:T(8,128)(2,1)S(1)}, bf16[136,1024]{1,0:T(8,128)(2,1)S(1)}, u32[]{:S(2)}, u32[]{:S(2)}) collective-permute-start(bf16[136,1024]{1,0:T(8,128)(2,1)S(1)} %copy-done.6), channel_id=1, source_target_pairs={{0,1},{1,2},{2,3},{4,5},{5,6},{6,7},{8,9},{9,10},{10,11},{12,13},{... | collective-permute-start | bytes 835592 | tf_op jit(solution)/shard_map/ppermute | solution.py:284
  46.0 22.3 %conditional.3 = (bf16[16,2,16,1024]{3,2,1,0:T(8,128)(2,1)S(1)}) conditional(s32[]{:T(128)} %convert_element_type.52, () %tuple.35, (bf16[2,8,1024]{2,1,0:T(8,128)(2,1)S(1)}, bf16[2,8,1024]{2,1,0:T(8,128)(2,1)S(1)}) %tuple.36), branch_computations={%region_0.1_spmd, %region_1.2_spmd} | conditional | flops 131072 | bytes 3342344 | solution.py:248
  46.1 22.2 %all_to_all.21 = bf16[16,2,16,1024]{3,2,1,0:T(8,128)(2,1)S(1)} all-to-all(bf16[16,2,16,1024]{3,2,1,0:T(8,128)(2,1)S(1)} %broadcast_in_dim.21), channel_id=1, replica_groups=mesh['zl'=8,'core'=2,'y'=4,'zh'=2,'x'=4] {'y','x'}, dimensions={0} | all-to-all | bytes 2097152 | tf_op jit(solution)/shard_map/cond/branch_1_fun/all_to_all | solution.py:241
  68.3 3.5 %collective-permute-start.7 = (bf16[128,1024]{1,0:T(8,128)(2,1)S(1)}, bf16[128,1024]{1,0:T(8,128)(2,1)S(1)}, u32[]{:S(2)}, u32[]{:S(2)}) collective-permute-start(bf16[128,1024]{1,0:T(8,128)(2,1)S(1)} %slice.37), channel_id=1, source_target_pairs={{2,3},{1,0},{6,7},{5,4},{10,11},{9,8},{14,15},{13,12},{18,19},{17,... | collective-permute-start | bytes 786440 | tf_op jit(solution)/shard_map/ppermute | solution.py:297
  71.9 3.8 %collective-permute-done.7.cross_v_ref = bf16[128,1024]{1,0:T(8,128)(2,1)S(1)} collective-permute-done((bf16[128,1024]{1,0:T(8,128)(2,1)S(1)}, bf16[128,1024]{1,0:T(8,128)(2,1)S(1)}, u32[]{:S(2)}, u32[]{:S(2)}) %collective-permute-start.7) | collective-permute-done | bytes 262176 | tf_op jit(solution)/shard_map/ppermute | solution.py:297
  75.7 0.7 copy-done.7
  76.4 12.1 %attend.1 = (bf16[128,1024]{1,0:T(8,128)(2,1)}, f32[2,128,1024]{2,1,0:T(8,128)}, bf16[2,128,1024]{2,1,0:T(8,128)(2,1)}, bf16[2,128,1024]{2,1,0:T(8,128)(2,1)}, b...) custom-call(s32[1]{0:T(128)} %copy.26.frames, ...), custom_call_target="tpu_custom_call" | custom-call | flops 1006632960 | bytes 8388608 | tf_op jit(solution)/shard_map/attend/pallas_call | solution.py:200
  88.5 1.3 collective-permute-start.10
  89.8 29.1 %conditional.4 = (f32[2,16,1024]{2,1,0:T(8,128)S(1)}, f32[1,1024]{1,0:T(1,128)S(1)}) conditional(s32[]{:T(128)} %convert_element_type.52, () %tuple.38, (bf16[16,2,16,1024]{3,2,1,0:T(8,128)(2,1)}, f32[16,1024]{1,0:T(8,128)S(1)}) %tuple.39), branch_computations={%region_2.3_spmd, %region_3.6_spmd} | conditional | flops 1031168 | bytes 4657204 | solution.py:248
  89.9 11.7 %all_to_all.22 = f32[16,1,1024]{2,1,0:T(1,128)S(1)} all-to-all(f32[16,1,1024]{2,1,0:T(1,128)S(1)} %broadcast_in_dim.22), channel_id=1, replica_groups=mesh['zl'=8,'core'=2,'y'=4,'zh'=2,'x'=4] {'y','x'}, dimensions={0} | all-to-all | bytes 131072 | tf_op jit(solution)/shard_map/cond/branch_1_fun/all_to_all | solution.py:318
  101.6 4.9 %all-to-all-start.1 = ((bf16[16,2,16,1024]{3,2,1,0:T(8,128)(2,1)}), bf16[16,2,16,1024]{3,2,1,0:T(8,128)(2,1)S(1)}, u32[]{:S(2)}, u32[]{:S(2)}) async-start(bf16[16,2,16,1024]{3,2,1,0:T(8,128)(2,1)} %get-tuple-element.17), calls=%async_computation.1 | async-start | bytes 2097152 | tf_op jit(solution)/shard_map/cond/branch_1_fun/all_to_all | solution.py:317
  106.5 12.2 %all-to-all-done.1 = bf16[16,2,16,1024]{3,2,1,0:T(8,128)(2,1)S(1)} async-done(((bf16[16,2,16,1024]{3,2,1,0:T(8,128)(2,1)}), bf16[16,2,16,1024]{3,2,1,0:T(8,128)(2,1)S(1)}, u32[]{:S(2)}, u32[]{:S(2)}) %all-to-all-start.1) | async-done | bytes 1048608 | tf_op jit(solution)/shard_map/cond/branch_1_fun/all_to_all | solution.py:317
  119.0 0.8 collective-permute-start.11
  119.9 14.2 %collective-permute-start.8 = (bf16[2,128,1024]{2,1,0:T(8,128)(2,1)}, bf16[2,128,1024]{2,1,0:T(8,128)(2,1)S(1)}, u32[]{:S(2)}, u32[]{:S(2)}) collective-permute-start(bf16[2,128,1024]{2,1,0:T(8,128)(2,1)} %get-tuple-element.57), channel_id=1, source_target_pairs={{0,1},{1,2},{2,3},{4,5},{5,6},{6,7},{8,9},{9,10},{10,11},{12,13},{... | collective-permute-start | bytes 1572872 | tf_op jit(solution)/shard_map/ppermute | solution.py:312
  134.1 1.9 %collective-permute-start.9 = (bf16[2,128,1024]{2,1,0:T(8,128)(2,1)S(1)}, bf16[2,128,1024]{2,1,0:T(8,128)(2,1)S(1)}, u32[]{:S(2)}, u32[]{:S(2)}) collective-permute-start(bf16[2,128,1024]{2,1,0:T(8,128)(2,1)S(1)} %copy-done.9), channel_id=1, source_target_pairs={{1,0},{2,1},{3,2},{5,4},{6,5},{7,6},{9,8},{10,9},{11,10},{13,12},{... | collective-permute-start | bytes 1572872 | tf_op jit(solution)/shard_map/ppermute | solution.py:313
  136.1 27.4 %conditional.5 = (f32[2,8,1024]{2,1,0:T(8,128)S(1)}, f32[1,1024]{1,0:T(1,128)S(1)}) conditional(s32[]{:T(128)} %convert_element_type.52, () %tuple.41, (f32[2,16,1024]{2,1,0:T(8,128)S(1)}, f32[1,1024]{1,0:T(1,128)S(1)}) %conditional.4), branch_computations={%region_6.7_spmd, %region_7.9_spmd} | conditional | flops 64512 | bytes 1024092 | solution.py:248
  136.1 0.7 broadcast_in_dim.24
  136.8 9.0 %all-to-all-start.3 = ((f32[32,1,1024]{2,1,0:T(1,128)}), f32[32,1,1024]{2,1,0:T(1,128)S(1)}, u32[]{:S(2)}, u32[]{:S(2)}) async-start(f32[32,1,1024]{2,1,0:T(1,128)} %broadcast_in_dim.24), calls=%async_computation.3 | async-start | bytes 262144 | tf_op jit(solution)/shard_map/cond/branch_1_fun/all_to_all | solution.py:241
  145.9 12.4 %collective-permute-start = (bf16[2,8,1024]{2,1,0:T(8,128)(2,1)S(1)}, bf16[2,8,1024]{2,1,0:T(8,128)(2,1)S(1)}, u32[]{:S(2)}, u32[]{:S(2)}) collective-permute-start(bf16[2,8,1024]{2,1,0:T(8,128)(2,1)S(1)} %slice.63), channel_id=1, source_target_pairs={{0,4},{4,0},{1,5},{5,1},{2,6},{6,2},{3,7},{7,3},{8,12},{12,8},{9,1... | collective-permute-start | bytes 98312 | tf_op jit(solution)/shard_map/cond/branch_1_fun/ppermute | solution.py:326
  158.3 5.1 %collective-permute-done = bf16[2,8,1024]{2,1,0:T(8,128)(2,1)S(1)} collective-permute-done((bf16[2,8,1024]{2,1,0:T(8,128)(2,1)S(1)}, bf16[2,8,1024]{2,1,0:T(8,128)(2,1)S(1)}, u32[]{:S(2)}, u32[]{:S(2)}) %collective-permute-start) | collective-permute-done | bytes 32800 | tf_op jit(solution)/shard_map/cond/branch_1_fun/ppermute | solution.py:326
  163.5 1.3 collective-permute-start.12
  165.0 0.7 broadcast_in_dim.47
  165.6 9.9 %all-to-all-start.4 = ((f32[16,1,1024]{2,1,0:T(1,128)}), f32[16,1,1024]{2,1,0:T(1,128)S(1)}, u32[]{:S(2)}, u32[]{:S(2)}) async-start(f32[16,1,1024]{2,1,0:T(1,128)} %broadcast_in_dim.47), calls=%async_computation.4 | async-start | bytes 131072 | tf_op jit(solution)/shard_map/all_to_all | solution.py:241
  175.5 6.3 %all-to-all-done.4 = f32[16,1,1024]{2,1,0:T(1,128)S(1)} async-done(((f32[16,1,1024]{2,1,0:T(1,128)}), f32[16,1,1024]{2,1,0:T(1,128)S(1)}, u32[]{:S(2)}, u32[]{:S(2)}) %all-to-all-start.4) | async-done | bytes 65568 | tf_op jit(solution)/shard_map/all_to_all | solution.py:241
  182.5 1.2 fusion.1
  (49 shorter events, 1.7 us)
Async XLA Ops:
  0.6 25.5 %collective-permute-start.4 = (bf16[128,1024]{1,0:T(8,128)(2,1)}, bf16[128,1024]{1,0:T(8,128)(2,1)S(1)}, u32[]{:S(2)}, u32[]{:S(2)}) collective-permute-start(bf16[128,1024]{1,0:T(8,128)(2,1)} %bitcast.45), channel_id=1, source_target_pairs={{1,0},{2,1},{3,2},{5,4},{6,5},{7,6},{9,8},{10,9},{11,10},{13,12},{... | collective-permute-start | bytes 786440 | tf_op jit(solution)/shard_map/ppermute | solution.py:281
  8.5 17.7 %collective-permute-start.3 = (bf16[128,1024]{1,0:T(8,128)(2,1)}, bf16[128,1024]{1,0:T(8,128)(2,1)S(1)}, u32[]{:S(2)}, u32[]{:S(2)}) collective-permute-start(bf16[128,1024]{1,0:T(8,128)(2,1)} %bitcast.46), channel_id=1, source_target_pairs={{0,1},{1,2},{2,3},{4,5},{5,6},{6,7},{8,9},{9,10},{10,11},{12,13},{... | collective-permute-start | bytes 786440 | tf_op jit(solution)/shard_map/ppermute | solution.py:280
  14.2 15.3 %copy-start.6 = (bf16[136,1024]{1,0:T(8,128)(2,1)S(1)}, bf16[136,1024]{1,0:T(8,128)(2,1)}, u32[]{:S(2)}) copy-start(bf16[136,1024]{1,0:T(8,128)(2,1)} %get-tuple-element.49) | copy-start | bytes 835588
  14.2 14.6 %collective-permute-start.5 = (bf16[2,8,1024]{2,1,0:T(8,128)(2,1)S(1)}, bf16[2,8,1024]{2,1,0:T(8,128)(2,1)S(1)}, u32[]{:S(2)}, u32[]{:S(2)}) collective-permute-start(bf16[2,8,1024]{2,1,0:T(8,128)(2,1)S(1)} %get-tuple-element.50), channel_id=1, source_target_pairs={{0,4},{4,0},{1,5},{5,1},{2,6},{6,2},{3,7},{7,3},{8,12},{12,8},{9,1... | collective-permute-start | bytes 98312 | tf_op jit(solution)/shard_map/ppermute | solution.py:283
  26.2 19.8 %copy-start.4 = (bf16[128,1024]{1,0:T(8,128)(2,1)}, bf16[128,1024]{1,0:T(8,128)(2,1)S(1)}, u32[]{:S(2)}) copy-start(bf16[128,1024]{1,0:T(8,128)(2,1)S(1)} %collective-permute-done.4.down_v_ref) | copy-start | bytes 786436
  26.2 19.8 %copy-start.5 = (bf16[128,1024]{1,0:T(8,128)(2,1)}, bf16[128,1024]{1,0:T(8,128)(2,1)S(1)}, u32[]{:S(2)}) copy-start(bf16[128,1024]{1,0:T(8,128)(2,1)S(1)} %collective-permute-done.3.up_v_ref) | copy-start | bytes 786436
  28.8 39.5 %collective-permute-start.6 = (bf16[136,1024]{1,0:T(8,128)(2,1)S(1)}, bf16[136,1024]{1,0:T(8,128)(2,1)S(1)}, u32[]{:S(2)}, u32[]{:S(2)}) collective-permute-start(bf16[136,1024]{1,0:T(8,128)(2,1)S(1)} %pad_select_fusion), channel_id=1, source_target_pairs={{3,4},{4,3},{2,5},{5,2},{7,8},{8,7},{6,9},{9,6},{11,12},{12,11},{1... | collective-permute-start | bytes 835592 | tf_op jit(solution)/shard_map/ppermute | solution.py:289
  29.5 42.4 %collective-permute-start.2 = (bf16[136,1024]{1,0:T(8,128)(2,1)S(1)}, bf16[136,1024]{1,0:T(8,128)(2,1)S(1)}, u32[]{:S(2)}, u32[]{:S(2)}) collective-permute-start(bf16[136,1024]{1,0:T(8,128)(2,1)S(1)} %copy-done.6), channel_id=1, source_target_pairs={{1,0},{2,1},{3,2},{5,4},{6,5},{7,6},{9,8},{10,9},{11,10},{13,12},{... | collective-permute-start | bytes 835592 | tf_op jit(solution)/shard_map/ppermute | solution.py:285
  33.4 38.5 %collective-permute-start.1 = (bf16[136,1024]{1,0:T(8,128)(2,1)S(1)}, bf16[136,1024]{1,0:T(8,128)(2,1)S(1)}, u32[]{:S(2)}, u32[]{:S(2)}) collective-permute-start(bf16[136,1024]{1,0:T(8,128)(2,1)S(1)} %copy-done.6), channel_id=1, source_target_pairs={{0,1},{1,2},{2,3},{4,5},{5,6},{6,7},{8,9},{9,10},{10,11},{12,13},{... | collective-permute-start | bytes 835592 | tf_op jit(solution)/shard_map/ppermute | solution.py:284
  68.3 7.4 %copy-start = (bf16[136,1024]{1,0:T(8,128)(2,1)}, bf16[136,1024]{1,0:T(8,128)(2,1)S(1)}, u32[]{:S(2)}) copy-start(bf16[136,1024]{1,0:T(8,128)(2,1)S(1)} %collective-permute-done.6.cross_k_ref.cross_go_ref) | copy-start | bytes 835588
  68.3 7.4 %collective-permute-start.7 = (bf16[128,1024]{1,0:T(8,128)(2,1)S(1)}, bf16[128,1024]{1,0:T(8,128)(2,1)S(1)}, u32[]{:S(2)}, u32[]{:S(2)}) collective-permute-start(bf16[128,1024]{1,0:T(8,128)(2,1)S(1)} %slice.37), channel_id=1, source_target_pairs={{2,3},{1,0},{6,7},{5,4},{10,11},{9,8},{14,15},{13,12},{18,19},{17,... | collective-permute-start | bytes 786440 | tf_op jit(solution)/shard_map/ppermute | solution.py:297
  71.9 3.9 %copy-start.1 = (bf16[136,1024]{1,0:T(8,128)(2,1)}, bf16[136,1024]{1,0:T(8,128)(2,1)S(1)}, u32[]{:S(2)}) copy-start(bf16[136,1024]{1,0:T(8,128)(2,1)S(1)} %collective-permute-done.2.down_k_ref.down_go_ref) | copy-start | bytes 835588
  71.9 3.8 %copy-start.2 = (bf16[136,1024]{1,0:T(8,128)(2,1)}, bf16[136,1024]{1,0:T(8,128)(2,1)S(1)}, u32[]{:S(2)}) copy-start(bf16[136,1024]{1,0:T(8,128)(2,1)S(1)} %collective-permute-done.1.up_k_ref.up_go_ref) | copy-start | bytes 835588
  75.7 0.7 copy-start.7
  88.5 30.4 %collective-permute-start.10 = (bf16[128,1024]{1,0:T(8,128)(2,1)}, bf16[128,1024]{1,0:T(8,128)(2,1)S(1)}, u32[]{:S(2)}, u32[]{:S(2)}) collective-permute-start(bf16[128,1024]{1,0:T(8,128)(2,1)} %get-tuple-element.60), channel_id=1, source_target_pairs={{3,2},{0,1},{7,6},{4,5},{11,10},{8,9},{15,14},{12,13},{19,18},{16,... | collective-permute-start | bytes 786440 | tf_op jit(solution)/shard_map/ppermute | solution.py:314
  89.8 29.1 %copy-start.8 = (bf16[128,1024]{1,0:T(8,128)(2,1)S(1)}, bf16[128,1024]{1,0:T(8,128)(2,1)}, u32[]{:S(2)}) copy-start(bf16[128,1024]{1,0:T(8,128)(2,1)} %get-tuple-element.59) | copy-start | bytes 786436
  89.8 44.3 %copy-start.9 = (bf16[2,128,1024]{2,1,0:T(8,128)(2,1)S(1)}, bf16[2,128,1024]{2,1,0:T(8,128)(2,1)}, u32[]{:S(2)}) copy-start(bf16[2,128,1024]{2,1,0:T(8,128)(2,1)} %get-tuple-element.58) | copy-start | bytes 1572868
  101.6 17.1 %all-to-all-start.1 = ((bf16[16,2,16,1024]{3,2,1,0:T(8,128)(2,1)}), bf16[16,2,16,1024]{3,2,1,0:T(8,128)(2,1)S(1)}, u32[]{:S(2)}, u32[]{:S(2)}) async-start(bf16[16,2,16,1024]{3,2,1,0:T(8,128)(2,1)} %get-tuple-element.17), calls=%async_computation.1 | async-start | bytes 2097152 | tf_op jit(solution)/shard_map/cond/branch_1_fun/all_to_all | solution.py:317
  118.9 63.6 %copy-start.3 = (f32[2,128,1024]{2,1,0:T(8,128)S(1)}, f32[2,128,1024]{2,1,0:T(8,128)}, u32[]{:S(2)}) copy-start(f32[2,128,1024]{2,1,0:T(8,128)} %get-tuple-element.56) | copy-start | bytes 3145732
  119.0 44.5 %collective-permute-start.11 = (bf16[128,1024]{1,0:T(8,128)(2,1)S(1)}, bf16[128,1024]{1,0:T(8,128)(2,1)S(1)}, u32[]{:S(2)}, u32[]{:S(2)}) collective-permute-start(bf16[128,1024]{1,0:T(8,128)(2,1)S(1)} %broadcast_select_fusion), channel_id=1, source_target_pairs={{3,4},{4,3},{2,5},{5,2},{7,8},{8,7},{6,9},{9,6},{11,12},{12,11},{1... | collective-permute-start | bytes 786440 | tf_op jit(solution)/shard_map/ppermute | solution.py:323
  119.9 62.6 %collective-permute-start.8 = (bf16[2,128,1024]{2,1,0:T(8,128)(2,1)}, bf16[2,128,1024]{2,1,0:T(8,128)(2,1)S(1)}, u32[]{:S(2)}, u32[]{:S(2)}) collective-permute-start(bf16[2,128,1024]{2,1,0:T(8,128)(2,1)} %get-tuple-element.57), channel_id=1, source_target_pairs={{0,1},{1,2},{2,3},{4,5},{5,6},{6,7},{8,9},{9,10},{10,11},{12,13},{... | collective-permute-start | bytes 1572872 | tf_op jit(solution)/shard_map/ppermute | solution.py:312
  134.1 48.4 %collective-permute-start.9 = (bf16[2,128,1024]{2,1,0:T(8,128)(2,1)S(1)}, bf16[2,128,1024]{2,1,0:T(8,128)(2,1)S(1)}, u32[]{:S(2)}, u32[]{:S(2)}) collective-permute-start(bf16[2,128,1024]{2,1,0:T(8,128)(2,1)S(1)} %copy-done.9), channel_id=1, source_target_pairs={{1,0},{2,1},{3,2},{5,4},{6,5},{7,6},{9,8},{10,9},{11,10},{13,12},{... | collective-permute-start | bytes 1572872 | tf_op jit(solution)/shard_map/ppermute | solution.py:313
  136.8 26.6 %all-to-all-start.3 = ((f32[32,1,1024]{2,1,0:T(1,128)}), f32[32,1,1024]{2,1,0:T(1,128)S(1)}, u32[]{:S(2)}, u32[]{:S(2)}) async-start(f32[32,1,1024]{2,1,0:T(1,128)} %broadcast_in_dim.24), calls=%async_computation.3 | async-start | bytes 262144 | tf_op jit(solution)/shard_map/cond/branch_1_fun/all_to_all | solution.py:241
  145.9 17.5 %collective-permute-start = (bf16[2,8,1024]{2,1,0:T(8,128)(2,1)S(1)}, bf16[2,8,1024]{2,1,0:T(8,128)(2,1)S(1)}, u32[]{:S(2)}, u32[]{:S(2)}) collective-permute-start(bf16[2,8,1024]{2,1,0:T(8,128)(2,1)S(1)} %slice.63), channel_id=1, source_target_pairs={{0,4},{4,0},{1,5},{5,1},{2,6},{6,2},{3,7},{7,3},{8,12},{12,8},{9,1... | collective-permute-start | bytes 98312 | tf_op jit(solution)/shard_map/cond/branch_1_fun/ppermute | solution.py:326
  163.5 19.0 %collective-permute-start.12 = (bf16[128,1024]{1,0:T(8,128)(2,1)S(1)}, bf16[128,1024]{1,0:T(8,128)(2,1)S(1)}, u32[]{:S(2)}, u32[]{:S(2)}) collective-permute-start(bf16[128,1024]{1,0:T(8,128)(2,1)S(1)} %collective-permute-done.11), channel_id=1, source_target_pairs={{2,3},{1,0},{6,7},{5,4},{10,11},{9,8},{14,15},{13,12},{18,19},{17,... | collective-permute-start | bytes 786440 | tf_op jit(solution)/shard_map/ppermute | solution.py:332
  165.6 16.2 %all-to-all-start.4 = ((f32[16,1,1024]{2,1,0:T(1,128)}), f32[16,1,1024]{2,1,0:T(1,128)S(1)}, u32[]{:S(2)}, u32[]{:S(2)}) async-start(f32[16,1,1024]{2,1,0:T(1,128)} %broadcast_in_dim.47), calls=%async_computation.4 | async-start | bytes 131072 | tf_op jit(solution)/shard_map/all_to_all | solution.py:241

commit v3 on v2

--- a/solution.py
+++ b/solution.py
@@ -8,6 +8,7 @@
 
 H = 8
 HD = 128
+HEADS = 4
 BLK = 128
 POOL = 16
 SUMM = BLK // POOL
@@ -106,7 +107,6 @@
     cross_dk_ref,
     cross_dv_ref,
     dsum_ref,
-    conv_ref,
     bias_ref,
 ):
     device, z_half = place()
@@ -127,79 +127,89 @@
 
     x = lax.axis_index("x")
     low, high = x == 0, x == 3
-    summary = summary_ref[...]
-
-    def window(up_ref, own_ref, down_ref, cross_ref):
-        cross = cross_ref[...]
-        return [
-            jnp.where(low, cross, up_ref[...]),
-            own_ref[...],
-            jnp.where(high, cross, down_ref[...]),
-        ]
-
-    keys = jnp.concatenate(
-        window(up_k_ref, k_ref, down_k_ref, cross_k_ref) + [summary[:, 0].reshape(-1, HD)],
-        axis=0,
-    )
-    values = jnp.concatenate(
-        window(up_v_ref, v_ref, down_v_ref, cross_v_ref) + [summary[:, 1].reshape(-1, HD)],
-        axis=0,
-    )
-    queries = q_ref[...]
-
-    row = first + lax.broadcasted_iota(jnp.int32, (BLK, 1), 0)
-    grad = jnp.where(row < frame_count, go_ref[...].astype(jnp.float32), 0.0)
-    cross_go = cross_go_ref[...].astype(jnp.float32)
-    before = jnp.where(low, cross_go, up_go_ref[...].astype(jnp.float32))
-    after = jnp.where(high, cross_go, down_go_ref[...].astype(jnp.float32))
-    reach = jnp.concatenate([before[:HALF], grad, after[HALF:]], axis=0)
-    shifted = [reach[2 * HALF - j : 2 * HALF - j + BLK] for j in range(KW)]
-    total = grad
-    for j in range(KW):
-        total = total + w_ref[j : j + 1, :] * shifted[j]
-    grad_attn = total.astype(jnp.bfloat16)
-
-    scores = dot(keys, queries, NT) * SCALE + bias_ref[...]
-    top = jnp.max(scores, axis=0, keepdims=True)
-    weight = jnp.exp(scores - top)
-    prob = weight * (1.0 / jnp.sum(weight, axis=0, keepdims=True))
-    prob_bf = prob.astype(jnp.bfloat16)
-    attn = dot(prob_bf, values, TN).astype(jnp.bfloat16).astype(jnp.float32)
-    delta = jnp.sum(
-        (grad_attn.astype(jnp.float32) * attn).T, axis=0, keepdims=True
-    )
-    dprob = dot(values, grad_attn, NT)
-    dscore = (prob * (dprob - delta)).astype(jnp.bfloat16)
-
-    dq_ref[...] = (dot(dscore, keys, TN) * SCALE).astype(jnp.bfloat16)
-    for side, part, cross_ref in (
-        (0, dot(dscore, queries, NN) * SCALE, cross_dk_ref),
-        (1, dot(prob_bf, grad_attn, NN), cross_dv_ref),
-    ):
-        to_prev_ref[side] = part[:BLK].astype(jnp.bfloat16)
-        center_ref[side] = part[BLK : 2 * BLK]
-        to_next_ref[side] = part[2 * BLK : WIN].astype(jnp.bfloat16)
-        cross_ref[...] = jnp.where(high, part[2 * BLK : WIN], part[:BLK]).astype(jnp.bfloat16)
-        dsum_ref[:, side] = (
-            part[WIN:].astype(jnp.bfloat16).reshape(dsum_ref.shape[0], 2 * SUMM, HD)
+
+    def one_head(c):
+
+        def window(up_ref, own_ref, down_ref, cross_ref):
+            cross = cross_ref[:BLK, c]
+            return [
+                jnp.where(low, cross, up_ref[:BLK, c]),
+                own_ref[:, c],
+                jnp.where(high, cross, down_ref[:, c]),
+            ]
+
+        keys = jnp.concatenate(
+            window(up_k_ref, k_ref, down_k_ref, cross_k_ref) + [summary_ref[:, 0, :, c].reshape(-1, HD)],
+            axis=0,
         )
-    conv_ref[...] = jnp.concatenate(
-        [jnp.sum(attn * shifted[j], axis=0, keepdims=True) for j in range(KW)]
-        + [jnp.zeros((16 - KW, HD), jnp.float32)],
-        axis=0,
-    )
+        values = jnp.concatenate(
+            window(up_v_ref, v_ref, down_v_ref, cross_v_ref) + [summary_ref[:, 1, :, c].reshape(-1, HD)],
+            axis=0,
+        )
+        queries = q_ref[:, c]
+
+        row = first + lax.broadcasted_iota(jnp.int32, (BLK, 1), 0)
+        grad = jnp.where(row < frame_count, go_ref[:, c].astype(jnp.float32), 0.0)
+        cross_go = cross_go_ref[:, c].astype(jnp.float32)
+        before = jnp.where(low, cross_go, up_go_ref[:, c].astype(jnp.float32))
+        after = jnp.where(high, cross_go, down_go_ref[:, c].astype(jnp.float32))
+        reach = jnp.concatenate([before[:HALF], grad, after[HALF:]], axis=0)
+        shifted = [reach[2 * HALF - j : 2 * HALF - j + BLK] for j in range(KW)]
+        total = grad
+        for j in range(KW):
+            total = total + w_ref[j : j + 1, c] * shifted[j]
+        grad_attn = total.astype(jnp.bfloat16)
+
+        scores = dot(keys, queries, NT) * SCALE + bias_ref[...]
+        top = jnp.max(scores, axis=0, keepdims=True)
+        weight = jnp.exp(scores - top)
+        prob = weight * (1.0 / jnp.sum(weight, axis=0, keepdims=True))
+        prob_bf = prob.astype(jnp.bfloat16)
+        attn = dot(prob_bf, values, TN).astype(jnp.bfloat16).astype(jnp.float32)
+        delta = jnp.sum(
+            (grad_attn.astype(jnp.float32) * attn).T, axis=0, keepdims=True
+        )
+        dprob = dot(values, grad_attn, NT)
+        dscore = (prob * (dprob - delta)).astype(jnp.bfloat16)
+
+        dq_ref[:, c] = (dot(dscore, keys, TN) * SCALE).astype(jnp.bfloat16)
+        for side, part, cross_ref in (
+            (0, dot(dscore, queries, NN) * SCALE, cross_dk_ref),
+            (1, dot(prob_bf, grad_attn, NN), cross_dv_ref),
+        ):
+            to_prev_ref[side, :, c] = part[:BLK].astype(jnp.bfloat16)
+            center_ref[side, :, c] = part[BLK : 2 * BLK]
+            to_next_ref[side, :, c] = part[2 * BLK : WIN].astype(jnp.bfloat16)
+            cross_ref[:, c] = jnp.where(high, part[2 * BLK : WIN], part[:BLK]).astype(jnp.bfloat16)
+            dsum_ref[:, side, : 2 * SUMM, c] = (
+                part[WIN:].astype(jnp.bfloat16).reshape(dsum_ref.shape[0], 2 * SUMM, HD)
+            )
+        empty = jnp.zeros((SUMM, HD), jnp.float32)
+        for j in range(16):
+            if j < KW:
+                tap = jnp.sum(attn * shifted[j], axis=0, keepdims=True)
+                big = tap.astype(jnp.bfloat16).astype(jnp.float32)
+                terms = (big + empty, (tap - big) + empty)
+            else:
+                terms = (empty, empty)
+            for side, term in enumerate(terms):
+                dsum_ref[j, side, 2 * SUMM :, c] = term.astype(jnp.bfloat16)
+
+    for head in range(HEADS):
+        one_head(slice(head * HD, (head + 1) * HD))
 
 
 def attend(frames, links, queries, keys, values, grad_out, halo_k, halo_v, summary, taps):
     width = queries.shape[1]
+    step = HEADS * HD
     smem = pl.BlockSpec(memory_space=pltpu.SMEM)
-    own = pl.BlockSpec((BLK, HD), lambda h: (0, h))
-    pair = pl.BlockSpec((2, BLK, HD), lambda h: (0, 0, h))
-    many = pl.BlockSpec((16, 2, 2 * SUMM, HD), lambda h: (0, 0, 0, h))
-    rim = pl.BlockSpec((8, HD), lambda h: (BLK // 8, h))
+    own = pl.BlockSpec((BLK, step), lambda h: (0, h))
+    pair = pl.BlockSpec((2, BLK, step), lambda h: (0, 0, h))
+    many = pl.BlockSpec((16, 2, 2 * SUMM, step), lambda h: (0, 0, 0, h))
+    rim = pl.BlockSpec((8, step), lambda h: (BLK // 8, h))
     return pl.pallas_call(
         attend_kernel,
-        grid=(width // HD,),
+        grid=(width // step,),
         out_shape=(
             jax.ShapeDtypeStruct((BLK, width), jnp.bfloat16),
             jax.ShapeDtypeStruct((2, BLK, width), jnp.float32),
@@ -207,13 +217,12 @@
             jax.ShapeDtypeStruct((2, BLK, width), jnp.bfloat16),
             jax.ShapeDtypeStruct((BLK, width), jnp.bfloat16),
             jax.ShapeDtypeStruct((BLK, width), jnp.bfloat16),
-            jax.ShapeDtypeStruct((16, 2, 2 * SUMM, width), jnp.bfloat16),
-            jax.ShapeDtypeStruct((16, width), jnp.float32),
+            jax.ShapeDtypeStruct((16, 2, 3 * SUMM, width), jnp.bfloat16),
         ),
         in_specs=[smem, smem]
         + [own] * 10
         + [rim] * 3
-        + [many, pl.BlockSpec((KW, HD), lambda h: (0, h))],
+        + [many, pl.BlockSpec((KW, step), lambda h: (0, h))],
         out_specs=(
             own,
             pair,
@@ -221,8 +230,7 @@
             pair,
             own,
             own,
-            many,
-            pl.BlockSpec((16, HD), lambda h: (0, h)),
+            pl.BlockSpec((16, 2, 3 * SUMM, step), lambda h: (0, 0, 0, h)),
         ),
         scratch_shapes=[pltpu.VMEM((ROWS, HD), jnp.float32)],
         compiler_params=pltpu.CompilerParams(vmem_limit_bytes=VMEM),
@@ -296,7 +304,7 @@
     cross_k, summary = lax.optimization_barrier((cross_k, summary))
     cross_v = lax.ppermute(cross_k[:BLK], TM, outward)
 
-    dq, center, to_prev, to_next, cross_dk, cross_dv, dsum, conv = attend(
+    dq, center, to_prev, to_next, cross_dk, cross_dv, dsum = attend(
         frames,
         links,
         queries,
@@ -313,24 +321,18 @@
     from_next = lax.ppermute(to_prev, TM, down)
     relay = lax.ppermute(cross_dv, TM, inward)
 
-    def to_owners(dsum, conv):
-        dsum = lax.all_to_all(dsum, PLANE, 0, 0, tiled=True)
-        tap = lax.all_to_all(conv[:, None], PLANE, 0, 0, tiled=True)
-        return jnp.sum(dsum.astype(jnp.float32), axis=0), jnp.sum(tap, axis=0)
-
-    dsum, tap = fenced(there, to_owners, dsum, conv)
-    relay, dsum, tap = lax.optimization_barrier((relay, dsum, tap))
+    relay, dsum = lax.optimization_barrier((relay, dsum))
+    dsum = lax.all_to_all(dsum, PLANE, 0, 0, tiled=True)
+    dsum = jnp.sum(dsum.astype(jnp.float32), axis=0)
+    tap = dsum[0, 2 * SUMM : 2 * SUMM + 1] + dsum[1, 2 * SUMM : 2 * SUMM + 1]
     cross_dk = lax.ppermute(jnp.where(edge, cross_dk, relay), TM, diagonal)
 
-    def along_line(dsum, tap):
-        other = lax.ppermute(dsum[:, SUMM:].astype(jnp.bfloat16), "zh", swap)
-        tap = jnp.sum(spread(tap, LINE, 32), axis=0)
-        return dsum[:, :SUMM] + other.astype(jnp.float32), tap
-
-    dsum, tap = fenced(there, along_line, dsum, tap)
+    tap = fenced(there, lambda tap: jnp.sum(spread(tap, LINE, 32), axis=0), tap)
     cross_dk, dsum, tap = lax.optimization_barrier((cross_dk, dsum, tap))
     cross_dv = lax.ppermute(cross_dk, TM, outward)
     taps = spread(tap, PLANE, 16)[:KW, 0]
+    other = lax.ppermute(dsum[:, SUMM : 2 * SUMM].astype(jnp.bfloat16), "zh", swap)
+    dsum = dsum[:, :SUMM] + other.astype(jnp.float32)
 
     row = lax.axis_index(TM) * BLK + jnp.arange(BLK, dtype=jnp.int32)
     valid = (row < frames[0]).astype(jnp.float32).reshape(SUMM, POOL)

time: 185 us -> 173 us (0.935)
  the two profiles are of different devices: /device:TPU:2 before, /device:TPU:38 now
where the time goes in v3:
time: 173 us
  starting transfers between devices  77 us (45%)
  blocking collectives  51.2 us (30%)
  waiting for transfers between devices  21.9 us (13%)
  Pallas kernels  13.8 us (8%)
  other arithmetic  4.82 us (3%)
  local copies, waits for them, and re-layouts  2.35 us (1%)
    all_to_all x2, blocking collectives, spread(): lax.all_to_all(jnp.broadcast_to(block[None], (count,) + block.shape), axe...  51.2 us
    ppermute x1, starting transfers between devices, per_device(): other_summary = lax.ppermute(own_summary, 'zh', swap)  14.9 us
    ppermute x1, starting transfers between devices, per_device(): cross_k = lax.ppermute(crossing, TM, diagonal)  14.5 us
    pallas_call x1, Pallas kernels, attend(): pl.pallas_call(attend_kernel, grid=(width // step,), out_shape=(jax.Shape...  10.6 us
    ppermute x1, starting transfers between devices, per_device(): cross_dk = lax.ppermute(jnp.where(edge, cross_dk, relay), TM, diagonal)  9.19 us
    all_to_all x1, starting transfers between devices, per_device(): dsum = lax.all_to_all(dsum, PLANE, 0, 0, tiled=True)  8.18 us
    ppermute x1, waiting for transfers between devices, per_device(): cross_v = lax.ppermute(cross_k[:BLK], TM, outward)  7.33 us
    all_to_all x1, starting transfers between devices, spread(): lax.all_to_all(jnp.broadcast_to(block[None], (count,) + block.shape), axe...  7.12 us
  transfers between devices with their start and end apart: 15, of which 7 were waited for; matrix products, arithmetic and copies ran while one was open for 2% of the time, Pallas kernels for 2%

profile of v3, /device:TPU:38, one launch (start us, length us, event | category | flops | bytes accessed | tf_op | source)
XLA Modules:
  0.0 172.6 jit_solution(16483904694655588026)
XLA Ops:
  0.6 2.8 %collective-permute-start.3 = (bf16[128,1024]{1,0:T(8,128)(2,1)}, bf16[128,1024]{1,0:T(8,128)(2,1)S(1)}, u32[]{:S(2)}, u32[]{:S(2)}) collective-permute-start(bf16[128,1024]{1,0:T(8,128)(2,1)} %bitcast.44), channel_id=1, source_target_pairs={{1,0},{2,1},{3,2},{5,4},{6,5},{7,6},{9,8},{10,9},{11,10},{13,12},{... | collective-permute-start | bytes 786440 | tf_op jit(solution)/shard_map/ppermute | solution.py:289
  3.4 1.3 collective-permute-start.2
  5.3 3.1 %pack.1 = (bf16[136,1024]{1,0:T(8,128)(2,1)}, bf16[2,8,1024]{2,1,0:T(8,128)(2,1)S(1)}) custom-call(s32[1]{0:T(128)} %copy.20.frames, bf16[128,1024]{1,0:T(8,128)(2,1)} %bitcast.42, bf16[128,1024]{1,0:T(8,128)(2,1)} %bitcast.46, bf16[128,1024]{1,0:T(8,128)(2,1)} %bitcast.48), custom_call_target="tpu_custom_call" | custom-call | tf_op jit(solution)/shard_map/pack/pallas_call | solution.py:57
  8.5 14.9 %collective-permute-start.4 = (bf16[2,8,1024]{2,1,0:T(8,128)(2,1)S(1)}, bf16[2,8,1024]{2,1,0:T(8,128)(2,1)S(1)}, u32[]{:S(2)}, u32[]{:S(2)}) collective-permute-start(bf16[2,8,1024]{2,1,0:T(8,128)(2,1)S(1)} %get-tuple-element.42), channel_id=1, source_target_pairs={{0,4},{4,0},{1,5},{5,1},{2,6},{6,2},{3,7},{7,3},{8,12},{12,8},{9,1... | collective-permute-start | bytes 98312 | tf_op jit(solution)/shard_map/ppermute | solution.py:291
  23.5 1.2 pad_select_fusion
  24.7 0.8 collective-permute-done.4
  25.5 14.5 %collective-permute-start.5 = (bf16[136,1024]{1,0:T(8,128)(2,1)S(1)}, bf16[136,1024]{1,0:T(8,128)(2,1)S(1)}, u32[]{:S(2)}, u32[]{:S(2)}) collective-permute-start(bf16[136,1024]{1,0:T(8,128)(2,1)S(1)} %pad_select_fusion), channel_id=1, source_target_pairs={{3,4},{4,3},{2,5},{5,2},{7,8},{8,7},{6,9},{9,6},{11,12},{12,11},{1... | collective-permute-start | bytes 835592 | tf_op jit(solution)/shard_map/ppermute | solution.py:297
  40.0 2.8 %collective-permute-start.1 = (bf16[136,1024]{1,0:T(8,128)(2,1)S(1)}, bf16[136,1024]{1,0:T(8,128)(2,1)S(1)}, u32[]{:S(2)}, u32[]{:S(2)}) collective-permute-start(bf16[136,1024]{1,0:T(8,128)(2,1)S(1)} %copy-done.6), channel_id=1, source_target_pairs={{1,0},{2,1},{3,2},{5,4},{6,5},{7,6},{9,8},{10,9},{11,10},{13,12},{... | collective-permute-start | bytes 835592 | tf_op jit(solution)/shard_map/ppermute | solution.py:293
  42.8 1.3 collective-permute-start
  44.1 24.3 %conditional.2 = (bf16[16,2,16,1024]{3,2,1,0:T(8,128)(2,1)S(1)}) conditional(s32[]{:T(128)} %convert_element_type.51, () %tuple.25, (bf16[2,8,1024]{2,1,0:T(8,128)(2,1)S(1)}, bf16[2,8,1024]{2,1,0:T(8,128)(2,1)S(1)}) %tuple.26), branch_computations={%region_0.1_spmd, %region_1.2_spmd} | conditional | flops 131072 | bytes 3342344 | solution.py:256
  44.3 24.1 %all_to_all.18 = bf16[16,2,16,1024]{3,2,1,0:T(8,128)(2,1)S(1)} all-to-all(bf16[16,2,16,1024]{3,2,1,0:T(8,128)(2,1)S(1)} %broadcast_in_dim.18), channel_id=1, replica_groups=mesh['zl'=8,'core'=2,'y'=4,'zh'=2,'x'=4] {'y','x'}, dimensions={0} | all-to-all | bytes 2097152 | tf_op jit(solution)/shard_map/cond/branch_1_fun/all_to_all | solution.py:249
  68.5 1.3 collective-permute-start.6
  69.8 7.3 %collective-permute-done.6.cross_v_ref = bf16[128,1024]{1,0:T(8,128)(2,1)S(1)} collective-permute-done((bf16[128,1024]{1,0:T(8,128)(2,1)S(1)}, bf16[128,1024]{1,0:T(8,128)(2,1)S(1)}, u32[]{:S(2)}, u32[]{:S(2)}) %collective-permute-start.6) | collective-permute-done | bytes 262176 | tf_op jit(solution)/shard_map/ppermute | solution.py:305
  77.1 0.7 copy-done.7
  77.8 10.6 %attend.1 = (bf16[128,1024]{1,0:T(8,128)(2,1)}, f32[2,128,1024]{2,1,0:T(8,128)}, bf16[2,128,1024]{2,1,0:T(8,128)(2,1)}, bf16[2,128,1024]{2,1,0:T(8,128)(2,1)}, b...) custom-call(s32[1]{0:T(128)} %copy.20.frames, s32[2]{0:T(128)} %bitcast.57, ...), custom_call_target="tpu_custom_call" | custom-call | flops 1006632960 | bytes 8388608 | tf_op jit(solution)/shard_map/attend/pallas_call | solution.py:210
  88.5 1.5 collective-permute-start.9
  90.0 4.2 %collective-permute-done.9 = bf16[128,1024]{1,0:T(8,128)(2,1)S(1)} collective-permute-done((bf16[128,1024]{1,0:T(8,128)(2,1)}, bf16[128,1024]{1,0:T(8,128)(2,1)S(1)}, u32[]{:S(2)}, u32[]{:S(2)}) %collective-permute-start.9) | collective-permute-done | bytes 262176 | tf_op jit(solution)/shard_map/ppermute | solution.py:322
  94.1 8.2 %all-to-all-start.2 = ((bf16[16,2,24,1024]{3,2,1,0:T(8,128)(2,1)}), bf16[16,2,24,1024]{3,2,1,0:T(8,128)(2,1)S(1)}, u32[]{:S(2)}, u32[]{:S(2)}) async-start(bf16[16,2,24,1024]{3,2,1,0:T(8,128)(2,1)} %get-tuple-element.55), calls=%async_computation.2 | async-start | bytes 3145728 | tf_op jit(solution)/shard_map/all_to_all | solution.py:325
  102.4 0.7 broadcast_select_fusion
  103.2 9.2 %collective-permute-start.10 = (bf16[128,1024]{1,0:T(8,128)(2,1)}, bf16[128,1024]{1,0:T(8,128)(2,1)}, u32[]{:S(2)}, u32[]{:S(2)}) collective-permute-start(bf16[128,1024]{1,0:T(8,128)(2,1)} %broadcast_select_fusion), channel_id=1, source_target_pairs={{3,4},{4,3},{2,5},{5,2},{7,8},{8,7},{6,9},{9,6},{11,12},{12,11},{1... | collective-permute-start | bytes 786440 | tf_op jit(solution)/shard_map/ppermute | solution.py:328
  112.4 1.3 collective-permute-start.7
  113.7 5.3 %collective-permute-start.8 = (bf16[2,128,1024]{2,1,0:T(8,128)(2,1)}, bf16[2,128,1024]{2,1,0:T(8,128)(2,1)}, u32[]{:S(2)}, u32[]{:S(2)}) collective-permute-start(bf16[2,128,1024]{2,1,0:T(8,128)(2,1)} %get-tuple-element.50), channel_id=1, source_target_pairs={{1,0},{2,1},{3,2},{5,4},{6,5},{7,6},{9,8},{10,9},{11,10},{13,12},{... | collective-permute-start | bytes 1572872 | tf_op jit(solution)/shard_map/ppermute | solution.py:321
  119.0 1.6 all-to-all-done.2
  120.9 27.2 %conditional.3 = (f32[1,1024]{1,0:T(1,128)S(1)}) conditional(s32[]{:T(128)} %convert_element_type.51, () %tuple.29, f32[2,24,1024]{2,1,0:T(8,128)S(1)} %convert_reduce_fusion), branch_computations={%region_3.4_spmd, %region_4.6_spmd} | conditional | flops 32768 | bytes 544780 | solution.py:256
  121.0 27.0 %all_to_all.19 = f32[32,1,1024]{2,1,0:T(1,128)S(1)} all-to-all(f32[32,1,1024]{2,1,0:T(1,128)S(1)} %broadcast_in_dim.19), channel_id=1, replica_groups=mesh['zl'=8,'core'=2,'y'=4,'zh'=2,'x'=4] {'zl','core','zh'}, dimensions={0} | all-to-all | bytes 262144 | tf_op jit(solution)/shard_map/cond/branch_1_fun/all_to_all | solution.py:249
  148.2 4.3 %collective-permute-start.11 = (bf16[2,8,1024]{2,1,0:T(8,128)(2,1)S(1)}, bf16[2,8,1024]{2,1,0:T(8,128)(2,1)S(1)}, u32[]{:S(2)}, u32[]{:S(2)}) collective-permute-start(bf16[2,8,1024]{2,1,0:T(8,128)(2,1)S(1)} %slice.77), channel_id=1, source_target_pairs={{0,4},{4,0},{1,5},{5,1},{2,6},{6,2},{3,7},{7,3},{8,12},{12,8},{9,1... | collective-permute-start | bytes 98312 | tf_op jit(solution)/shard_map/ppermute | solution.py:334
  153.3 7.1 %all-to-all-start.3 = ((f32[16,1,1024]{2,1,0:T(1,128)}), f32[16,1,1024]{2,1,0:T(1,128)S(1)}, u32[]{:S(2)}, u32[]{:S(2)}) async-start(f32[16,1,1024]{2,1,0:T(1,128)} %broadcast_in_dim.42), calls=%async_computation.3 | async-start | bytes 131072 | tf_op jit(solution)/shard_map/all_to_all | solution.py:249
  160.4 1.3 collective-permute-start.12
  161.7 1.6 collective-permute-done.11
  163.3 2.8 %all-to-all-done.3 = f32[16,1,1024]{2,1,0:T(1,128)S(1)} async-done(((f32[16,1,1024]{2,1,0:T(1,128)}), f32[16,1,1024]{2,1,0:T(1,128)S(1)}, u32[]{:S(2)}, u32[]{:S(2)}) %all-to-all-start.3) | async-done | bytes 65568 | tf_op jit(solution)/shard_map/all_to_all | solution.py:249
  166.8 3.6 %collective-permute-done.12 = bf16[128,1024]{1,0:T(8,128)(2,1)S(1)} collective-permute-done((bf16[128,1024]{1,0:T(8,128)(2,1)}, bf16[128,1024]{1,0:T(8,128)(2,1)S(1)}, u32[]{:S(2)}, u32[]{:S(2)}) %collective-permute-start.12) | collective-permute-done | bytes 262176 | tf_op jit(solution)/shard_map/ppermute | solution.py:332
  170.3 2.3 %fusion.1 = (bf16[128,1024]{1,0:T(8,128)(2,1)}, bf16[128,1024]{1,0:T(8,128)(2,1)}) fusion(bf16[128,1024]{1,0:T(8,128)(2,1)S(1)} %collective-permute-done.12, f32[2,128,1024]{2,1,0:T(8,128)S(1)} %copy-done.3, bf16[2,128,1024]{2,1,0:T(8,128)(2,1)} %collective-permute-done.8, bf16[2,128,1024]{2,1,0:T(8,128)(2,1)S(1)} %collective-permute-done.7, ...), kind=kLoop, calls=%fused_computation.5 | loop fusion | flops 2621440 | bytes 3211777 | tf_op jit(solution)/shard_map/convert_element_type | solution.py:345
  (43 shorter events, 2.3 us)
Async XLA Ops:
  0.6 22.8 %collective-permute-start.3 = (bf16[128,1024]{1,0:T(8,128)(2,1)}, bf16[128,1024]{1,0:T(8,128)(2,1)S(1)}, u32[]{:S(2)}, u32[]{:S(2)}) collective-permute-start(bf16[128,1024]{1,0:T(8,128)(2,1)} %bitcast.44), channel_id=1, source_target_pairs={{1,0},{2,1},{3,2},{5,4},{6,5},{7,6},{9,8},{10,9},{11,10},{13,12},{... | collective-permute-start | bytes 786440 | tf_op jit(solution)/shard_map/ppermute | solution.py:289
  3.4 20.1 %collective-permute-start.2 = (bf16[128,1024]{1,0:T(8,128)(2,1)}, bf16[128,1024]{1,0:T(8,128)(2,1)S(1)}, u32[]{:S(2)}, u32[]{:S(2)}) collective-permute-start(bf16[128,1024]{1,0:T(8,128)(2,1)} %bitcast.45), channel_id=1, source_target_pairs={{0,1},{1,2},{2,3},{4,5},{5,6},{6,7},{8,9},{9,10},{10,11},{12,13},{... | collective-permute-start | bytes 786440 | tf_op jit(solution)/shard_map/ppermute | solution.py:288
  8.5 31.5 %copy-start.6 = (bf16[136,1024]{1,0:T(8,128)(2,1)S(1)}, bf16[136,1024]{1,0:T(8,128)(2,1)}, u32[]{:S(2)}) copy-start(bf16[136,1024]{1,0:T(8,128)(2,1)} %get-tuple-element.41) | copy-start | bytes 835588
  8.5 17.1 %collective-permute-start.4 = (bf16[2,8,1024]{2,1,0:T(8,128)(2,1)S(1)}, bf16[2,8,1024]{2,1,0:T(8,128)(2,1)S(1)}, u32[]{:S(2)}, u32[]{:S(2)}) collective-permute-start(bf16[2,8,1024]{2,1,0:T(8,128)(2,1)S(1)} %get-tuple-element.42), channel_id=1, source_target_pairs={{0,4},{4,0},{1,5},{5,1},{2,6},{6,2},{3,7},{7,3},{8,12},{12,8},{9,1... | collective-permute-start | bytes 98312 | tf_op jit(solution)/shard_map/ppermute | solution.py:291
  23.5 20.7 %copy-start.4 = (bf16[128,1024]{1,0:T(8,128)(2,1)}, bf16[128,1024]{1,0:T(8,128)(2,1)S(1)}, u32[]{:S(2)}) copy-start(bf16[128,1024]{1,0:T(8,128)(2,1)S(1)} %collective-permute-done.3.down_v_ref) | copy-start | bytes 786436
  23.5 20.7 %copy-start.5 = (bf16[128,1024]{1,0:T(8,128)(2,1)}, bf16[128,1024]{1,0:T(8,128)(2,1)S(1)}, u32[]{:S(2)}) copy-start(bf16[128,1024]{1,0:T(8,128)(2,1)S(1)} %collective-permute-done.2.up_v_ref) | copy-start | bytes 786436
  25.5 42.9 %collective-permute-start.5 = (bf16[136,1024]{1,0:T(8,128)(2,1)S(1)}, bf16[136,1024]{1,0:T(8,128)(2,1)S(1)}, u32[]{:S(2)}, u32[]{:S(2)}) collective-permute-start(bf16[136,1024]{1,0:T(8,128)(2,1)S(1)} %pad_select_fusion), channel_id=1, source_target_pairs={{3,4},{4,3},{2,5},{5,2},{7,8},{8,7},{6,9},{9,6},{11,12},{12,11},{1... | collective-permute-start | bytes 835592 | tf_op jit(solution)/shard_map/ppermute | solution.py:297
  40.0 29.7 %collective-permute-start.1 = (bf16[136,1024]{1,0:T(8,128)(2,1)S(1)}, bf16[136,1024]{1,0:T(8,128)(2,1)S(1)}, u32[]{:S(2)}, u32[]{:S(2)}) collective-permute-start(bf16[136,1024]{1,0:T(8,128)(2,1)S(1)} %copy-done.6), channel_id=1, source_target_pairs={{1,0},{2,1},{3,2},{5,4},{6,5},{7,6},{9,8},{10,9},{11,10},{13,12},{... | collective-permute-start | bytes 835592 | tf_op jit(solution)/shard_map/ppermute | solution.py:293
  42.8 27.0 %collective-permute-start = (bf16[136,1024]{1,0:T(8,128)(2,1)S(1)}, bf16[136,1024]{1,0:T(8,128)(2,1)S(1)}, u32[]{:S(2)}, u32[]{:S(2)}) collective-permute-start(bf16[136,1024]{1,0:T(8,128)(2,1)S(1)} %copy-done.6), channel_id=1, source_target_pairs={{0,1},{1,2},{2,3},{4,5},{5,6},{6,7},{8,9},{9,10},{10,11},{12,13},{... | collective-permute-start | bytes 835592 | tf_op jit(solution)/shard_map/ppermute | solution.py:292
  68.4 8.7 %copy-start = (bf16[136,1024]{1,0:T(8,128)(2,1)}, bf16[136,1024]{1,0:T(8,128)(2,1)S(1)}, u32[]{:S(2)}) copy-start(bf16[136,1024]{1,0:T(8,128)(2,1)S(1)} %collective-permute-done.5.cross_k_ref.cross_go_ref) | copy-start | bytes 835588
  68.5 8.7 %collective-permute-start.6 = (bf16[128,1024]{1,0:T(8,128)(2,1)S(1)}, bf16[128,1024]{1,0:T(8,128)(2,1)S(1)}, u32[]{:S(2)}, u32[]{:S(2)}) collective-permute-start(bf16[128,1024]{1,0:T(8,128)(2,1)S(1)} %slice.45), channel_id=1, source_target_pairs={{2,3},{1,0},{6,7},{5,4},{10,11},{9,8},{14,15},{13,12},{18,19},{17,... | collective-permute-start | bytes 786440 | tf_op jit(solution)/shard_map/ppermute | solution.py:305
  69.8 7.4 %copy-start.1 = (bf16[136,1024]{1,0:T(8,128)(2,1)}, bf16[136,1024]{1,0:T(8,128)(2,1)S(1)}, u32[]{:S(2)}) copy-start(bf16[136,1024]{1,0:T(8,128)(2,1)S(1)} %collective-permute-done.1.down_k_ref.down_go_ref) | copy-start | bytes 835588
  69.8 7.4 %copy-start.2 = (bf16[136,1024]{1,0:T(8,128)(2,1)}, bf16[136,1024]{1,0:T(8,128)(2,1)S(1)}, u32[]{:S(2)}) copy-start(bf16[136,1024]{1,0:T(8,128)(2,1)S(1)} %collective-permute-done.up_k_ref.up_go_ref) | copy-start | bytes 835588
  77.1 0.7 copy-start.7
  88.5 5.6 %collective-permute-start.9 = (bf16[128,1024]{1,0:T(8,128)(2,1)}, bf16[128,1024]{1,0:T(8,128)(2,1)S(1)}, u32[]{:S(2)}, u32[]{:S(2)}) collective-permute-start(bf16[128,1024]{1,0:T(8,128)(2,1)} %get-tuple-element.52), channel_id=1, source_target_pairs={{3,2},{0,1},{7,6},{4,5},{11,10},{8,9},{15,14},{12,13},{19,18},{16,... | collective-permute-start | bytes 786440 | tf_op jit(solution)/shard_map/ppermute | solution.py:322
  94.1 8.3 %copy-start.8 = (bf16[128,1024]{1,0:T(8,128)(2,1)S(1)}, bf16[128,1024]{1,0:T(8,128)(2,1)}, u32[]{:S(2)}) copy-start(bf16[128,1024]{1,0:T(8,128)(2,1)} %get-tuple-element.51) | copy-start | bytes 786436
  94.1 26.5 %all-to-all-start.2 = ((bf16[16,2,24,1024]{3,2,1,0:T(8,128)(2,1)}), bf16[16,2,24,1024]{3,2,1,0:T(8,128)(2,1)S(1)}, u32[]{:S(2)}, u32[]{:S(2)}) async-start(bf16[16,2,24,1024]{3,2,1,0:T(8,128)(2,1)} %get-tuple-element.55), calls=%async_computation.2 | async-start | bytes 3145728 | tf_op jit(solution)/shard_map/all_to_all | solution.py:325
  103.2 67.2 %copy-start.3 = (f32[2,128,1024]{2,1,0:T(8,128)S(1)}, f32[2,128,1024]{2,1,0:T(8,128)}, u32[]{:S(2)}) copy-start(f32[2,128,1024]{2,1,0:T(8,128)} %get-tuple-element.48) | copy-start | bytes 3145732
  103.2 45.0 %collective-permute-start.10 = (bf16[128,1024]{1,0:T(8,128)(2,1)}, bf16[128,1024]{1,0:T(8,128)(2,1)}, u32[]{:S(2)}, u32[]{:S(2)}) collective-permute-start(bf16[128,1024]{1,0:T(8,128)(2,1)} %broadcast_select_fusion), channel_id=1, source_target_pairs={{3,4},{4,3},{2,5},{5,2},{7,8},{8,7},{6,9},{9,6},{11,12},{12,11},{1... | collective-permute-start | bytes 786440 | tf_op jit(solution)/shard_map/ppermute | solution.py:328
  112.4 54.4 %collective-permute-start.7 = (bf16[2,128,1024]{2,1,0:T(8,128)(2,1)}, bf16[2,128,1024]{2,1,0:T(8,128)(2,1)S(1)}, u32[]{:S(2)}, u32[]{:S(2)}) collective-permute-start(bf16[2,128,1024]{2,1,0:T(8,128)(2,1)} %get-tuple-element.49), channel_id=1, source_target_pairs={{0,1},{1,2},{2,3},{4,5},{5,6},{6,7},{8,9},{9,10},{10,11},{12,13},{... | collective-permute-start | bytes 1572872 | tf_op jit(solution)/shard_map/ppermute | solution.py:320
  113.7 53.1 %collective-permute-start.8 = (bf16[2,128,1024]{2,1,0:T(8,128)(2,1)}, bf16[2,128,1024]{2,1,0:T(8,128)(2,1)}, u32[]{:S(2)}, u32[]{:S(2)}) collective-permute-start(bf16[2,128,1024]{2,1,0:T(8,128)(2,1)} %get-tuple-element.50), channel_id=1, source_target_pairs={{1,0},{2,1},{3,2},{5,4},{6,5},{7,6},{9,8},{10,9},{11,10},{13,12},{... | collective-permute-start | bytes 1572872 | tf_op jit(solution)/shard_map/ppermute | solution.py:321
  148.2 15.1 %collective-permute-start.11 = (bf16[2,8,1024]{2,1,0:T(8,128)(2,1)S(1)}, bf16[2,8,1024]{2,1,0:T(8,128)(2,1)S(1)}, u32[]{:S(2)}, u32[]{:S(2)}) collective-permute-start(bf16[2,8,1024]{2,1,0:T(8,128)(2,1)S(1)} %slice.77), channel_id=1, source_target_pairs={{0,4},{4,0},{1,5},{5,1},{2,6},{6,2},{3,7},{7,3},{8,12},{12,8},{9,1... | collective-permute-start | bytes 98312 | tf_op jit(solution)/shard_map/ppermute | solution.py:334
  153.3 12.8 %all-to-all-start.3 = ((f32[16,1,1024]{2,1,0:T(1,128)}), f32[16,1,1024]{2,1,0:T(1,128)S(1)}, u32[]{:S(2)}, u32[]{:S(2)}) async-start(f32[16,1,1024]{2,1,0:T(1,128)} %broadcast_in_dim.42), calls=%async_computation.3 | async-start | bytes 131072 | tf_op jit(solution)/shard_map/all_to_all | solution.py:249
  160.4 9.9 %collective-permute-start.12 = (bf16[128,1024]{1,0:T(8,128)(2,1)}, bf16[128,1024]{1,0:T(8,128)(2,1)S(1)}, u32[]{:S(2)}, u32[]{:S(2)}) collective-permute-start(bf16[128,1024]{1,0:T(8,128)(2,1)} %collective-permute-done.10), channel_id=1, source_target_pairs={{2,3},{1,0},{6,7},{5,4},{10,11},{9,8},{14,15},{13,12},{18,19},{17,... | collective-permute-start | bytes 786440 | tf_op jit(solution)/shard_map/ppermute | solution.py:332

commit v4 on v3

--- a/solution.py
+++ b/solution.py
@@ -52,7 +52,7 @@
 
 def pack(frames, keys, values, grad_out):
     width = keys.shape[1]
-    chunk = 256
+    chunk = 512
     own = pl.BlockSpec((BLK, chunk), lambda c: (0, c))
     return pl.pallas_call(
         pack_kernel,

time: 173 us -> 172 us (level)
  transfers between devices with their start and end apart: 15 -> 15, of which waited for: 7 -> 7; matrix products, arithmetic and copies ran while one was open for 2% -> 2% of each run, Pallas kernels for 2% -> 1%
where the time goes in v4:
time: 172 us; the launch traced here: 171 us
  starting transfers between devices  77 us (45%)
  blocking collectives  51.2 us (30%)
  waiting for transfers between devices  21.9 us (13%)
  Pallas kernels  12.6 us (7%)
  other arithmetic  4.82 us (3%)
  local copies, waits for them, and re-layouts  2.35 us (1%)
    all_to_all x2, blocking collectives, spread(): lax.all_to_all(jnp.broadcast_to(block[None], (count,) + block.shape), axe...  51.2 us
    ppermute x1, starting transfers between devices, per_device(): other_summary = lax.ppermute(own_summary, 'zh', swap)  14.9 us
    ppermute x1, starting transfers between devices, per_device(): cross_k = lax.ppermute(crossing, TM, diagonal)  14.5 us
    pallas_call x1, Pallas kernels, attend(): pl.pallas_call(attend_kernel, grid=(width // step,), out_shape=(jax.Shape...  10.6 us
    ppermute x1, starting transfers between devices, per_device(): cross_dk = lax.ppermute(jnp.where(edge, cross_dk, relay), TM, diagonal)  9.19 us
    all_to_all x1, starting transfers between devices, per_device(): dsum = lax.all_to_all(dsum, PLANE, 0, 0, tiled=True)  8.18 us
    ppermute x1, waiting for transfers between devices, per_device(): cross_v = lax.ppermute(cross_k[:BLK], TM, outward)  7.33 us
    all_to_all x1, starting transfers between devices, spread(): lax.all_to_all(jnp.broadcast_to(block[None], (count,) + block.shape), axe...  7.12 us
  transfers between devices with their start and end apart: 15, of which 7 were waited for; matrix products, arithmetic and copies ran while one was open for 2% of the time, Pallas kernels for 1%

profile of v4, /device:TPU:38, one launch (start us, length us, event | category | flops | bytes accessed | tf_op | source)
XLA Modules:
  0.0 171.4 jit_solution(9972515123095298817)
XLA Ops:
  0.6 2.8 %collective-permute-start.3 = (bf16[128,1024]{1,0:T(8,128)(2,1)}, bf16[128,1024]{1,0:T(8,128)(2,1)S(1)}, u32[]{:S(2)}, u32[]{:S(2)}) collective-permute-start(bf16[128,1024]{1,0:T(8,128)(2,1)} %bitcast.44), channel_id=1, source_target_pairs={{1,0},{2,1},{3,2},{5,4},{6,5},{7,6},{9,8},{10,9},{11,10},{13,12},{... | collective-permute-start | bytes 786440 | tf_op jit(solution)/shard_map/ppermute | solution.py:289
  3.4 1.3 collective-permute-start.2
  5.3 1.9 %pack.1 = (bf16[136,1024]{1,0:T(8,128)(2,1)}, bf16[2,8,1024]{2,1,0:T(8,128)(2,1)S(1)}) custom-call(s32[1]{0:T(128)} %copy.20.frames, bf16[128,1024]{1,0:T(8,128)(2,1)} %bitcast.42, bf16[128,1024]{1,0:T(8,128)(2,1)} %bitcast.46, bf16[128,1024]{1,0:T(8,128)(2,1)} %bitcast.48), custom_call_target="tpu_custom_call" | custom-call | tf_op jit(solution)/shard_map/pack/pallas_call | solution.py:57
  7.3 14.9 %collective-permute-start.4 = (bf16[2,8,1024]{2,1,0:T(8,128)(2,1)S(1)}, bf16[2,8,1024]{2,1,0:T(8,128)(2,1)S(1)}, u32[]{:S(2)}, u32[]{:S(2)}) collective-permute-start(bf16[2,8,1024]{2,1,0:T(8,128)(2,1)S(1)} %get-tuple-element.42), channel_id=1, source_target_pairs={{0,4},{4,0},{1,5},{5,1},{2,6},{6,2},{3,7},{7,3},{8,12},{12,8},{9,1... | collective-permute-start | bytes 98312 | tf_op jit(solution)/shard_map/ppermute | solution.py:291
  22.3 1.2 pad_select_fusion
  23.5 0.8 collective-permute-done.4
  24.3 14.5 %collective-permute-start.5 = (bf16[136,1024]{1,0:T(8,128)(2,1)S(1)}, bf16[136,1024]{1,0:T(8,128)(2,1)S(1)}, u32[]{:S(2)}, u32[]{:S(2)}) collective-permute-start(bf16[136,1024]{1,0:T(8,128)(2,1)S(1)} %pad_select_fusion), channel_id=1, source_target_pairs={{3,4},{4,3},{2,5},{5,2},{7,8},{8,7},{6,9},{9,6},{11,12},{12,11},{1... | collective-permute-start | bytes 835592 | tf_op jit(solution)/shard_map/ppermute | solution.py:297
  38.8 2.8 %collective-permute-start.1 = (bf16[136,1024]{1,0:T(8,128)(2,1)S(1)}, bf16[136,1024]{1,0:T(8,128)(2,1)S(1)}, u32[]{:S(2)}, u32[]{:S(2)}) collective-permute-start(bf16[136,1024]{1,0:T(8,128)(2,1)S(1)} %copy-done.6), channel_id=1, source_target_pairs={{1,0},{2,1},{3,2},{5,4},{6,5},{7,6},{9,8},{10,9},{11,10},{13,12},{... | collective-permute-start | bytes 835592 | tf_op jit(solution)/shard_map/ppermute | solution.py:293
  41.6 1.3 collective-permute-start
  42.9 24.3 %conditional.2 = (bf16[16,2,16,1024]{3,2,1,0:T(8,128)(2,1)S(1)}) conditional(s32[]{:T(128)} %convert_element_type.51, () %tuple.25, (bf16[2,8,1024]{2,1,0:T(8,128)(2,1)S(1)}, bf16[2,8,1024]{2,1,0:T(8,128)(2,1)S(1)}) %tuple.26), branch_computations={%region_0.1_spmd, %region_1.2_spmd} | conditional | flops 131072 | bytes 3342344 | solution.py:256
  43.1 24.1 %all_to_all.18 = bf16[16,2,16,1024]{3,2,1,0:T(8,128)(2,1)S(1)} all-to-all(bf16[16,2,16,1024]{3,2,1,0:T(8,128)(2,1)S(1)} %broadcast_in_dim.18), channel_id=1, replica_groups=mesh['zl'=8,'core'=2,'y'=4,'zh'=2,'x'=4] {'y','x'}, dimensions={0} | all-to-all | bytes 2097152 | tf_op jit(solution)/shard_map/cond/branch_1_fun/all_to_all | solution.py:249
  67.2 1.3 collective-permute-start.6
  68.6 7.3 %collective-permute-done.6.cross_v_ref = bf16[128,1024]{1,0:T(8,128)(2,1)S(1)} collective-permute-done((bf16[128,1024]{1,0:T(8,128)(2,1)S(1)}, bf16[128,1024]{1,0:T(8,128)(2,1)S(1)}, u32[]{:S(2)}, u32[]{:S(2)}) %collective-permute-start.6) | collective-permute-done | bytes 262176 | tf_op jit(solution)/shard_map/ppermute | solution.py:305
  75.9 0.7 copy-done.7
  76.6 10.6 %attend.1 = (bf16[128,1024]{1,0:T(8,128)(2,1)}, f32[2,128,1024]{2,1,0:T(8,128)}, bf16[2,128,1024]{2,1,0:T(8,128)(2,1)}, bf16[2,128,1024]{2,1,0:T(8,128)(2,1)}, b...) custom-call(s32[1]{0:T(128)} %copy.20.frames, s32[2]{0:T(128)} %bitcast.57, ...), custom_call_target="tpu_custom_call" | custom-call | flops 1006632960 | bytes 8388608 | tf_op jit(solution)/shard_map/attend/pallas_call | solution.py:210
  87.3 1.5 collective-permute-start.9
  88.7 4.2 %collective-permute-done.9 = bf16[128,1024]{1,0:T(8,128)(2,1)S(1)} collective-permute-done((bf16[128,1024]{1,0:T(8,128)(2,1)}, bf16[128,1024]{1,0:T(8,128)(2,1)S(1)}, u32[]{:S(2)}, u32[]{:S(2)}) %collective-permute-start.9) | collective-permute-done | bytes 262176 | tf_op jit(solution)/shard_map/ppermute | solution.py:322
  92.9 8.2 %all-to-all-start.2 = ((bf16[16,2,24,1024]{3,2,1,0:T(8,128)(2,1)}), bf16[16,2,24,1024]{3,2,1,0:T(8,128)(2,1)S(1)}, u32[]{:S(2)}, u32[]{:S(2)}) async-start(bf16[16,2,24,1024]{3,2,1,0:T(8,128)(2,1)} %get-tuple-element.55), calls=%async_computation.2 | async-start | bytes 3145728 | tf_op jit(solution)/shard_map/all_to_all | solution.py:325
  101.2 0.7 broadcast_select_fusion
  101.9 9.2 %collective-permute-start.10 = (bf16[128,1024]{1,0:T(8,128)(2,1)}, bf16[128,1024]{1,0:T(8,128)(2,1)}, u32[]{:S(2)}, u32[]{:S(2)}) collective-permute-start(bf16[128,1024]{1,0:T(8,128)(2,1)} %broadcast_select_fusion), channel_id=1, source_target_pairs={{3,4},{4,3},{2,5},{5,2},{7,8},{8,7},{6,9},{9,6},{11,12},{12,11},{1... | collective-permute-start | bytes 786440 | tf_op jit(solution)/shard_map/ppermute | solution.py:328
  111.1 1.3 collective-permute-start.7
  112.4 5.3 %collective-permute-start.8 = (bf16[2,128,1024]{2,1,0:T(8,128)(2,1)}, bf16[2,128,1024]{2,1,0:T(8,128)(2,1)}, u32[]{:S(2)}, u32[]{:S(2)}) collective-permute-start(bf16[2,128,1024]{2,1,0:T(8,128)(2,1)} %get-tuple-element.50), channel_id=1, source_target_pairs={{1,0},{2,1},{3,2},{5,4},{6,5},{7,6},{9,8},{10,9},{11,10},{13,12},{... | collective-permute-start | bytes 1572872 | tf_op jit(solution)/shard_map/ppermute | solution.py:321
  117.8 1.6 all-to-all-done.2
  119.7 27.2 %conditional.3 = (f32[1,1024]{1,0:T(1,128)S(1)}) conditional(s32[]{:T(128)} %convert_element_type.51, () %tuple.29, f32[2,24,1024]{2,1,0:T(8,128)S(1)} %convert_reduce_fusion), branch_computations={%region_3.4_spmd, %region_4.6_spmd} | conditional | flops 32768 | bytes 544780 | solution.py:256
  119.8 27.0 %all_to_all.19 = f32[32,1,1024]{2,1,0:T(1,128)S(1)} all-to-all(f32[32,1,1024]{2,1,0:T(1,128)S(1)} %broadcast_in_dim.19), channel_id=1, replica_groups=mesh['zl'=8,'core'=2,'y'=4,'zh'=2,'x'=4] {'zl','core','zh'}, dimensions={0} | all-to-all | bytes 262144 | tf_op jit(solution)/shard_map/cond/branch_1_fun/all_to_all | solution.py:249
  147.0 4.3 %collective-permute-start.11 = (bf16[2,8,1024]{2,1,0:T(8,128)(2,1)S(1)}, bf16[2,8,1024]{2,1,0:T(8,128)(2,1)S(1)}, u32[]{:S(2)}, u32[]{:S(2)}) collective-permute-start(bf16[2,8,1024]{2,1,0:T(8,128)(2,1)S(1)} %slice.77), channel_id=1, source_target_pairs={{0,4},{4,0},{1,5},{5,1},{2,6},{6,2},{3,7},{7,3},{8,12},{12,8},{9,1... | collective-permute-start | bytes 98312 | tf_op jit(solution)/shard_map/ppermute | solution.py:334
  152.1 7.1 %all-to-all-start.3 = ((f32[16,1,1024]{2,1,0:T(1,128)}), f32[16,1,1024]{2,1,0:T(1,128)S(1)}, u32[]{:S(2)}, u32[]{:S(2)}) async-start(f32[16,1,1024]{2,1,0:T(1,128)} %broadcast_in_dim.42), calls=%async_computation.3 | async-start | bytes 131072 | tf_op jit(solution)/shard_map/all_to_all | solution.py:249
  159.2 1.3 collective-permute-start.12
  160.5 1.6 collective-permute-done.11
  162.1 2.8 %all-to-all-done.3 = f32[16,1,1024]{2,1,0:T(1,128)S(1)} async-done(((f32[16,1,1024]{2,1,0:T(1,128)}), f32[16,1,1024]{2,1,0:T(1,128)S(1)}, u32[]{:S(2)}, u32[]{:S(2)}) %all-to-all-start.3) | async-done | bytes 65568 | tf_op jit(solution)/shard_map/all_to_all | solution.py:249
  165.5 3.6 %collective-permute-done.12 = bf16[128,1024]{1,0:T(8,128)(2,1)S(1)} collective-permute-done((bf16[128,1024]{1,0:T(8,128)(2,1)}, bf16[128,1024]{1,0:T(8,128)(2,1)S(1)}, u32[]{:S(2)}, u32[]{:S(2)}) %collective-permute-start.12) | collective-permute-done | bytes 262176 | tf_op jit(solution)/shard_map/ppermute | solution.py:332
  169.1 2.3 %fusion.1 = (bf16[128,1024]{1,0:T(8,128)(2,1)}, bf16[128,1024]{1,0:T(8,128)(2,1)}) fusion(bf16[128,1024]{1,0:T(8,128)(2,1)S(1)} %collective-permute-done.12, f32[2,128,1024]{2,1,0:T(8,128)S(1)} %copy-done.3, bf16[2,128,1024]{2,1,0:T(8,128)(2,1)} %collective-permute-done.8, bf16[2,128,1024]{2,1,0:T(8,128)(2,1)S(1)} %collective-permute-done.7, ...), kind=kLoop, calls=%fused_computation.5 | loop fusion | flops 2621440 | bytes 3211777 | tf_op jit(solution)/shard_map/convert_element_type | solution.py:345
  (43 shorter events, 2.3 us)
Async XLA Ops:
  0.6 21.6 %collective-permute-start.3 = (bf16[128,1024]{1,0:T(8,128)(2,1)}, bf16[128,1024]{1,0:T(8,128)(2,1)S(1)}, u32[]{:S(2)}, u32[]{:S(2)}) collective-permute-start(bf16[128,1024]{1,0:T(8,128)(2,1)} %bitcast.44), channel_id=1, source_target_pairs={{1,0},{2,1},{3,2},{5,4},{6,5},{7,6},{9,8},{10,9},{11,10},{13,12},{... | collective-permute-start | bytes 786440 | tf_op jit(solution)/shard_map/ppermute | solution.py:289
  3.4 18.9 %collective-permute-start.2 = (bf16[128,1024]{1,0:T(8,128)(2,1)}, bf16[128,1024]{1,0:T(8,128)(2,1)S(1)}, u32[]{:S(2)}, u32[]{:S(2)}) collective-permute-start(bf16[128,1024]{1,0:T(8,128)(2,1)} %bitcast.45), channel_id=1, source_target_pairs={{0,1},{1,2},{2,3},{4,5},{5,6},{6,7},{8,9},{9,10},{10,11},{12,13},{... | collective-permute-start | bytes 786440 | tf_op jit(solution)/shard_map/ppermute | solution.py:288
  7.2 31.5 %copy-start.6 = (bf16[136,1024]{1,0:T(8,128)(2,1)S(1)}, bf16[136,1024]{1,0:T(8,128)(2,1)}, u32[]{:S(2)}) copy-start(bf16[136,1024]{1,0:T(8,128)(2,1)} %get-tuple-element.41) | copy-start | bytes 835588
  7.3 17.1 %collective-permute-start.4 = (bf16[2,8,1024]{2,1,0:T(8,128)(2,1)S(1)}, bf16[2,8,1024]{2,1,0:T(8,128)(2,1)S(1)}, u32[]{:S(2)}, u32[]{:S(2)}) collective-permute-start(bf16[2,8,1024]{2,1,0:T(8,128)(2,1)S(1)} %get-tuple-element.42), channel_id=1, source_target_pairs={{0,4},{4,0},{1,5},{5,1},{2,6},{6,2},{3,7},{7,3},{8,12},{12,8},{9,1... | collective-permute-start | bytes 98312 | tf_op jit(solution)/shard_map/ppermute | solution.py:291
  22.2 20.7 %copy-start.4 = (bf16[128,1024]{1,0:T(8,128)(2,1)}, bf16[128,1024]{1,0:T(8,128)(2,1)S(1)}, u32[]{:S(2)}) copy-start(bf16[128,1024]{1,0:T(8,128)(2,1)S(1)} %collective-permute-done.3.down_v_ref) | copy-start | bytes 786436
  22.2 20.7 %copy-start.5 = (bf16[128,1024]{1,0:T(8,128)(2,1)}, bf16[128,1024]{1,0:T(8,128)(2,1)S(1)}, u32[]{:S(2)}) copy-start(bf16[128,1024]{1,0:T(8,128)(2,1)S(1)} %collective-permute-done.2.up_v_ref) | copy-start | bytes 786436
  24.3 42.9 %collective-permute-start.5 = (bf16[136,1024]{1,0:T(8,128)(2,1)S(1)}, bf16[136,1024]{1,0:T(8,128)(2,1)S(1)}, u32[]{:S(2)}, u32[]{:S(2)}) collective-permute-start(bf16[136,1024]{1,0:T(8,128)(2,1)S(1)} %pad_select_fusion), channel_id=1, source_target_pairs={{3,4},{4,3},{2,5},{5,2},{7,8},{8,7},{6,9},{9,6},{11,12},{12,11},{1... | collective-permute-start | bytes 835592 | tf_op jit(solution)/shard_map/ppermute | solution.py:297
  38.8 29.7 %collective-permute-start.1 = (bf16[136,1024]{1,0:T(8,128)(2,1)S(1)}, bf16[136,1024]{1,0:T(8,128)(2,1)S(1)}, u32[]{:S(2)}, u32[]{:S(2)}) collective-permute-start(bf16[136,1024]{1,0:T(8,128)(2,1)S(1)} %copy-done.6), channel_id=1, source_target_pairs={{1,0},{2,1},{3,2},{5,4},{6,5},{7,6},{9,8},{10,9},{11,10},{13,12},{... | collective-permute-start | bytes 835592 | tf_op jit(solution)/shard_map/ppermute | solution.py:293
  41.6 27.0 %collective-permute-start = (bf16[136,1024]{1,0:T(8,128)(2,1)S(1)}, bf16[136,1024]{1,0:T(8,128)(2,1)S(1)}, u32[]{:S(2)}, u32[]{:S(2)}) collective-permute-start(bf16[136,1024]{1,0:T(8,128)(2,1)S(1)} %copy-done.6), channel_id=1, source_target_pairs={{0,1},{1,2},{2,3},{4,5},{5,6},{6,7},{8,9},{9,10},{10,11},{12,13},{... | collective-permute-start | bytes 835592 | tf_op jit(solution)/shard_map/ppermute | solution.py:292
  67.2 8.7 %copy-start = (bf16[136,1024]{1,0:T(8,128)(2,1)}, bf16[136,1024]{1,0:T(8,128)(2,1)S(1)}, u32[]{:S(2)}) copy-start(bf16[136,1024]{1,0:T(8,128)(2,1)S(1)} %collective-permute-done.5.cross_k_ref.cross_go_ref) | copy-start | bytes 835588
  67.2 8.7 %collective-permute-start.6 = (bf16[128,1024]{1,0:T(8,128)(2,1)S(1)}, bf16[128,1024]{1,0:T(8,128)(2,1)S(1)}, u32[]{:S(2)}, u32[]{:S(2)}) collective-permute-start(bf16[128,1024]{1,0:T(8,128)(2,1)S(1)} %slice.45), channel_id=1, source_target_pairs={{2,3},{1,0},{6,7},{5,4},{10,11},{9,8},{14,15},{13,12},{18,19},{17,... | collective-permute-start | bytes 786440 | tf_op jit(solution)/shard_map/ppermute | solution.py:305
  68.5 7.4 %copy-start.1 = (bf16[136,1024]{1,0:T(8,128)(2,1)}, bf16[136,1024]{1,0:T(8,128)(2,1)S(1)}, u32[]{:S(2)}) copy-start(bf16[136,1024]{1,0:T(8,128)(2,1)S(1)} %collective-permute-done.1.down_k_ref.down_go_ref) | copy-start | bytes 835588
  68.6 7.4 %copy-start.2 = (bf16[136,1024]{1,0:T(8,128)(2,1)}, bf16[136,1024]{1,0:T(8,128)(2,1)S(1)}, u32[]{:S(2)}) copy-start(bf16[136,1024]{1,0:T(8,128)(2,1)S(1)} %collective-permute-done.up_k_ref.up_go_ref) | copy-start | bytes 835588
  75.9 0.7 copy-start.7
  87.3 5.6 %collective-permute-start.9 = (bf16[128,1024]{1,0:T(8,128)(2,1)}, bf16[128,1024]{1,0:T(8,128)(2,1)S(1)}, u32[]{:S(2)}, u32[]{:S(2)}) collective-permute-start(bf16[128,1024]{1,0:T(8,128)(2,1)} %get-tuple-element.52), channel_id=1, source_target_pairs={{3,2},{0,1},{7,6},{4,5},{11,10},{8,9},{15,14},{12,13},{19,18},{16,... | collective-permute-start | bytes 786440 | tf_op jit(solution)/shard_map/ppermute | solution.py:322
  92.9 8.3 %copy-start.8 = (bf16[128,1024]{1,0:T(8,128)(2,1)S(1)}, bf16[128,1024]{1,0:T(8,128)(2,1)}, u32[]{:S(2)}) copy-start(bf16[128,1024]{1,0:T(8,128)(2,1)} %get-tuple-element.51) | copy-start | bytes 786436
  92.9 26.5 %all-to-all-start.2 = ((bf16[16,2,24,1024]{3,2,1,0:T(8,128)(2,1)}), bf16[16,2,24,1024]{3,2,1,0:T(8,128)(2,1)S(1)}, u32[]{:S(2)}, u32[]{:S(2)}) async-start(bf16[16,2,24,1024]{3,2,1,0:T(8,128)(2,1)} %get-tuple-element.55), calls=%async_computation.2 | async-start | bytes 3145728 | tf_op jit(solution)/shard_map/all_to_all | solution.py:325
  101.9 67.2 %copy-start.3 = (f32[2,128,1024]{2,1,0:T(8,128)S(1)}, f32[2,128,1024]{2,1,0:T(8,128)}, u32[]{:S(2)}) copy-start(f32[2,128,1024]{2,1,0:T(8,128)} %get-tuple-element.48) | copy-start | bytes 3145732
  101.9 45.0 %collective-permute-start.10 = (bf16[128,1024]{1,0:T(8,128)(2,1)}, bf16[128,1024]{1,0:T(8,128)(2,1)}, u32[]{:S(2)}, u32[]{:S(2)}) collective-permute-start(bf16[128,1024]{1,0:T(8,128)(2,1)} %broadcast_select_fusion), channel_id=1, source_target_pairs={{3,4},{4,3},{2,5},{5,2},{7,8},{8,7},{6,9},{9,6},{11,12},{12,11},{1... | collective-permute-start | bytes 786440 | tf_op jit(solution)/shard_map/ppermute | solution.py:328
  111.1 54.4 %collective-permute-start.7 = (bf16[2,128,1024]{2,1,0:T(8,128)(2,1)}, bf16[2,128,1024]{2,1,0:T(8,128)(2,1)S(1)}, u32[]{:S(2)}, u32[]{:S(2)}) collective-permute-start(bf16[2,128,1024]{2,1,0:T(8,128)(2,1)} %get-tuple-element.49), channel_id=1, source_target_pairs={{0,1},{1,2},{2,3},{4,5},{5,6},{6,7},{8,9},{9,10},{10,11},{12,13},{... | collective-permute-start | bytes 1572872 | tf_op jit(solution)/shard_map/ppermute | solution.py:320
  112.4 53.1 %collective-permute-start.8 = (bf16[2,128,1024]{2,1,0:T(8,128)(2,1)}, bf16[2,128,1024]{2,1,0:T(8,128)(2,1)}, u32[]{:S(2)}, u32[]{:S(2)}) collective-permute-start(bf16[2,128,1024]{2,1,0:T(8,128)(2,1)} %get-tuple-element.50), channel_id=1, source_target_pairs={{1,0},{2,1},{3,2},{5,4},{6,5},{7,6},{9,8},{10,9},{11,10},{13,12},{... | collective-permute-start | bytes 1572872 | tf_op jit(solution)/shard_map/ppermute | solution.py:321
  147.0 15.1 %collective-permute-start.11 = (bf16[2,8,1024]{2,1,0:T(8,128)(2,1)S(1)}, bf16[2,8,1024]{2,1,0:T(8,128)(2,1)S(1)}, u32[]{:S(2)}, u32[]{:S(2)}) collective-permute-start(bf16[2,8,1024]{2,1,0:T(8,128)(2,1)S(1)} %slice.77), channel_id=1, source_target_pairs={{0,4},{4,0},{1,5},{5,1},{2,6},{6,2},{3,7},{7,3},{8,12},{12,8},{9,1... | collective-permute-start | bytes 98312 | tf_op jit(solution)/shard_map/ppermute | solution.py:334
  152.1 12.8 %all-to-all-start.3 = ((f32[16,1,1024]{2,1,0:T(1,128)}), f32[16,1,1024]{2,1,0:T(1,128)S(1)}, u32[]{:S(2)}, u32[]{:S(2)}) async-start(f32[16,1,1024]{2,1,0:T(1,128)} %broadcast_in_dim.42), calls=%async_computation.3 | async-start | bytes 131072 | tf_op jit(solution)/shard_map/all_to_all | solution.py:249
  159.2 9.9 %collective-permute-start.12 = (bf16[128,1024]{1,0:T(8,128)(2,1)}, bf16[128,1024]{1,0:T(8,128)(2,1)S(1)}, u32[]{:S(2)}, u32[]{:S(2)}) collective-permute-start(bf16[128,1024]{1,0:T(8,128)(2,1)} %collective-permute-done.10), channel_id=1, source_target_pairs={{2,3},{1,0},{6,7},{5,4},{10,11},{9,8},{14,15},{13,12},{18,19},{17,... | collective-permute-start | bytes 786440 | tf_op jit(solution)/shard_map/ppermute | solution.py:332

commit v5 on v4

--- a/solution.py
+++ b/solution.py
@@ -330,7 +330,7 @@
     tap = fenced(there, lambda tap: jnp.sum(spread(tap, LINE, 32), axis=0), tap)
     cross_dk, dsum, tap = lax.optimization_barrier((cross_dk, dsum, tap))
     cross_dv = lax.ppermute(cross_dk, TM, outward)
-    taps = spread(tap, PLANE, 16)[:KW, 0]
+    taps = fenced(there, lambda tap: spread(tap, PLANE, 16)[:KW, 0], tap)
     other = lax.ppermute(dsum[:, SUMM : 2 * SUMM].astype(jnp.bfloat16), "zh", swap)
     dsum = dsum[:, :SUMM] + other.astype(jnp.float32)
 

time: 172 us -> 172 us (level)
  the two profiles are of different devices: /device:TPU:38 before, /device:TPU:32 now
where the time goes in v5:
time: 172 us; the launch traced here: 171 us
  blocking collectives  74.4 us (43%)
  starting transfers between devices  48.2 us (28%)
  waiting for transfers between devices  28.5 us (17%)
  Pallas kernels  12.5 us (7%)
  other arithmetic  4.84 us (3%)
    all_to_all x3, blocking collectives, spread(): lax.all_to_all(jnp.broadcast_to(block[None], (count,) + block.shape), axe...  74.4 us
    all_to_all x1, waiting for transfers between devices, per_device(): dsum = lax.all_to_all(dsum, PLANE, 0, 0, tiled=True)  16.7 us
    ppermute x1, starting transfers between devices, per_device(): other_summary = lax.ppermute(own_summary, 'zh', swap)  14.9 us
    pallas_call x1, Pallas kernels, attend(): pl.pallas_call(attend_kernel, grid=(width // step,), out_shape=(jax.Shape...  10.6 us
    ppermute x1, waiting for transfers between devices, per_device(): cross_v = lax.ppermute(cross_k[:BLK], TM, outward)  6.92 us
    all_to_all x1, starting transfers between devices, per_device(): dsum = lax.all_to_all(dsum, PLANE, 0, 0, tiled=True)  6.62 us
    ppermute x1, starting transfers between devices, per_device(): up_v = lax.ppermute(values, TM, up)  4.57 us
    ppermute x1, starting transfers between devices, per_device(): up_k = lax.ppermute(packed, TM, up)  4.56 us
  transfers between devices with their start and end apart: 14, of which 4 were waited for; matrix products, arithmetic and copies ran while one was open for 2% of the time, Pallas kernels for 1%

profile of v5, /device:TPU:32, one launch (start us, length us, event | category | flops | bytes accessed | tf_op | source)
XLA Modules:
  0.0 171.3 jit_solution(4015387919312275299)
XLA Ops:
  0.6 1.3 collective-permute-start.3
  1.9 4.6 %collective-permute-start.2 = (bf16[128,1024]{1,0:T(8,128)(2,1)}, bf16[128,1024]{1,0:T(8,128)(2,1)S(1)}, u32[]{:S(2)}, u32[]{:S(2)}) collective-permute-start(bf16[128,1024]{1,0:T(8,128)(2,1)} %bitcast.45), channel_id=1, source_target_pairs={{0,1},{1,2},{2,3},{4,5},{5,6},{6,7},{8,9},{9,10},{10,11},{12,13},{... | collective-permute-start | bytes 786440 | tf_op jit(solution)/shard_map/ppermute | solution.py:288
  7.1 1.9 %pack.1 = (bf16[136,1024]{1,0:T(8,128)(2,1)}, bf16[2,8,1024]{2,1,0:T(8,128)(2,1)S(1)}) custom-call(s32[1]{0:T(128)} %copy.22.frames, bf16[128,1024]{1,0:T(8,128)(2,1)} %bitcast.42, bf16[128,1024]{1,0:T(8,128)(2,1)} %bitcast.46, bf16[128,1024]{1,0:T(8,128)(2,1)} %bitcast.48), custom_call_target="tpu_custom_call" | custom-call | tf_op jit(solution)/shard_map/pack/pallas_call | solution.py:57
  9.1 14.9 %collective-permute-start.4 = (bf16[2,8,1024]{2,1,0:T(8,128)(2,1)S(1)}, bf16[2,8,1024]{2,1,0:T(8,128)(2,1)S(1)}, u32[]{:S(2)}, u32[]{:S(2)}) collective-permute-start(bf16[2,8,1024]{2,1,0:T(8,128)(2,1)S(1)} %get-tuple-element.46), channel_id=1, source_target_pairs={{0,4},{4,0},{1,5},{5,1},{2,6},{6,2},{3,7},{7,3},{8,12},{12,8},{9,1... | collective-permute-start | bytes 98312 | tf_op jit(solution)/shard_map/ppermute | solution.py:291
  24.1 1.2 pad_select_fusion
  25.3 0.7 collective-permute-done.4
  26.0 0.7 collective-permute-start.5
  26.7 1.3 collective-permute-start.1
  28.0 4.6 %collective-permute-start = (bf16[136,1024]{1,0:T(8,128)(2,1)S(1)}, bf16[136,1024]{1,0:T(8,128)(2,1)S(1)}, u32[]{:S(2)}, u32[]{:S(2)}) collective-permute-start(bf16[136,1024]{1,0:T(8,128)(2,1)S(1)} %copy-done.6), channel_id=1, source_target_pairs={{0,1},{1,2},{2,3},{4,5},{5,6},{6,7},{8,9},{9,10},{10,11},{12,13},{... | collective-permute-start | bytes 835592 | tf_op jit(solution)/shard_map/ppermute | solution.py:292
  32.6 36.2 %conditional.3 = (bf16[16,2,16,1024]{3,2,1,0:T(8,128)(2,1)S(1)}) conditional(s32[]{:T(128)} %convert_element_type.52, () %tuple.31, (bf16[2,8,1024]{2,1,0:T(8,128)(2,1)S(1)}, bf16[2,8,1024]{2,1,0:T(8,128)(2,1)S(1)}) %tuple.32), branch_computations={%region_0.1_spmd, %region_1.2_spmd} | conditional | flops 131072 | bytes 3342344 | solution.py:256
  32.7 36.1 %all_to_all.17 = bf16[16,2,16,1024]{3,2,1,0:T(8,128)(2,1)S(1)} all-to-all(bf16[16,2,16,1024]{3,2,1,0:T(8,128)(2,1)S(1)} %broadcast_in_dim.18), channel_id=1, replica_groups=mesh['zl'=8,'core'=2,'y'=4,'zh'=2,'x'=4] {'y','x'}, dimensions={0} | all-to-all | bytes 2097152 | tf_op jit(solution)/shard_map/cond/branch_1_fun/all_to_all | solution.py:249
  68.8 1.3 collective-permute-start.6
  70.2 6.9 %collective-permute-done.6.cross_v_ref = bf16[128,1024]{1,0:T(8,128)(2,1)S(1)} collective-permute-done((bf16[128,1024]{1,0:T(8,128)(2,1)S(1)}, bf16[128,1024]{1,0:T(8,128)(2,1)S(1)}, u32[]{:S(2)}, u32[]{:S(2)}) %collective-permute-start.6) | collective-permute-done | bytes 262176 | tf_op jit(solution)/shard_map/ppermute | solution.py:305
  77.1 0.7 copy-done.7
  77.8 10.6 %attend.1 = (bf16[128,1024]{1,0:T(8,128)(2,1)}, f32[2,128,1024]{2,1,0:T(8,128)}, bf16[2,128,1024]{2,1,0:T(8,128)(2,1)}, bf16[2,128,1024]{2,1,0:T(8,128)(2,1)}, b...) custom-call(s32[1]{0:T(128)} %copy.22.frames, s32[2]{0:T(128)} %bitcast.57, ...), custom_call_target="tpu_custom_call" | custom-call | flops 1006632960 | bytes 8388608 | tf_op jit(solution)/shard_map/attend/pallas_call | solution.py:210
  88.4 1.5 collective-permute-start.9
  89.9 4.2 %collective-permute-done.9 = bf16[128,1024]{1,0:T(8,128)(2,1)S(1)} collective-permute-done((bf16[128,1024]{1,0:T(8,128)(2,1)}, bf16[128,1024]{1,0:T(8,128)(2,1)S(1)}, u32[]{:S(2)}, u32[]{:S(2)}) %collective-permute-start.9) | collective-permute-done | bytes 262176 | tf_op jit(solution)/shard_map/ppermute | solution.py:322
  94.1 6.6 %all-to-all-start.3 = ((bf16[16,2,24,1024]{3,2,1,0:T(8,128)(2,1)}), bf16[16,2,24,1024]{3,2,1,0:T(8,128)(2,1)S(1)}, u32[]{:S(2)}, u32[]{:S(2)}) async-start(bf16[16,2,24,1024]{3,2,1,0:T(8,128)(2,1)} %get-tuple-element.59), calls=%async_computation.3 | async-start | bytes 3145728 | tf_op jit(solution)/shard_map/all_to_all | solution.py:325
  100.7 0.1 convert_reduce_fusion.1
  100.8 0.7 broadcast_select_fusion
  101.6 1.4 collective-permute-start.10
  103.0 3.8 %collective-permute-start.7 = (bf16[2,128,1024]{2,1,0:T(8,128)(2,1)}, bf16[2,128,1024]{2,1,0:T(8,128)(2,1)S(1)}, u32[]{:S(2)}, u32[]{:S(2)}) collective-permute-start(bf16[2,128,1024]{2,1,0:T(8,128)(2,1)} %get-tuple-element.53), channel_id=1, source_target_pairs={{0,1},{1,2},{2,3},{4,5},{5,6},{6,7},{8,9},{9,10},{10,11},{12,13},{... | collective-permute-start | bytes 1572872 | tf_op jit(solution)/shard_map/ppermute | solution.py:320
  106.8 1.4 collective-permute-start.8
  108.2 16.7 %all-to-all-done.3 = bf16[16,2,24,1024]{3,2,1,0:T(8,128)(2,1)S(1)} async-done(((bf16[16,2,24,1024]{3,2,1,0:T(8,128)(2,1)}), bf16[16,2,24,1024]{3,2,1,0:T(8,128)(2,1)S(1)}, u32[]{:S(2)}, u32[]{:S(2)}) %all-to-all-start.3) | async-done | bytes 1572896 | tf_op jit(solution)/shard_map/all_to_all | solution.py:325
  124.9 0.3 convert_reduce_fusion
  125.2 25.3 %conditional.4 = (f32[1,1024]{1,0:T(1,128)S(1)}) conditional(s32[]{:T(128)} %convert_element_type.52, () %tuple.35, f32[2,24,1024]{2,1,0:T(8,128)S(1)} %convert_reduce_fusion), branch_computations={%region_3.4_spmd, %region_4.6_spmd} | conditional | flops 32768 | bytes 544780 | solution.py:256
  125.3 25.1 %all_to_all.18 = f32[32,1,1024]{2,1,0:T(1,128)S(1)} all-to-all(f32[32,1,1024]{2,1,0:T(1,128)S(1)} %broadcast_in_dim.19), channel_id=1, replica_groups=mesh['zl'=8,'core'=2,'y'=4,'zh'=2,'x'=4] {'zl','core','zh'}, dimensions={0} | all-to-all | bytes 262144 | tf_op jit(solution)/shard_map/cond/branch_1_fun/all_to_all | solution.py:249
  150.5 3.6 %collective-permute-start.11 = (bf16[2,8,1024]{2,1,0:T(8,128)(2,1)S(1)}, bf16[2,8,1024]{2,1,0:T(8,128)(2,1)S(1)}, u32[]{:S(2)}, u32[]{:S(2)}) collective-permute-start(bf16[2,8,1024]{2,1,0:T(8,128)(2,1)S(1)} %slice.76), channel_id=1, source_target_pairs={{0,4},{4,0},{1,5},{5,1},{2,6},{6,2},{3,7},{7,3},{8,12},{12,8},{9,1... | collective-permute-start | bytes 98312 | tf_op jit(solution)/shard_map/ppermute | solution.py:334
  154.2 1.3 collective-permute-start.12
  155.5 13.4 %conditional.5 = (f32[9,1024]{1,0:T(8,128)S(1)}) conditional(s32[]{:T(128)} %convert_element_type.52, () %tuple.37, f32[1,1024]{1,0:T(1,128)S(1)} %get-tuple-element.68), branch_computations={%region_7.8_spmd, %region_8.9_spmd} | conditional | bytes 348168 | solution.py:256
  155.6 13.3 %all_to_all.19 = f32[16,1,1024]{2,1,0:T(1,128)S(1)} all-to-all(f32[16,1,1024]{2,1,0:T(1,128)S(1)} %broadcast_in_dim.25), channel_id=1, replica_groups=mesh['zl'=8,'core'=2,'y'=4,'zh'=2,'x'=4] {'y','x'}, dimensions={0} | all-to-all | bytes 131072 | tf_op jit(solution)/shard_map/cond/branch_1_fun/all_to_all | solution.py:249
  169.0 2.3 %fusion.1 = (bf16[128,1024]{1,0:T(8,128)(2,1)}, bf16[128,1024]{1,0:T(8,128)(2,1)}) fusion(bf16[128,1024]{1,0:T(8,128)(2,1)S(1)} %collective-permute-done.12, f32[2,128,1024]{2,1,0:T(8,128)S(1)} %copy-done.3, bf16[2,128,1024]{2,1,0:T(8,128)(2,1)} %collective-permute-done.8, bf16[2,128,1024]{2,1,0:T(8,128)(2,1)S(1)} %collective-permute-done.7, ...), kind=kLoop, calls=%fused_computation.6 | loop fusion | flops 2621440 | bytes 3211777 | tf_op jit(solution)/shard_map/convert_element_type | solution.py:345
  (45 shorter events, 0.7 us)
Async XLA Ops:
  0.6 23.4 %collective-permute-start.3 = (bf16[128,1024]{1,0:T(8,128)(2,1)}, bf16[128,1024]{1,0:T(8,128)(2,1)S(1)}, u32[]{:S(2)}, u32[]{:S(2)}) collective-permute-start(bf16[128,1024]{1,0:T(8,128)(2,1)} %bitcast.44), channel_id=1, source_target_pairs={{1,0},{2,1},{3,2},{5,4},{6,5},{7,6},{9,8},{10,9},{11,10},{13,12},{... | collective-permute-start | bytes 786440 | tf_op jit(solution)/shard_map/ppermute | solution.py:289
  1.9 22.1 %collective-permute-start.2 = (bf16[128,1024]{1,0:T(8,128)(2,1)}, bf16[128,1024]{1,0:T(8,128)(2,1)S(1)}, u32[]{:S(2)}, u32[]{:S(2)}) collective-permute-start(bf16[128,1024]{1,0:T(8,128)(2,1)} %bitcast.45), channel_id=1, source_target_pairs={{0,1},{1,2},{2,3},{4,5},{5,6},{6,7},{8,9},{9,10},{10,11},{12,13},{... | collective-permute-start | bytes 786440 | tf_op jit(solution)/shard_map/ppermute | solution.py:288
  9.1 17.6 %copy-start.6 = (bf16[136,1024]{1,0:T(8,128)(2,1)S(1)}, bf16[136,1024]{1,0:T(8,128)(2,1)}, u32[]{:S(2)}) copy-start(bf16[136,1024]{1,0:T(8,128)(2,1)} %get-tuple-element.45) | copy-start | bytes 835588
  9.1 16.9 %collective-permute-start.4 = (bf16[2,8,1024]{2,1,0:T(8,128)(2,1)S(1)}, bf16[2,8,1024]{2,1,0:T(8,128)(2,1)S(1)}, u32[]{:S(2)}, u32[]{:S(2)}) collective-permute-start(bf16[2,8,1024]{2,1,0:T(8,128)(2,1)S(1)} %get-tuple-element.46), channel_id=1, source_target_pairs={{0,4},{4,0},{1,5},{5,1},{2,6},{6,2},{3,7},{7,3},{8,12},{12,8},{9,1... | collective-permute-start | bytes 98312 | tf_op jit(solution)/shard_map/ppermute | solution.py:291
  24.0 8.5 %copy-start.4 = (bf16[128,1024]{1,0:T(8,128)(2,1)}, bf16[128,1024]{1,0:T(8,128)(2,1)S(1)}, u32[]{:S(2)}) copy-start(bf16[128,1024]{1,0:T(8,128)(2,1)S(1)} %collective-permute-done.3.down_v_ref) | copy-start | bytes 786436
  24.1 8.5 %copy-start.5 = (bf16[128,1024]{1,0:T(8,128)(2,1)}, bf16[128,1024]{1,0:T(8,128)(2,1)S(1)}, u32[]{:S(2)}) copy-start(bf16[128,1024]{1,0:T(8,128)(2,1)S(1)} %collective-permute-done.2.up_v_ref) | copy-start | bytes 786436
  26.0 42.8 %collective-permute-start.5 = (bf16[136,1024]{1,0:T(8,128)(2,1)S(1)}, bf16[136,1024]{1,0:T(8,128)(2,1)S(1)}, u32[]{:S(2)}, u32[]{:S(2)}) collective-permute-start(bf16[136,1024]{1,0:T(8,128)(2,1)S(1)} %pad_select_fusion), channel_id=1, source_target_pairs={{3,4},{4,3},{2,5},{5,2},{7,8},{8,7},{6,9},{9,6},{11,12},{12,11},{1... | collective-permute-start | bytes 835592 | tf_op jit(solution)/shard_map/ppermute | solution.py:297
  26.7 43.4 %collective-permute-start.1 = (bf16[136,1024]{1,0:T(8,128)(2,1)S(1)}, bf16[136,1024]{1,0:T(8,128)(2,1)S(1)}, u32[]{:S(2)}, u32[]{:S(2)}) collective-permute-start(bf16[136,1024]{1,0:T(8,128)(2,1)S(1)} %copy-done.6), channel_id=1, source_target_pairs={{1,0},{2,1},{3,2},{5,4},{6,5},{7,6},{9,8},{10,9},{11,10},{13,12},{... | collective-permute-start | bytes 835592 | tf_op jit(solution)/shard_map/ppermute | solution.py:293
  28.0 42.2 %collective-permute-start = (bf16[136,1024]{1,0:T(8,128)(2,1)S(1)}, bf16[136,1024]{1,0:T(8,128)(2,1)S(1)}, u32[]{:S(2)}, u32[]{:S(2)}) collective-permute-start(bf16[136,1024]{1,0:T(8,128)(2,1)S(1)} %copy-done.6), channel_id=1, source_target_pairs={{0,1},{1,2},{2,3},{4,5},{5,6},{6,7},{8,9},{9,10},{10,11},{12,13},{... | collective-permute-start | bytes 835592 | tf_op jit(solution)/shard_map/ppermute | solution.py:292
  68.8 8.3 %copy-start = (bf16[136,1024]{1,0:T(8,128)(2,1)}, bf16[136,1024]{1,0:T(8,128)(2,1)S(1)}, u32[]{:S(2)}) copy-start(bf16[136,1024]{1,0:T(8,128)(2,1)S(1)} %collective-permute-done.5.cross_k_ref.cross_go_ref) | copy-start | bytes 835588
  68.8 8.3 %collective-permute-start.6 = (bf16[128,1024]{1,0:T(8,128)(2,1)S(1)}, bf16[128,1024]{1,0:T(8,128)(2,1)S(1)}, u32[]{:S(2)}, u32[]{:S(2)}) collective-permute-start(bf16[128,1024]{1,0:T(8,128)(2,1)S(1)} %slice.45), channel_id=1, source_target_pairs={{2,3},{1,0},{6,7},{5,4},{10,11},{9,8},{14,15},{13,12},{18,19},{17,... | collective-permute-start | bytes 786440 | tf_op jit(solution)/shard_map/ppermute | solution.py:305
  70.1 7.0 %copy-start.1 = (bf16[136,1024]{1,0:T(8,128)(2,1)}, bf16[136,1024]{1,0:T(8,128)(2,1)S(1)}, u32[]{:S(2)}) copy-start(bf16[136,1024]{1,0:T(8,128)(2,1)S(1)} %collective-permute-done.1.down_k_ref.down_go_ref) | copy-start | bytes 835588
  70.2 6.9 %copy-start.2 = (bf16[136,1024]{1,0:T(8,128)(2,1)}, bf16[136,1024]{1,0:T(8,128)(2,1)S(1)}, u32[]{:S(2)}) copy-start(bf16[136,1024]{1,0:T(8,128)(2,1)S(1)} %collective-permute-done.up_k_ref.up_go_ref) | copy-start | bytes 835588
  77.1 0.7 copy-start.7
  88.4 5.6 %collective-permute-start.9 = (bf16[128,1024]{1,0:T(8,128)(2,1)}, bf16[128,1024]{1,0:T(8,128)(2,1)S(1)}, u32[]{:S(2)}, u32[]{:S(2)}) collective-permute-start(bf16[128,1024]{1,0:T(8,128)(2,1)} %get-tuple-element.56), channel_id=1, source_target_pairs={{3,2},{0,1},{7,6},{4,5},{11,10},{8,9},{15,14},{12,13},{19,18},{16,... | collective-permute-start | bytes 786440 | tf_op jit(solution)/shard_map/ppermute | solution.py:322
  94.1 6.8 %copy-start.8 = (bf16[128,1024]{1,0:T(8,128)(2,1)S(1)}, bf16[128,1024]{1,0:T(8,128)(2,1)}, u32[]{:S(2)}) copy-start(bf16[128,1024]{1,0:T(8,128)(2,1)} %get-tuple-element.55) | copy-start | bytes 786436
  94.1 30.8 %all-to-all-start.3 = ((bf16[16,2,24,1024]{3,2,1,0:T(8,128)(2,1)}), bf16[16,2,24,1024]{3,2,1,0:T(8,128)(2,1)S(1)}, u32[]{:S(2)}, u32[]{:S(2)}) async-start(bf16[16,2,24,1024]{3,2,1,0:T(8,128)(2,1)} %get-tuple-element.59), calls=%async_computation.3 | async-start | bytes 3145728 | tf_op jit(solution)/shard_map/all_to_all | solution.py:325
  101.6 48.9 %collective-permute-start.10 = (bf16[128,1024]{1,0:T(8,128)(2,1)}, bf16[128,1024]{1,0:T(8,128)(2,1)}, u32[]{:S(2)}, u32[]{:S(2)}) collective-permute-start(bf16[128,1024]{1,0:T(8,128)(2,1)} %broadcast_select_fusion), channel_id=1, source_target_pairs={{3,4},{4,3},{2,5},{5,2},{7,8},{8,7},{6,9},{9,6},{11,12},{12,11},{1... | collective-permute-start | bytes 786440 | tf_op jit(solution)/shard_map/ppermute | solution.py:328
  103.0 66.0 %collective-permute-start.7 = (bf16[2,128,1024]{2,1,0:T(8,128)(2,1)}, bf16[2,128,1024]{2,1,0:T(8,128)(2,1)S(1)}, u32[]{:S(2)}, u32[]{:S(2)}) collective-permute-start(bf16[2,128,1024]{2,1,0:T(8,128)(2,1)} %get-tuple-element.53), channel_id=1, source_target_pairs={{0,1},{1,2},{2,3},{4,5},{5,6},{6,7},{8,9},{9,10},{10,11},{12,13},{... | collective-permute-start | bytes 1572872 | tf_op jit(solution)/shard_map/ppermute | solution.py:320
  106.8 62.2 %copy-start.3 = (f32[2,128,1024]{2,1,0:T(8,128)S(1)}, f32[2,128,1024]{2,1,0:T(8,128)}, u32[]{:S(2)}) copy-start(f32[2,128,1024]{2,1,0:T(8,128)} %get-tuple-element.52) | copy-start | bytes 3145732
  106.8 62.2 %collective-permute-start.8 = (bf16[2,128,1024]{2,1,0:T(8,128)(2,1)}, bf16[2,128,1024]{2,1,0:T(8,128)(2,1)}, u32[]{:S(2)}, u32[]{:S(2)}) collective-permute-start(bf16[2,128,1024]{2,1,0:T(8,128)(2,1)} %get-tuple-element.54), channel_id=1, source_target_pairs={{1,0},{2,1},{3,2},{5,4},{6,5},{7,6},{9,8},{10,9},{11,10},{13,12},{... | collective-permute-start | bytes 1572872 | tf_op jit(solution)/shard_map/ppermute | solution.py:321
  150.5 18.4 %collective-permute-start.11 = (bf16[2,8,1024]{2,1,0:T(8,128)(2,1)S(1)}, bf16[2,8,1024]{2,1,0:T(8,128)(2,1)S(1)}, u32[]{:S(2)}, u32[]{:S(2)}) collective-permute-start(bf16[2,8,1024]{2,1,0:T(8,128)(2,1)S(1)} %slice.76), channel_id=1, source_target_pairs={{0,4},{4,0},{1,5},{5,1},{2,6},{6,2},{3,7},{7,3},{8,12},{12,8},{9,1... | collective-permute-start | bytes 98312 | tf_op jit(solution)/shard_map/ppermute | solution.py:334
  154.2 14.8 %collective-permute-start.12 = (bf16[128,1024]{1,0:T(8,128)(2,1)}, bf16[128,1024]{1,0:T(8,128)(2,1)S(1)}, u32[]{:S(2)}, u32[]{:S(2)}) collective-permute-start(bf16[128,1024]{1,0:T(8,128)(2,1)} %collective-permute-done.10), channel_id=1, source_target_pairs={{2,3},{1,0},{6,7},{5,4},{10,11},{9,8},{14,15},{13,12},{18,19},{17,... | collective-permute-start | bytes 786440 | tf_op jit(solution)/shard_map/ppermute | solution.py:332
  168.9 2.4 %copy-start.9 = (f32[9,1024]{1,0:T(8,128)}, f32[9,1024]{1,0:T(8,128)S(1)}, u32[]{:S(2)}) copy-start(f32[9,1024]{1,0:T(8,128)S(1)} %get-tuple-element.69) | copy-start | bytes 110596

commit v6 on v4

--- a/solution.py
+++ b/solution.py
@@ -165,14 +165,12 @@
         weight = jnp.exp(scores - top)
         prob = weight * (1.0 / jnp.sum(weight, axis=0, keepdims=True))
         prob_bf = prob.astype(jnp.bfloat16)
-        attn = dot(prob_bf, values, TN).astype(jnp.bfloat16).astype(jnp.float32)
-        delta = jnp.sum(
-            (grad_attn.astype(jnp.float32) * attn).T, axis=0, keepdims=True
-        )
+        attn = dot(values, prob_bf, TN).T.astype(jnp.bfloat16).astype(jnp.float32)
         dprob = dot(values, grad_attn, NT)
+        delta = jnp.sum(prob * dprob, axis=0, keepdims=True)
         dscore = (prob * (dprob - delta)).astype(jnp.bfloat16)
 
-        dq_ref[:, c] = (dot(dscore, keys, TN) * SCALE).astype(jnp.bfloat16)
+        dq_ref[:, c] = (dot(keys, dscore, TN).T * SCALE).astype(jnp.bfloat16)
         for side, part, cross_ref in (
             (0, dot(dscore, queries, NN) * SCALE, cross_dk_ref),
             (1, dot(prob_bf, grad_attn, NN), cross_dv_ref),

time: 172 us -> 170 us (0.988)
  Pallas kernels: 12.6 us -> 10.3 us
    pallas_call x1, Pallas kernels: 10.6 us -> 8.36 us  [attend(): pl.pallas_call(attend_kernel, grid=(width // step,), out_shape=(jax.Shape...]
where the time goes in v6:
time: 170 us; the launch traced here: 169 us
  starting transfers between devices  76.9 us (45%)
  blocking collectives  51.2 us (30%)
  waiting for transfers between devices  22 us (13%)
  Pallas kernels  10.3 us (6%)
  other arithmetic  4.82 us (3%)
  local copies, waits for them, and re-layouts  2.35 us (1%)
    all_to_all x2, blocking collectives, spread(): lax.all_to_all(jnp.broadcast_to(block[None], (count,) + block.shape), axe...  51.2 us
    ppermute x1, starting transfers between devices, per_device(): other_summary = lax.ppermute(own_summary, 'zh', swap)  14.9 us
    ppermute x1, starting transfers between devices, per_device(): cross_k = lax.ppermute(crossing, TM, diagonal)  14.5 us
    ppermute x1, starting transfers between devices, per_device(): cross_dk = lax.ppermute(jnp.where(edge, cross_dk, relay), TM, diagonal)  9.19 us
    pallas_call x1, Pallas kernels, attend(): pl.pallas_call(attend_kernel, grid=(width // step,), out_shape=(jax.Shape...  8.36 us
    all_to_all x1, starting transfers between devices, per_device(): dsum = lax.all_to_all(dsum, PLANE, 0, 0, tiled=True)  8.18 us
    ppermute x1, waiting for transfers between devices, per_device(): cross_v = lax.ppermute(cross_k[:BLK], TM, outward)  7.33 us
    all_to_all x1, starting transfers between devices, spread(): lax.all_to_all(jnp.broadcast_to(block[None], (count,) + block.shape), axe...  7.08 us
  transfers between devices with their start and end apart: 15, of which 7 were waited for; matrix products, arithmetic and copies ran while one was open for 2% of the time, Pallas kernels for 1%

profile of v6, /device:TPU:38, one launch (start us, length us, event | category | flops | bytes accessed | tf_op | source)
XLA Modules:
  0.0 169.1 jit_solution(17718799846239449508)
XLA Ops:
  0.6 2.8 %collective-permute-start.3 = (bf16[128,1024]{1,0:T(8,128)(2,1)}, bf16[128,1024]{1,0:T(8,128)(2,1)S(1)}, u32[]{:S(2)}, u32[]{:S(2)}) collective-permute-start(bf16[128,1024]{1,0:T(8,128)(2,1)} %bitcast.44), channel_id=1, source_target_pairs={{1,0},{2,1},{3,2},{5,4},{6,5},{7,6},{9,8},{10,9},{11,10},{13,12},{... | collective-permute-start | bytes 786440 | tf_op jit(solution)/shard_map/ppermute | solution.py:287
  3.4 1.3 collective-permute-start.2
  5.3 1.9 %pack.1 = (bf16[136,1024]{1,0:T(8,128)(2,1)}, bf16[2,8,1024]{2,1,0:T(8,128)(2,1)S(1)}) custom-call(s32[1]{0:T(128)} %copy.20.frames, bf16[128,1024]{1,0:T(8,128)(2,1)} %bitcast.42, bf16[128,1024]{1,0:T(8,128)(2,1)} %bitcast.46, bf16[128,1024]{1,0:T(8,128)(2,1)} %bitcast.48), custom_call_target="tpu_custom_call" | custom-call | tf_op jit(solution)/shard_map/pack/pallas_call | solution.py:57
  7.3 14.9 %collective-permute-start.4 = (bf16[2,8,1024]{2,1,0:T(8,128)(2,1)S(1)}, bf16[2,8,1024]{2,1,0:T(8,128)(2,1)S(1)}, u32[]{:S(2)}, u32[]{:S(2)}) collective-permute-start(bf16[2,8,1024]{2,1,0:T(8,128)(2,1)S(1)} %get-tuple-element.42), channel_id=1, source_target_pairs={{0,4},{4,0},{1,5},{5,1},{2,6},{6,2},{3,7},{7,3},{8,12},{12,8},{9,1... | collective-permute-start | bytes 98312 | tf_op jit(solution)/shard_map/ppermute | solution.py:289
  22.3 1.2 pad_select_fusion
  23.5 0.8 collective-permute-done.4
  24.3 14.5 %collective-permute-start.5 = (bf16[136,1024]{1,0:T(8,128)(2,1)S(1)}, bf16[136,1024]{1,0:T(8,128)(2,1)S(1)}, u32[]{:S(2)}, u32[]{:S(2)}) collective-permute-start(bf16[136,1024]{1,0:T(8,128)(2,1)S(1)} %pad_select_fusion), channel_id=1, source_target_pairs={{3,4},{4,3},{2,5},{5,2},{7,8},{8,7},{6,9},{9,6},{11,12},{12,11},{1... | collective-permute-start | bytes 835592 | tf_op jit(solution)/shard_map/ppermute | solution.py:295
  38.8 2.8 %collective-permute-start.1 = (bf16[136,1024]{1,0:T(8,128)(2,1)S(1)}, bf16[136,1024]{1,0:T(8,128)(2,1)S(1)}, u32[]{:S(2)}, u32[]{:S(2)}) collective-permute-start(bf16[136,1024]{1,0:T(8,128)(2,1)S(1)} %copy-done.6), channel_id=1, source_target_pairs={{1,0},{2,1},{3,2},{5,4},{6,5},{7,6},{9,8},{10,9},{11,10},{13,12},{... | collective-permute-start | bytes 835592 | tf_op jit(solution)/shard_map/ppermute | solution.py:291
  41.6 1.3 collective-permute-start
  42.9 24.3 %conditional.2 = (bf16[16,2,16,1024]{3,2,1,0:T(8,128)(2,1)S(1)}) conditional(s32[]{:T(128)} %convert_element_type.51, () %tuple.25, (bf16[2,8,1024]{2,1,0:T(8,128)(2,1)S(1)}, bf16[2,8,1024]{2,1,0:T(8,128)(2,1)S(1)}) %tuple.26), branch_computations={%region_0.1_spmd, %region_1.2_spmd} | conditional | flops 131072 | bytes 3342344 | solution.py:254
  43.1 24.1 %all_to_all.18 = bf16[16,2,16,1024]{3,2,1,0:T(8,128)(2,1)S(1)} all-to-all(bf16[16,2,16,1024]{3,2,1,0:T(8,128)(2,1)S(1)} %broadcast_in_dim.18), channel_id=1, replica_groups=mesh['zl'=8,'core'=2,'y'=4,'zh'=2,'x'=4] {'y','x'}, dimensions={0} | all-to-all | bytes 2097152 | tf_op jit(solution)/shard_map/cond/branch_1_fun/all_to_all | solution.py:247
  67.2 1.3 collective-permute-start.6
  68.6 7.3 %collective-permute-done.6.cross_v_ref = bf16[128,1024]{1,0:T(8,128)(2,1)S(1)} collective-permute-done((bf16[128,1024]{1,0:T(8,128)(2,1)S(1)}, bf16[128,1024]{1,0:T(8,128)(2,1)S(1)}, u32[]{:S(2)}, u32[]{:S(2)}) %collective-permute-start.6) | collective-permute-done | bytes 262176 | tf_op jit(solution)/shard_map/ppermute | solution.py:303
  75.9 0.7 copy-done.7
  76.6 8.4 %attend.1 = (bf16[128,1024]{1,0:T(8,128)(2,1)}, f32[2,128,1024]{2,1,0:T(8,128)}, bf16[2,128,1024]{2,1,0:T(8,128)(2,1)}, bf16[2,128,1024]{2,1,0:T(8,128)(2,1)}, b...) custom-call(s32[1]{0:T(128)} %copy.20.frames, s32[2]{0:T(128)} %bitcast.57, ...), custom_call_target="tpu_custom_call" | custom-call | flops 1006632960 | bytes 8388608 | tf_op jit(solution)/shard_map/attend/pallas_call | solution.py:208
  85.0 1.5 collective-permute-start.9
  86.4 4.2 %collective-permute-done.9 = bf16[128,1024]{1,0:T(8,128)(2,1)S(1)} collective-permute-done((bf16[128,1024]{1,0:T(8,128)(2,1)}, bf16[128,1024]{1,0:T(8,128)(2,1)S(1)}, u32[]{:S(2)}, u32[]{:S(2)}) %collective-permute-start.9) | collective-permute-done | bytes 262176 | tf_op jit(solution)/shard_map/ppermute | solution.py:320
  90.6 8.2 %all-to-all-start.2 = ((bf16[16,2,24,1024]{3,2,1,0:T(8,128)(2,1)}), bf16[16,2,24,1024]{3,2,1,0:T(8,128)(2,1)S(1)}, u32[]{:S(2)}, u32[]{:S(2)}) async-start(bf16[16,2,24,1024]{3,2,1,0:T(8,128)(2,1)} %get-tuple-element.55), calls=%async_computation.2 | async-start | bytes 3145728 | tf_op jit(solution)/shard_map/all_to_all | solution.py:323
  98.9 0.7 broadcast_select_fusion
  99.7 9.2 %collective-permute-start.10 = (bf16[128,1024]{1,0:T(8,128)(2,1)}, bf16[128,1024]{1,0:T(8,128)(2,1)}, u32[]{:S(2)}, u32[]{:S(2)}) collective-permute-start(bf16[128,1024]{1,0:T(8,128)(2,1)} %broadcast_select_fusion), channel_id=1, source_target_pairs={{3,4},{4,3},{2,5},{5,2},{7,8},{8,7},{6,9},{9,6},{11,12},{12,11},{1... | collective-permute-start | bytes 786440 | tf_op jit(solution)/shard_map/ppermute | solution.py:326
  108.9 1.3 collective-permute-start.7
  110.2 5.3 %collective-permute-start.8 = (bf16[2,128,1024]{2,1,0:T(8,128)(2,1)}, bf16[2,128,1024]{2,1,0:T(8,128)(2,1)}, u32[]{:S(2)}, u32[]{:S(2)}) collective-permute-start(bf16[2,128,1024]{2,1,0:T(8,128)(2,1)} %get-tuple-element.50), channel_id=1, source_target_pairs={{1,0},{2,1},{3,2},{5,4},{6,5},{7,6},{9,8},{10,9},{11,10},{13,12},{... | collective-permute-start | bytes 1572872 | tf_op jit(solution)/shard_map/ppermute | solution.py:319
  115.5 1.6 all-to-all-done.2
  117.4 27.2 %conditional.3 = (f32[1,1024]{1,0:T(1,128)S(1)}) conditional(s32[]{:T(128)} %convert_element_type.51, () %tuple.29, f32[2,24,1024]{2,1,0:T(8,128)S(1)} %convert_reduce_fusion), branch_computations={%region_3.4_spmd, %region_4.6_spmd} | conditional | flops 32768 | bytes 544780 | solution.py:254
  117.5 27.0 %all_to_all.19 = f32[32,1,1024]{2,1,0:T(1,128)S(1)} all-to-all(f32[32,1,1024]{2,1,0:T(1,128)S(1)} %broadcast_in_dim.19), channel_id=1, replica_groups=mesh['zl'=8,'core'=2,'y'=4,'zh'=2,'x'=4] {'zl','core','zh'}, dimensions={0} | all-to-all | bytes 262144 | tf_op jit(solution)/shard_map/cond/branch_1_fun/all_to_all | solution.py:247
  144.7 4.3 %collective-permute-start.11 = (bf16[2,8,1024]{2,1,0:T(8,128)(2,1)S(1)}, bf16[2,8,1024]{2,1,0:T(8,128)(2,1)S(1)}, u32[]{:S(2)}, u32[]{:S(2)}) collective-permute-start(bf16[2,8,1024]{2,1,0:T(8,128)(2,1)S(1)} %slice.77), channel_id=1, source_target_pairs={{0,4},{4,0},{1,5},{5,1},{2,6},{6,2},{3,7},{7,3},{8,12},{12,8},{9,1... | collective-permute-start | bytes 98312 | tf_op jit(solution)/shard_map/ppermute | solution.py:332
  149.8 7.1 %all-to-all-start.3 = ((f32[16,1,1024]{2,1,0:T(1,128)}), f32[16,1,1024]{2,1,0:T(1,128)S(1)}, u32[]{:S(2)}, u32[]{:S(2)}) async-start(f32[16,1,1024]{2,1,0:T(1,128)} %broadcast_in_dim.42), calls=%async_computation.3 | async-start | bytes 131072 | tf_op jit(solution)/shard_map/all_to_all | solution.py:247
  156.9 1.3 collective-permute-start.12
  158.2 1.6 collective-permute-done.11
  159.8 2.8 %all-to-all-done.3 = f32[16,1,1024]{2,1,0:T(1,128)S(1)} async-done(((f32[16,1,1024]{2,1,0:T(1,128)}), f32[16,1,1024]{2,1,0:T(1,128)S(1)}, u32[]{:S(2)}, u32[]{:S(2)}) %all-to-all-start.3) | async-done | bytes 65568 | tf_op jit(solution)/shard_map/all_to_all | solution.py:247
  163.2 3.6 %collective-permute-done.12 = bf16[128,1024]{1,0:T(8,128)(2,1)S(1)} collective-permute-done((bf16[128,1024]{1,0:T(8,128)(2,1)}, bf16[128,1024]{1,0:T(8,128)(2,1)S(1)}, u32[]{:S(2)}, u32[]{:S(2)}) %collective-permute-start.12) | collective-permute-done | bytes 262176 | tf_op jit(solution)/shard_map/ppermute | solution.py:330
  166.8 2.3 %fusion.1 = (bf16[128,1024]{1,0:T(8,128)(2,1)}, bf16[128,1024]{1,0:T(8,128)(2,1)}) fusion(bf16[128,1024]{1,0:T(8,128)(2,1)S(1)} %collective-permute-done.12, f32[2,128,1024]{2,1,0:T(8,128)S(1)} %copy-done.3, bf16[2,128,1024]{2,1,0:T(8,128)(2,1)} %collective-permute-done.8, bf16[2,128,1024]{2,1,0:T(8,128)(2,1)S(1)} %collective-permute-done.7, ...), kind=kLoop, calls=%fused_computation.5 | loop fusion | flops 2621440 | bytes 3211777 | tf_op jit(solution)/shard_map/convert_element_type | solution.py:343
  (43 shorter events, 2.3 us)
Async XLA Ops:
  0.6 21.6 %collective-permute-start.3 = (bf16[128,1024]{1,0:T(8,128)(2,1)}, bf16[128,1024]{1,0:T(8,128)(2,1)S(1)}, u32[]{:S(2)}, u32[]{:S(2)}) collective-permute-start(bf16[128,1024]{1,0:T(8,128)(2,1)} %bitcast.44), channel_id=1, source_target_pairs={{1,0},{2,1},{3,2},{5,4},{6,5},{7,6},{9,8},{10,9},{11,10},{13,12},{... | collective-permute-start | bytes 786440 | tf_op jit(solution)/shard_map/ppermute | solution.py:287
  3.4 18.9 %collective-permute-start.2 = (bf16[128,1024]{1,0:T(8,128)(2,1)}, bf16[128,1024]{1,0:T(8,128)(2,1)S(1)}, u32[]{:S(2)}, u32[]{:S(2)}) collective-permute-start(bf16[128,1024]{1,0:T(8,128)(2,1)} %bitcast.45), channel_id=1, source_target_pairs={{0,1},{1,2},{2,3},{4,5},{5,6},{6,7},{8,9},{9,10},{10,11},{12,13},{... | collective-permute-start | bytes 786440 | tf_op jit(solution)/shard_map/ppermute | solution.py:286
  7.2 31.5 %copy-start.6 = (bf16[136,1024]{1,0:T(8,128)(2,1)S(1)}, bf16[136,1024]{1,0:T(8,128)(2,1)}, u32[]{:S(2)}) copy-start(bf16[136,1024]{1,0:T(8,128)(2,1)} %get-tuple-element.41) | copy-start | bytes 835588
  7.3 17.1 %collective-permute-start.4 = (bf16[2,8,1024]{2,1,0:T(8,128)(2,1)S(1)}, bf16[2,8,1024]{2,1,0:T(8,128)(2,1)S(1)}, u32[]{:S(2)}, u32[]{:S(2)}) collective-permute-start(bf16[2,8,1024]{2,1,0:T(8,128)(2,1)S(1)} %get-tuple-element.42), channel_id=1, source_target_pairs={{0,4},{4,0},{1,5},{5,1},{2,6},{6,2},{3,7},{7,3},{8,12},{12,8},{9,1... | collective-permute-start | bytes 98312 | tf_op jit(solution)/shard_map/ppermute | solution.py:289
  22.2 20.7 %copy-start.4 = (bf16[128,1024]{1,0:T(8,128)(2,1)}, bf16[128,1024]{1,0:T(8,128)(2,1)S(1)}, u32[]{:S(2)}) copy-start(bf16[128,1024]{1,0:T(8,128)(2,1)S(1)} %collective-permute-done.3.down_v_ref) | copy-start | bytes 786436
  22.2 20.7 %copy-start.5 = (bf16[128,1024]{1,0:T(8,128)(2,1)}, bf16[128,1024]{1,0:T(8,128)(2,1)S(1)}, u32[]{:S(2)}) copy-start(bf16[128,1024]{1,0:T(8,128)(2,1)S(1)} %collective-permute-done.2.up_v_ref) | copy-start | bytes 786436
  24.3 42.9 %collective-permute-start.5 = (bf16[136,1024]{1,0:T(8,128)(2,1)S(1)}, bf16[136,1024]{1,0:T(8,128)(2,1)S(1)}, u32[]{:S(2)}, u32[]{:S(2)}) collective-permute-start(bf16[136,1024]{1,0:T(8,128)(2,1)S(1)} %pad_select_fusion), channel_id=1, source_target_pairs={{3,4},{4,3},{2,5},{5,2},{7,8},{8,7},{6,9},{9,6},{11,12},{12,11},{1... | collective-permute-start | bytes 835592 | tf_op jit(solution)/shard_map/ppermute | solution.py:295
  38.8 29.7 %collective-permute-start.1 = (bf16[136,1024]{1,0:T(8,128)(2,1)S(1)}, bf16[136,1024]{1,0:T(8,128)(2,1)S(1)}, u32[]{:S(2)}, u32[]{:S(2)}) collective-permute-start(bf16[136,1024]{1,0:T(8,128)(2,1)S(1)} %copy-done.6), channel_id=1, source_target_pairs={{1,0},{2,1},{3,2},{5,4},{6,5},{7,6},{9,8},{10,9},{11,10},{13,12},{... | collective-permute-start | bytes 835592 | tf_op jit(solution)/shard_map/ppermute | solution.py:291
  41.6 27.0 %collective-permute-start = (bf16[136,1024]{1,0:T(8,128)(2,1)S(1)}, bf16[136,1024]{1,0:T(8,128)(2,1)S(1)}, u32[]{:S(2)}, u32[]{:S(2)}) collective-permute-start(bf16[136,1024]{1,0:T(8,128)(2,1)S(1)} %copy-done.6), channel_id=1, source_target_pairs={{0,1},{1,2},{2,3},{4,5},{5,6},{6,7},{8,9},{9,10},{10,11},{12,13},{... | collective-permute-start | bytes 835592 | tf_op jit(solution)/shard_map/ppermute | solution.py:290
  67.2 8.7 %copy-start = (bf16[136,1024]{1,0:T(8,128)(2,1)}, bf16[136,1024]{1,0:T(8,128)(2,1)S(1)}, u32[]{:S(2)}) copy-start(bf16[136,1024]{1,0:T(8,128)(2,1)S(1)} %collective-permute-done.5.cross_k_ref.cross_go_ref) | copy-start | bytes 835588
  67.2 8.7 %collective-permute-start.6 = (bf16[128,1024]{1,0:T(8,128)(2,1)S(1)}, bf16[128,1024]{1,0:T(8,128)(2,1)S(1)}, u32[]{:S(2)}, u32[]{:S(2)}) collective-permute-start(bf16[128,1024]{1,0:T(8,128)(2,1)S(1)} %slice.45), channel_id=1, source_target_pairs={{2,3},{1,0},{6,7},{5,4},{10,11},{9,8},{14,15},{13,12},{18,19},{17,... | collective-permute-start | bytes 786440 | tf_op jit(solution)/shard_map/ppermute | solution.py:303
  68.5 7.4 %copy-start.1 = (bf16[136,1024]{1,0:T(8,128)(2,1)}, bf16[136,1024]{1,0:T(8,128)(2,1)S(1)}, u32[]{:S(2)}) copy-start(bf16[136,1024]{1,0:T(8,128)(2,1)S(1)} %collective-permute-done.1.down_k_ref.down_go_ref) | copy-start | bytes 835588
  68.6 7.4 %copy-start.2 = (bf16[136,1024]{1,0:T(8,128)(2,1)}, bf16[136,1024]{1,0:T(8,128)(2,1)S(1)}, u32[]{:S(2)}) copy-start(bf16[136,1024]{1,0:T(8,128)(2,1)S(1)} %collective-permute-done.up_k_ref.up_go_ref) | copy-start | bytes 835588
  75.9 0.7 copy-start.7
  85.0 5.7 %collective-permute-start.9 = (bf16[128,1024]{1,0:T(8,128)(2,1)}, bf16[128,1024]{1,0:T(8,128)(2,1)S(1)}, u32[]{:S(2)}, u32[]{:S(2)}) collective-permute-start(bf16[128,1024]{1,0:T(8,128)(2,1)} %get-tuple-element.52), channel_id=1, source_target_pairs={{3,2},{0,1},{7,6},{4,5},{11,10},{8,9},{15,14},{12,13},{19,18},{16,... | collective-permute-start | bytes 786440 | tf_op jit(solution)/shard_map/ppermute | solution.py:320
  90.6 8.3 %copy-start.8 = (bf16[128,1024]{1,0:T(8,128)(2,1)S(1)}, bf16[128,1024]{1,0:T(8,128)(2,1)}, u32[]{:S(2)}) copy-start(bf16[128,1024]{1,0:T(8,128)(2,1)} %get-tuple-element.51) | copy-start | bytes 786436
  90.6 26.5 %all-to-all-start.2 = ((bf16[16,2,24,1024]{3,2,1,0:T(8,128)(2,1)}), bf16[16,2,24,1024]{3,2,1,0:T(8,128)(2,1)S(1)}, u32[]{:S(2)}, u32[]{:S(2)}) async-start(bf16[16,2,24,1024]{3,2,1,0:T(8,128)(2,1)} %get-tuple-element.55), calls=%async_computation.2 | async-start | bytes 3145728 | tf_op jit(solution)/shard_map/all_to_all | solution.py:323
  99.7 67.2 %copy-start.3 = (f32[2,128,1024]{2,1,0:T(8,128)S(1)}, f32[2,128,1024]{2,1,0:T(8,128)}, u32[]{:S(2)}) copy-start(f32[2,128,1024]{2,1,0:T(8,128)} %get-tuple-element.48) | copy-start | bytes 3145732
  99.7 45.0 %collective-permute-start.10 = (bf16[128,1024]{1,0:T(8,128)(2,1)}, bf16[128,1024]{1,0:T(8,128)(2,1)}, u32[]{:S(2)}, u32[]{:S(2)}) collective-permute-start(bf16[128,1024]{1,0:T(8,128)(2,1)} %broadcast_select_fusion), channel_id=1, source_target_pairs={{3,4},{4,3},{2,5},{5,2},{7,8},{8,7},{6,9},{9,6},{11,12},{12,11},{1... | collective-permute-start | bytes 786440 | tf_op jit(solution)/shard_map/ppermute | solution.py:326
  108.9 54.3 %collective-permute-start.7 = (bf16[2,128,1024]{2,1,0:T(8,128)(2,1)}, bf16[2,128,1024]{2,1,0:T(8,128)(2,1)S(1)}, u32[]{:S(2)}, u32[]{:S(2)}) collective-permute-start(bf16[2,128,1024]{2,1,0:T(8,128)(2,1)} %get-tuple-element.49), channel_id=1, source_target_pairs={{0,1},{1,2},{2,3},{4,5},{5,6},{6,7},{8,9},{9,10},{10,11},{12,13},{... | collective-permute-start | bytes 1572872 | tf_op jit(solution)/shard_map/ppermute | solution.py:318
  110.2 53.1 %collective-permute-start.8 = (bf16[2,128,1024]{2,1,0:T(8,128)(2,1)}, bf16[2,128,1024]{2,1,0:T(8,128)(2,1)}, u32[]{:S(2)}, u32[]{:S(2)}) collective-permute-start(bf16[2,128,1024]{2,1,0:T(8,128)(2,1)} %get-tuple-element.50), channel_id=1, source_target_pairs={{1,0},{2,1},{3,2},{5,4},{6,5},{7,6},{9,8},{10,9},{11,10},{13,12},{... | collective-permute-start | bytes 1572872 | tf_op jit(solution)/shard_map/ppermute | solution.py:319
  144.7 15.1 %collective-permute-start.11 = (bf16[2,8,1024]{2,1,0:T(8,128)(2,1)S(1)}, bf16[2,8,1024]{2,1,0:T(8,128)(2,1)S(1)}, u32[]{:S(2)}, u32[]{:S(2)}) collective-permute-start(bf16[2,8,1024]{2,1,0:T(8,128)(2,1)S(1)} %slice.77), channel_id=1, source_target_pairs={{0,4},{4,0},{1,5},{5,1},{2,6},{6,2},{3,7},{7,3},{8,12},{12,8},{9,1... | collective-permute-start | bytes 98312 | tf_op jit(solution)/shard_map/ppermute | solution.py:332
  149.8 12.8 %all-to-all-start.3 = ((f32[16,1,1024]{2,1,0:T(1,128)}), f32[16,1,1024]{2,1,0:T(1,128)S(1)}, u32[]{:S(2)}, u32[]{:S(2)}) async-start(f32[16,1,1024]{2,1,0:T(1,128)} %broadcast_in_dim.42), calls=%async_computation.3 | async-start | bytes 131072 | tf_op jit(solution)/shard_map/all_to_all | solution.py:247
  156.9 10.0 %collective-permute-start.12 = (bf16[128,1024]{1,0:T(8,128)(2,1)}, bf16[128,1024]{1,0:T(8,128)(2,1)S(1)}, u32[]{:S(2)}, u32[]{:S(2)}) collective-permute-start(bf16[128,1024]{1,0:T(8,128)(2,1)} %collective-permute-done.10), channel_id=1, source_target_pairs={{2,3},{1,0},{6,7},{5,4},{10,11},{9,8},{14,15},{13,12},{18,19},{17,... | collective-permute-start | bytes 786440 | tf_op jit(solution)/shard_map/ppermute | solution.py:330
